TPU v7x, 32 devices: a whole 2x2x4 slice. The times are simulated.
32 devices in a mesh: doc: 2 (over y), seg: 16 (over z, x, core).
Axes of the slice: x: 2, y: 2, z: 4, core: 2. Of those that a mesh axis runs over, the one named last changes fastest.
Arguments:
- tokens: bfloat16 [12, 2048, 768], P('doc', 'seg'), may hold values from -6 to 6
- token_mask: int32 [12, 2048], P('doc', 'seg'), may hold values from 0 to 1, as said below
- doc_lengths: int32 [2, 7], P('doc'), may hold values from 1 to 48, 96 in all within a row
- seg_qkv: bfloat16 [3, 768, 768], replicated, may hold values from -0.21875 to 0.21875
- seg_proj: bfloat16 [768, 768], replicated, may hold values from -1.25 to 1.25
- seg_up: bfloat16 [768, 3072], replicated, may hold values from -0.21875 to 0.21875
- seg_down: bfloat16 [3072, 768], replicated, may hold values from -0.109375 to 0.109375
- seg_bias: bfloat16 [3072], replicated, may hold values from -3 to 3
- seg_gains: bfloat16 [2, 768], replicated, may hold values from 0.5 to 1.5
- seg_shifts: bfloat16 [6, 768], replicated, may hold values from -3 to 3
- cross_qkv: bfloat16 [3, 768, 768], replicated, may hold values from -0.21875 to 0.21875
- cross_proj: bfloat16 [768, 768], replicated, may hold values from -1.25 to 1.25
- cross_up: bfloat16 [768, 3072], replicated, may hold values from -0.21875 to 0.21875
- cross_down: bfloat16 [3072, 768], replicated, may hold values from -0.109375 to 0.109375
- cross_bias: bfloat16 [3072], replicated, may hold values from -3 to 3
- cross_gains: bfloat16 [2, 768], replicated, may hold values from 0.5 to 1.5
- cross_shifts: bfloat16 [6, 768], replicated, may hold values from -3 to 3
- positions: bfloat16 [64, 768], replicated, may hold values from -3 to 3
- cotangent: bfloat16 [12, 2048, 768], P('doc', 'seg'), may hold values from -6 to 6
Outputs:
- mixed: bfloat16 [12, 2048, 768], P('doc', 'seg')
- input_grad: bfloat16 [12, 2048, 768], P('doc', 'seg')
- seg_qkv_grad: float32 [3, 768, 768], P(None, 'seg')
- seg_proj_grad: float32 [768, 768], P('seg')
- seg_up_grad: float32 [768, 3072], P('seg')
- seg_down_grad: float32 [3072, 768], P('seg')
- seg_bias_grad: float32 [3072], P('seg')
- seg_gains_grad: float32 [2, 768], P(None, 'seg')
- seg_shifts_grad: float32 [6, 768], P(None, 'seg')
- cross_qkv_grad: float32 [3, 768, 768], P(None, 'seg')
- cross_proj_grad: float32 [768, 768], P('seg')
- cross_up_grad: float32 [768, 3072], P('seg')
- cross_down_grad: float32 [3072, 768], P('seg')
- cross_bias_grad: float32 [3072], P('seg')
- cross_gains_grad: float32 [2, 768], P(None, 'seg')
- cross_shifts_grad: float32 [6, 768], P(None, 'seg')
- positions_grad: float32 [64, 768], P(None, 'seg')
Inputs may be any that keep to these rules, and one draw needn't show every extreme that they name: `doc_lengths`: each row of a group sums to 96; one document of each group has exactly 48 segments. `token_mask`: in every segment the live tokens are a prefix of 32 tokens or more; the first token is always live.
All inputs are finite; a program needn't handle non-finite values.
Results may differ from a plain program's by a relative error of at most 0.023.
Values may be sent and summed in bfloat16 or wider, within the bound.
No kernel may reach another device: no remote copies, remote signals or barrier semaphores. Data moves between devices by JAX's collectives and lax.ppermute only.
A program may use at most 192 MiB of HBM per device.

v0:
```python
import functools

import jax
import jax.numpy as jnp
from jax import lax
from jax.experimental import pallas as pl
from jax.experimental.pallas import tpu as pltpu
from jax.sharding import PartitionSpec as P

f32, bf16 = jnp.float32, jnp.bfloat16
VMEM_BYTES = 60 * 2**20
EPS = 1e-6
PAIR = 128
HD = 64
CHUNK = 768
TILE = 384
NEG = -1e30
SMALL_ROWS = 16

S = jax.ShapeDtypeStruct
V = pltpu.VMEM
VM = pl.BlockSpec(memory_space=pltpu.VMEM)
SM = pl.BlockSpec(memory_space=pltpu.SMEM)
ANY = pl.BlockSpec(memory_space=pl.ANY)
PARAMS = pltpu.CompilerParams(vmem_limit_bytes=VMEM_BYTES)


def cost(micros):
    return pl.CostEstimate(flops=int(micros * 1e9), bytes_accessed=int(micros * 3e6), transcendentals=0)


def nn(a, b):
    return lax.dot_general(a, b, (((1,), (0,)), ((), ())), preferred_element_type=f32)


def nt(a, b):
    return lax.dot_general(a, b, (((1,), (1,)), ((), ())), preferred_element_type=f32)


def tn(a, b):
    return lax.dot_general(a, b, (((0,), (0,)), ((), ())), preferred_element_type=f32)


def gelu_both(u):
    phi = lax.erf(u * 0.70710678118654752) * 0.5 + 0.5
    return u * phi, phi + u * (jnp.exp(u * u * -0.5) * 0.39894228040143268)


def norm(r):
    c = r - jnp.mean(r, axis=-1, keepdims=True)
    inv = lax.rsqrt(jnp.mean(c * c, axis=-1, keepdims=True) + EPS)
    return c * inv, inv


def norm_back(g, n, inv, gain):
    t = g * gain
    return inv * (t - jnp.mean(t, axis=-1, keepdims=True) - n * jnp.mean(t * n, axis=-1, keepdims=True))


def row_sum(x):
    return jnp.sum(x, axis=0, keepdims=True)


def halves(x):
    low = lax.broadcasted_iota(jnp.int32, x.shape, 1) < HD
    zero = jnp.zeros_like(x)
    return jnp.where(low, x, zero), jnp.where(low, zero, x)


def two(x):
    return jnp.concatenate(halves(x), axis=0)


def softmax(t):
    t = jnp.exp(t - jnp.max(t, axis=-1, keepdims=True))
    return (t * (1.0 / jnp.sum(t, axis=-1, keepdims=True))).astype(bf16)


def start_all(sems, *pairs):
    copies = [pltpu.make_async_copy(a, b, sems.at[n]) for n, (a, b) in enumerate(pairs)]
    for c in copies:
        c.start()
    return copies


def whole(a):
    return pl.BlockSpec(a.shape, lambda i, n=len(a.shape): (0,) * n)


def split_of(members, n, spread, D):
    per = n * D // members if spread else D // members
    return None if per % 16 or TILE % (2 * per) else (per, D // (2 * per) if spread else 0)


def grad_outs(members, n, spread, D, extra=0):
    split = split_of(members, n, spread, D)
    if not split:
        return [S((n, D, D), bf16)], [V((n, D, D), bf16), pltpu.SemaphoreType.DMA((n, 2))]
    per, step = split
    rows = per if spread else n * per
    return [S((members // 2, rows + extra, D), bf16)] * 2, [V((n, D // (2 * per), 2, per, D), bf16), pltpu.SemaphoreType.DMA((n, 2))]


def turned(m, bits):
    return m if bits < 2 else (m & ~3) | ((m & 1) << 1) | ((m >> 1) & 1)


def emit_grads(split, core, left, right, outs, stage, sems):
    n, D = stage.shape[0], stage.shape[-1]
    bits = outs[0].shape[0].bit_length() - 1

    def copies(j):
        if not split:
            return [pltpu.make_async_copy(stage.at[j], outs[0].at[j], sems.at[j, 0])]
        per, step = split
        res = []
        for k in range(stage.shape[1]):
            m = j * step + k if step else k
            theirs, ours = jnp.where(core == 1, m, turned(m, bits)), jnp.where(core == 0, m, turned(m, bits))
            rows = pl.ds(0, per) if step else pl.ds(j * per, per)
            res += [pltpu.make_async_copy(stage.at[j, k, 1 - core], outs[0].at[theirs, rows], sems.at[j, 0]),
                    pltpu.make_async_copy(stage.at[j, k, core], outs[1].at[ours, rows], sems.at[j, 1])]
        return res

    for j in range(n):
        for t in range(D // TILE):
            res = tn(left(j, slice(t * TILE, (t + 1) * TILE)), right(j)).astype(bf16)
            if split:
                k = TILE // (2 * split[0])
                stage[j, t * k:(t + 1) * k] = res.reshape((k, 2, split[0], D))
            else:
                stage[j, t * TILE:(t + 1) * TILE, :] = res
        for x in copies(j):
            x.start()

    def end():
        for j in range(n):
            for x in copies(j):
                x.wait()

    return end


def forward_kernel(n_docs, split, n_grads, meta, lengths, tok, cot, mask, wqkv_h, wo_h, wu_h, wd_h, bias, gains, shifts, *rest):
    (q_o, k_o, v_o, p_o, ob_o, n_o, inv_o, y1b_o, dg_o, gm_o, gr2_o, mixed_o, pack_o, small_o), rest = rest[:14], rest[14:]
    grads, (wqkv, wo, wu, wd, gb_s, gm_s, sems, stage, gsems) = rest[:n_grads], rest[n_grads:]
    i = pl.program_id(0)
    segs, pairs = p_o.shape[0], p_o.shape[1]
    B, D = tok.shape
    L = B // segs
    n = wu.shape[0]
    ga, sh = gains[...].astype(f32), shifts[...].astype(f32)
    cs = [slice(c * CHUNK, (c + 1) * CHUNK) for c in range(n)]
    load = lambda a, b, m: pltpu.make_async_copy(a, b, sems.at[m])
    first = [load(wqkv_h, wqkv, 0), load(wo_h, wo, 1)]
    ups = [load(wu_h.at[:, c], wu.at[j], 2 + j) for j, c in enumerate(cs)]
    downs = [load(wd_h.at[c, :], wd.at[j], 2 + n + j) for j, c in enumerate(cs)]

    @pl.when(i == 0)
    def _():
        for c in first + ups + downs:
            c.start()
        small_o[...] = jnp.zeros_like(small_o)
        first[0].wait()

    hb = tok[...]
    q_o[...] = ((nn(hb, wqkv[0]) + sh[0:1]) * 0.125).astype(bf16)
    k_o[...] = nn(hb, wqkv[1]).astype(bf16)
    v_o[...] = (nn(hb, wqkv[2]) + sh[1:2]).astype(bf16)
    col = [slice(j * PAIR, (j + 1) * PAIR) for j in range(pairs)]
    for s in range(segs):
        rows = slice(s * L, (s + 1) * L)
        live = jnp.where(mask[pl.ds(i * segs + s, 1), :] > 0, 0.0, NEG).astype(f32)
        scores = [nt(q_o[rows, c], two(k_o[rows, c])) for c in col]
        probs = [jnp.concatenate([softmax(t[:, e:e + L] + live) for e in (0, L)], axis=1) for t in scores]
        for j, c in enumerate(col):
            p_o[s, j] = probs[j]
            ob_o[rows, c] = nn(probs[j], two(v_o[rows, c])).astype(bf16)

    @pl.when(i == 0)
    def _():
        for c in first[1:] + ups + downs:
            c.wait()

    n1, inv1 = norm(hb.astype(f32) + nn(ob_o[...], wo[...]) + sh[2:3])
    n_o[...] = n1
    inv_o[...] = inv1
    y1 = n1 * ga[0:1] + sh[3:4]
    y1b_o[...] = y1.astype(bf16)
    up = lambda j: nn(y1b_o[...], wu[j]) + bias[:, cs[j]].astype(f32)
    here = pl.ds(pl.multiple_of(i * B, B), B)
    u, acc = up(0), y1 + sh[4:5]
    for j in range(n):
        after = up(j + 1) if j + 1 < n else None
        g, d = gelu_both(u)
        gb = g.astype(bf16)
        gb_s[j, here, :] = gb
        dg_o[j] = d.astype(bf16)
        acc = acc + nn(gb, wd[j])
        u = after
    n2, inv2 = norm(acc)
    mixed_o[...] = (n2 * ga[1:2] + sh[5:6]).astype(bf16)
    row = lax.broadcasted_iota(jnp.int32, n2.shape, 0)
    gz = jnp.where(row % L == 0, 0.0, cot[...].astype(f32))
    small_o[0:1, :] += row_sum(gz * n2)
    small_o[1:2, :] += row_sum(gz)
    gr2 = norm_back(gz, n2, inv2, ga[1:2])
    gr2_o[...] = gr2
    gm = gr2.astype(bf16)
    gm_o[...] = gm
    gm_s[here, :] = gm
    small_o[2:3, :] += row_sum(gm.astype(f32))

    lane = lax.broadcasted_iota(jnp.int32, (1, 128), 1)
    for s in range(segs):
        g = (i * segs + s) * meta[2] + meta[0]
        before, doc, pos = jnp.int32(0), meta[1] * 32, g
        for d in range(n_docs):
            before = before + lengths[0, d]
            passed = g >= before
            doc = doc + passed.astype(jnp.int32)
            pos = jnp.where(passed, g - before, pos)
        extra = jnp.where(lane == 0, doc, jnp.where(lane == 1, pos, 0)).astype(f32)
        top = slice(s * L, s * L + 1)
        high = inv1[top].astype(bf16).astype(f32)
        extra = jnp.where(lane == 2, high, jnp.where(lane == 3, inv1[top] - high, extra))
        pack_o[s, :, :D] = n1[top].astype(bf16)
        pack_o[s, :, D:2 * D] = cot[s * L:s * L + 16, :][0:1]
        pack_o[s, :, 2 * D:] = extra.astype(bf16)

    @pl.when(i == pl.num_programs(0) - 1)
    def _():
        emit_grads(split, meta[3], lambda j, c: gb_s[j, :, c], lambda j: gm_s[...], grads, stage, gsems)()


def forward(meta, lengths, tok, cot, mask, wqkv, wo, wu, wd, bias, gains, shifts, members, step=2):
    T, D = tok.shape
    segs_dev, L = mask.shape
    pairs, B, n = D // PAIR, L * step, wu.shape[1] // CHUNK
    rowblk = pl.BlockSpec((B, D), lambda i: (i, 0))
    wide = pl.BlockSpec((n, B, CHUNK), lambda i: (0, i, 0))
    row = lambda dt: (S((T, D), dt), rowblk)
    outs = [row(bf16), row(bf16), row(bf16),
            (S((segs_dev, pairs, L, 2 * L), bf16), pl.BlockSpec((step, pairs, L, 2 * L), lambda i: (i, 0, 0, 0))),
            row(bf16), row(f32), (S((T, 1), f32), pl.BlockSpec((B, 1), lambda i: (i, 0))), row(bf16), (S((n, T, CHUNK), bf16), wide),
            row(bf16), row(f32), row(bf16),
            (S((segs_dev, 1, 2 * D + 128), bf16), pl.BlockSpec((step, 1, 2 * D + 128), lambda i: (i, 0, 0))),
            (S((8, D), f32), whole(S((8, D), f32)))]
    grads, scratch = grad_outs(members, n, True, D)
    return pl.pallas_call(
        functools.partial(forward_kernel, lengths.shape[1], split_of(members, n, True, D), len(grads)),
        grid=(segs_dev // step,),
        in_specs=[SM, SM, rowblk, rowblk, whole(mask), ANY, ANY, ANY, ANY, whole(bias), whole(gains), whole(shifts)],
        out_specs=[o[1] for o in outs] + [ANY] * len(grads),
        out_shape=[o[0] for o in outs] + grads,
        scratch_shapes=[V(wqkv.shape, bf16), V(wo.shape, bf16), V((n, D, CHUNK), bf16), V((n, CHUNK, D), bf16), V((n, T, CHUNK), bf16),
                        V((T, D), bf16), pltpu.SemaphoreType.DMA((2 + 2 * n,))] + scratch,
        compiler_params=PARAMS,
        name="seg_forward", cost_estimate=cost(30),
    )(meta, lengths, tok, cot, mask, wqkv, wo, wu, wd, bias, gains, shifts)


def ffn_back_kernel(split, n_grads, meta, n1, inv1, y1b, dg, gm, gr2, wu_h, wd_h, gains, gr1_o, gbias_o, small_o, *rest):
    grads, (wu, wd, y1b_s, gu_s, sems, stage, gsems) = rest[:n_grads], rest[n_grads:]
    i = pl.program_id(0)
    n = wu.shape[0]
    B = n1.shape[0]
    cs = [slice(c * CHUNK, (c + 1) * CHUNK) for c in range(n)]
    ups = [pltpu.make_async_copy(wu_h.at[:, c], wu.at[j], sems.at[0, j]) for j, c in enumerate(cs)]
    downs = [pltpu.make_async_copy(wd_h.at[c, :], wd.at[j], sems.at[1, j]) for j, c in enumerate(cs)]

    @pl.when(i == 0)
    def _():
        for j in range(n):
            downs[j].start()
            ups[j].start()
        small_o[...] = jnp.zeros_like(small_o)
        gbias_o[...] = jnp.zeros_like(gbias_o)

    def await_first(*copies):
        @pl.when(i == 0)
        def _():
            for c in copies:
                c.wait()

    here = pl.ds(pl.multiple_of(i * B, B), B)
    y1b_s[here, :] = y1b[...]
    await_first(downs[0])
    t, acc = nt(gm[...], wd[0]), gr2[...]
    for j in range(n):
        await_first(ups[j], *downs[j + 1:j + 2])
        after = nt(gm[...], wd[j + 1]) if j + 1 < n else None
        gu = (t * dg[j].astype(f32)).astype(bf16)
        gu_s[j, here, :] = gu
        gbias_o[j:j + 1, :] += row_sum(gu.astype(f32))
        acc = acc + nt(gu, wu[j])
        t = after
    n1v = n1[...]
    small_o[0:1, :] += row_sum(acc * n1v)
    small_o[1:2, :] += row_sum(acc)
    gr1_o[...] = norm_back(acc, n1v, inv1[...], gains[...].astype(f32)[0:1])

    @pl.when(i == pl.num_programs(0) - 1)
    def _():
        emit_grads(split, meta[3], lambda j, c: y1b_s[:, c], lambda j: gu_s[j], grads, stage, gsems)()


def ffn_back(meta, n1, inv1, y1b, dg, gm, gr2, wu, wd, gains, members, B=256):
    T, D = n1.shape
    n = wu.shape[1] // CHUNK
    rowblk = pl.BlockSpec((B, D), lambda i: (i, 0))
    grads, scratch = grad_outs(members, n, False, D)
    shapes = [S((T, D), f32), S((8, CHUNK), f32), S((8, D), f32)]
    return pl.pallas_call(
        functools.partial(ffn_back_kernel, split_of(members, n, False, D), len(grads)),
        grid=(T // B,),
        in_specs=[SM, rowblk, pl.BlockSpec((B, 1), lambda i: (i, 0)), rowblk, pl.BlockSpec((n, B, CHUNK), lambda i: (0, i, 0)), rowblk, rowblk,
                  ANY, ANY, whole(gains)],
        out_specs=[rowblk, whole(shapes[1]), whole(shapes[2])] + [ANY] * len(grads),
        out_shape=shapes + grads,
        scratch_shapes=[V((n, D, CHUNK), bf16), V((n, CHUNK, D), bf16), V((T, D), bf16), V((n, T, CHUNK), bf16),
                        pltpu.SemaphoreType.DMA((2, n))] + scratch,
        compiler_params=PARAMS,
        name="seg_ffn_back", cost_estimate=cost(20),
    )(meta, n1, inv1, y1b, dg, gm, gr2, wu, wd, gains)


def attn_back_kernel(split, n_grads, is_last, meta, *rest):
    if is_last:
        (base_gh, first_v, small_f, small_b, sums_a, gbias, ga_in), rest = rest[:7], rest[7:]
    else:
        (gr1, gr1c, ob), rest = rest[:3], rest[3:]
    (p, q, k, v, tok, wqkv, wo), rest = rest[:7], rest[7:]
    if is_last:
        (gh_o, vec_o), rest = rest[:2], rest[2:]
    else:
        (gh_o, ga_o, first_v_o, sums_o), rest = rest[:4], rest[4:]
    grads, rest = rest[:n_grads], rest[n_grads:]
    go_s, g_s, left_s, sums, rest = *rest[:4], rest[4:]
    if is_last:
        vec_s, wsems, rest = *rest[:2], rest[2:]
    stage, gsems = rest
    i = pl.program_id(0)
    segs, pairs = p.shape[0], p.shape[1]
    B, D = tok.shape
    L, H = B // segs, pairs * PAIR
    here = pl.ds(pl.multiple_of(i * B, B), B)

    @pl.when(i == 0)
    def _():
        sums[...] = jnp.zeros_like(sums)

    left_s[0, here, :] = tok[...]
    if is_last:
        acc, ga = base_gh[...], ga_in[...]
    else:
        row = lax.broadcasted_iota(jnp.int32, (B, 1), 0)
        acc = gr1[...]
        for s in range(segs):
            acc = jnp.where(row == s * L, gr1c[s], acc)
        ga = acc.astype(bf16)
        ga_o[...] = ga
        g_s[1, here, :] = ga
        left_s[1, here, :] = ob[...]
    go_s[...] = nt(ga, wo[...]).astype(bf16)
    col = [slice(j * PAIR, (j + 1) * PAIR) for j in range(pairs)]
    beside = lambda c: slice(H + c.start, H + c.stop)
    eighth = jnp.asarray(0.125, bf16)
    for s in range(segs):
        rows = slice(s * L, (s + 1) * L)
        out = pl.ds(pl.multiple_of(i * B, B) + s * L, L)
        gps = [nt(go_s[rows, c], two(v[rows, c])) for c in col]
        for j, c in enumerate(col):
            pb = p[s, j]
            gv = tn(jnp.concatenate([pb[:, :L], pb[:, L:]], axis=0), two(go_s[rows, c])).astype(bf16)
            if is_last:
                g_s[1, out, beside(c)] = gv
            else:
                first_v_o[rows, c] = gv
        gss = []
        for j, gp in enumerate(gps):
            pf = p[s, j].astype(f32)
            gs = []
            for e in (0, L):
                pe, ge = pf[:, e:e + L], gp[:, e:e + L]
                gs.append((pe * (ge - jnp.sum(pe * ge, axis=-1, keepdims=True))).astype(bf16))
            gss.append(gs)
        for c, gs in zip(col, gss):
            g_s[0, out, c] = nn(jnp.concatenate(gs, axis=1), two(k[rows, c])).astype(bf16) * eighth
            g_s[0, out, beside(c)] = tn(jnp.concatenate(gs, axis=0), two(q[rows, c])).astype(bf16)
    if is_last:
        g_s[1, here, :H] = first_v[...]
        gv = g_s[1, here, H:]
    else:
        gv = first_v_o[...]
    gq, gk = g_s[0, here, :H], g_s[0, here, H:]
    gh_o[...] = (acc + nt(gq, wqkv[0]) + nt(gk, wqkv[1]) + nt(gv, wqkv[2])).astype(gh_o.dtype)
    for m in range(2):
        sums[m:m + 1, :] += row_sum(g_s[m, here, :].astype(f32))

    @pl.when(i == pl.num_programs(0) - 1)
    def _():
        tail = []
        if is_last:
            vec = jnp.concatenate([
                gbias[0:4, :], small_b[0:1, :], small_f[0:1, :], jnp.concatenate([sums_a[0:1, :H], sums[0:1, :H]], axis=1), sums[1:2, :],
                sums_a[1:2, :], small_b[1:2, :], small_f[2:3, :], small_f[1:2, :], jnp.zeros((4, D), f32)], axis=0)
            vec_o[...] = vec
            if split:
                for m in range(vec_s.shape[0]):
                    vec_s[m] = vec.astype(bf16)
                tail = [pltpu.make_async_copy(vec_s, h.at[:, pl.ds(h.shape[1] - SMALL_ROWS, SMALL_ROWS)], wsems.at[m]) for m, h in enumerate(grads)]
        else:
            sums_o[...] = sums[...]
        for x in tail:
            x.start()
        emit_grads(split, meta[3], lambda j, c: left_s[0 if is_last else j, :, c], lambda j: g_s[j], grads, stage, gsems)()
        for x in tail:
            x.wait()


def attn_back(meta, before_it, p, q, k, v, tok, wqkv, wo, members, is_last, step=2):
    T, D = tok.shape
    segs_dev, all_pairs, L = p.shape[:3]
    pairs, H, half = all_pairs // 2, D // 2, int(is_last)
    B = L * step
    rowblk = pl.BlockSpec((B, D), lambda i: (i, 0))
    halfblk = pl.BlockSpec((B, H), lambda i: (i, half))
    firstblk = pl.BlockSpec((B, H), lambda i: (i, 0))
    split = split_of(members, 2, False, D)
    grads, scratch = grad_outs(members, 2, False, D, SMALL_ROWS if is_last else 0)
    small = S((8, D), f32)
    if is_last:
        vec = S((SMALL_ROWS, D), f32)
        specs = [rowblk, firstblk] + [whole(x) for x in before_it[2:6]] + [rowblk]
        outs = [(S((T, D), bf16), rowblk), (vec, whole(vec))]
        more = [V((members // 2, SMALL_ROWS, D), bf16), pltpu.SemaphoreType.DMA((2,))]
    else:
        specs = [rowblk, pl.BlockSpec((step, 1, D), lambda i: (i, 0, 0)), rowblk]
        outs = [(S((T, D), f32), rowblk), (S((T, D), bf16), rowblk), (S((T, H), bf16), firstblk), (small, whole(small))]
        more = []
    return pl.pallas_call(
        functools.partial(attn_back_kernel, split, len(grads), is_last),
        grid=(segs_dev // step,),
        in_specs=[SM] + specs + [pl.BlockSpec((step, pairs, L, 2 * L), lambda i: (i, half, 0, 0)), halfblk, halfblk, halfblk, rowblk,
                                 pl.BlockSpec((3, D, H), lambda i: (0, 0, half)), pl.BlockSpec((H, D), lambda i: (half, 0))],
        out_specs=[o[1] for o in outs] + [ANY] * len(grads),
        out_shape=[o[0] for o in outs] + grads,
        scratch_shapes=[V((B, H), bf16), V((2, T, D), bf16), V((2, T, D), bf16), V((8, D), f32)] + more + scratch,
        compiler_params=PARAMS,
        name="seg_attention_back", cost_estimate=cost(12),
    )(meta, *before_it, p, q, k, v, tok, wqkv, wo)


def onehot(rows, width, start):
    at = lax.broadcasted_iota(jnp.int32, (rows, width), 0) + start
    return (at == lax.broadcasted_iota(jnp.int32, (rows, width), 1)).astype(bf16)


def nt_exact(x, pick):
    a = x.astype(bf16)
    rest = x - a.astype(f32)
    b = rest.astype(bf16)
    return nt(a, pick) + nt(b, pick) + nt((rest - b.astype(f32)).astype(bf16), pick)


def own_vectors(vec, member, r, F):
    D = vec.shape[1]
    wide = F // D
    per = r * wide
    fits = D // per
    parts = nt_exact(vec, onehot(per, D, lax.rem(member, fits) * per))
    line = lax.broadcasted_iota(jnp.int32, parts.shape, 0)
    bias = row_sum(jnp.where(line == lax.div(member, fits), parts, 0.0))
    rest = nt_exact(vec, onehot(r, D, member * r))
    return bias, rest[wide:wide + 2], rest[wide + 2:wide + 8]


def cross_kernel(r, meta, rows_in, mixed_h, swu_h, swd_h, xqkv_h, xo_h, xu_h, xd_h, sbias, sgains, sshifts, xbias, xgains, xshifts, pos,
                 mixed_o, gr1_o, svec_o, gqkv_o, go_o, gu_o, gd_o, gbias_o, ggains_o, gshifts_o, gpos_o, sgu_o, sgd_o,
                 swu, swd, xqkv, xo, xu, xd, sgb, sdg, xgb, xdg, sgu, xgu, q_s, k_s, v_s, p_s, o_s, go_s, gq_s, gk_s, gv_s,
                 cls_s, gr1_s, vec_s, svec_s, patch, sems, psems):
    n, D = swu.shape[0], swu.shape[1]
    R = rows_in.shape[0]
    cs = [slice(c * CHUNK, (c + 1) * CHUNK) for c in range(n)]
    col = [slice(c, c + PAIR) for c in range(0, D, PAIR)]
    queue = []
    for wu_h, wd_h, wu, wd in ((swu_h, swd_h, swu, swd), (xu_h, xd_h, xu, xd)):
        for j, c in enumerate(cs):
            queue += [(wu_h.at[:, c], wu.at[j]), (wd_h.at[c, :], wd.at[j])]
    queue[2 * n:2 * n] = [(xqkv_h.at[m], xqkv.at[m]) for m in range(3)] + [(xo_h, xo)]
    copies = [pltpu.make_async_copy(a, b, sems.at[m]) for m, (a, b) in enumerate(queue)]
    ahead, waited = 6, [0]
    for x in copies[:ahead]:
        x.start()

    def need(count):
        for _ in range(count):
            m = waited[0]
            copies[m].wait()
            if m + ahead < len(copies):
                copies[m + ahead].start()
            waited[0] = m + 1

    segs, L = patch.shape[0], mixed_h.shape[0] // patch.shape[0]
    fetch = [pltpu.make_async_copy(mixed_h.at[pl.ds(s * L, 16), :], patch.at[s], psems.at[s]) for s in range(segs)]
    for x in fetch:
        x.start()
    sg, ss = sgains[...].astype(f32), sshifts[...].astype(f32)
    xg, xs = xgains[...].astype(f32), xshifts[...].astype(f32)
    eighth = jnp.asarray(0.125, bf16)

    def ffn_f(acc, yb, wu, wd, bias, gb_s, dg_s):
        def up(j):
            need(1)
            return nn(yb, wu[j]) + bias[:, cs[j]].astype(f32)

        for j in range(n):
            g, d = gelu_both(up(j))
            gb = g.astype(bf16)
            gb_s[:, cs[j]] = gb
            dg_s[:, cs[j]] = d.astype(bf16)
            need(1)
            acc = acc + nn(gb, wd[j])
        return acc

    def ffn_b(acc, gm, wu, wd, dg_s, gu_s, vec):
        t = nt(gm, wd[0])
        for j in range(n):
            after = nt(gm, wd[j + 1]) if j + 1 < n else None
            gu = (t * dg_s[:, cs[j]].astype(f32)).astype(bf16)
            gu_s[:, cs[j]] = gu
            vec[j:j + 1, :] = row_sum(gu.astype(f32))
            acc = acc + nt(gu, wu[j])
            t = after
        return acc

    vec_s[...] = jnp.zeros_like(vec_s)
    svec_s[...] = jnp.zeros_like(svec_s)
    n1 = rows_in[:, :D].astype(f32)
    extra = rows_in[:, 2 * D:].astype(f32)
    spos = extra[:, 1:2].astype(jnp.int32)
    inv1 = extra[:, 2:3] + extra[:, 3:4]
    lane = lax.broadcasted_iota(jnp.int32, (8, extra.shape[1]), 1)
    did_row = nt((lane == 0).astype(bf16), extra.astype(bf16))[0:1]
    allowed = extra[:, 0:1] == did_row
    placed = (lax.broadcasted_iota(jnp.int32, (R, pos.shape[0]), 1) == spos).astype(bf16)

    y1 = n1 * sg[0:1] + ss[3:4]
    y1b = y1.astype(bf16)
    n2, inv2 = norm(ffn_f(y1 + ss[4:5], y1b, swu, swd, sbias, sgb, sdg))
    h = n2 * sg[1:2] + ss[5:6] + nn(placed, pos[...])

    hb = h.astype(bf16)
    need(1)
    q_s[...] = ((nn(hb, xqkv[0]) + xs[0:1]) * 0.125).astype(bf16)
    need(1)
    k_s[...] = nn(hb, xqkv[1]).astype(bf16)
    need(1)
    v_s[...] = (nn(hb, xqkv[2]) + xs[1:2]).astype(bf16)
    early = R <= 256
    pair_scores = lambda c: [nt(x, k_s[:, c]) for x in halves(q_s[:, c])]
    scores = [pair_scores(c) for c in col] if early else None
    for j, c in enumerate(col):
        out, v2 = 0.0, halves(v_s[:, c])
        sc = scores[j] if early else pair_scores(c)
        for e in range(2):
            pb = softmax(jnp.where(allowed, sc[e], NEG))
            p_s[2 * j + e] = pb
            out = out + nn(pb, v2[e])
        o_s[:, c] = out.astype(bf16)
    need(1)
    m1, minv1 = norm(h + nn(o_s[...], xo[...]) + xs[2:3])
    z1 = m1 * xg[0:1] + xs[3:4]
    z1b = z1.astype(bf16)
    m2, minv2 = norm(ffn_f(z1 + xs[4:5], z1b, xu, xd, xbias, xgb, xdg))
    cls_s[...] = m2 * xg[1:2] + xs[5:6]

    gz = rows_in[:, D:2 * D].astype(f32)
    vec_s[n + 1:n + 2, :] = row_sum(gz * m2)
    vec_s[n + 7:n + 8, :] = row_sum(gz)
    gr2 = norm_back(gz, m2, minv2, xg[1:2])
    xgm = gr2.astype(bf16)
    vec_s[n + 6:n + 7, :] = row_sum(xgm.astype(f32))
    gy1 = ffn_b(gr2, xgm, xu, xd, xdg, xgu, vec_s)
    vec_s[n:n + 1, :] = row_sum(gy1 * m1)
    vec_s[n + 5:n + 6, :] = row_sum(gy1)
    gr1 = norm_back(gy1, m1, minv1, xg[0:1])
    xga = gr1.astype(bf16)
    vec_s[n + 4:n + 5, :] = row_sum(xga.astype(f32))
    go_s[...] = nt(xga, xo[...]).astype(bf16)
    pair_gps = lambda c: [nt(x, v_s[:, c]) for x in halves(go_s[:, c])]
    gps = [pair_gps(c) for c in col] if early else None
    for j, c in enumerate(col):
        gpj = gps[j] if early else pair_gps(c)
        q2, k2, g2 = halves(q_s[:, c]), halves(k_s[:, c]), halves(go_s[:, c])
        gq = gk = gv = 0.0
        for e in range(2):
            pb = p_s[2 * j + e]
            pf = pb.astype(f32)
            gp = gpj[e]
            gs = (pf * (gp - jnp.sum(pf * gp, axis=-1, keepdims=True))).astype(bf16)
            gq = gq + nn(gs, k2[e])
            gk = gk + tn(gs, q2[e])
            gv = gv + tn(pb, g2[e])
        gq_s[:, c] = gq.astype(bf16) * eighth
        gk_s[:, c] = gk.astype(bf16)
        gv_s[:, c] = gv.astype(bf16)
    vec_s[n + 2:n + 3, :] = row_sum(gq_s[...].astype(f32))
    vec_s[n + 3:n + 4, :] = row_sum(gv_s[...].astype(f32))
    gcls = gr1 + nt(gq_s[...], xqkv[0]) + nt(gk_s[...], xqkv[1]) + nt(gv_s[...], xqkv[2])

    svec_s[n + 1:n + 2, :] = row_sum(gcls * n2)
    svec_s[n + 7:n + 8, :] = row_sum(gcls)
    gr2 = norm_back(gcls, n2, inv2, sg[1:2])
    sgm = gr2.astype(bf16)
    svec_s[n + 6:n + 7, :] = row_sum(sgm.astype(f32))
    gy1 = ffn_b(gr2, sgm, swu, swd, sdg, sgu, svec_s)
    svec_s[n:n + 1, :] = row_sum(gy1 * n1)
    svec_s[n + 5:n + 6, :] = row_sum(gy1)
    gr1_s[...] = norm_back(gy1, n1, inv1, sg[0:1])
    svec_o[...] = svec_s[...]

    for x in fetch:
        x.wait()
    top = lax.broadcasted_iota(jnp.int32, (16, 1), 0) == 0
    for s in range(segs):
        line = pl.ds(meta[4] + s, 1)
        gr1_o[s] = gr1_s[line, :]
        patch[s] = jnp.where(top, cls_s[line, :], patch[s].astype(f32)).astype(bf16)
    store = [pltpu.make_async_copy(patch.at[s], mixed_o.at[pl.ds(s * L, 16), :], psems.at[s]) for s in range(segs)]
    for x in store:
        x.start()

    member = meta[0]
    pick = onehot(r, D, member * r)
    own = lambda x: nt(pick, x).astype(bf16)
    pick_wide = onehot(r * n, n * D, member * r * n)
    own_wide = lambda x: nt(pick_wide, x).astype(bf16)
    hbt = own(hb)
    for m, g in enumerate((gq_s, gk_s, gv_s)):
        gqkv_o[m] = nn(hbt, g[...])
    go_o[...] = nn(own(o_s[...]), xga)
    gd_o[...] = nn(own_wide(xgb[...]), xgm)
    sgd_o[...] = nn(own_wide(sgb[...]), sgm)
    z1t, y1t = own(z1b), own(y1b)
    for c in cs:
        gu_o[:, c] = nn(z1t, xgu[:, c])
        sgu_o[:, c] = nn(y1t, sgu[:, c])
    bias, gains, shifts = own_vectors(vec_s[...], member, r, n * D)
    gbias_o[...] = bias
    ggains_o[...] = gains
    gshifts_o[...] = shifts
    gown = nt_exact(gcls, pick)
    high = gown.astype(bf16)
    gpos_o[...] = tn(placed, high) + tn(placed, (gown - high.astype(f32)).astype(bf16))
    for x in store:
        x.wait()


def cross(meta, rows_in, mixed, seg_params, cross_params, pos, segs, r):
    swu, swd, sbias, sgains, sshifts = seg_params
    xqkv, xo, xu, xd, xbias, xgains, xshifts = cross_params
    R = rows_in.shape[0]
    D, F = swu.shape
    n = F // CHUNK
    outs = [S(mixed.shape, bf16), S((segs, 1, D), f32), S((SMALL_ROWS, D), f32), S((3, r, D), f32), S((r, D), f32), S((r, F), f32),
            S((r * n, D), f32), S((1, r * n), f32), S((2, r), f32), S((6, r), f32), S((pos.shape[0], r), f32), S((r, F), f32), S((r * n, D), f32)]
    up, down, row = V((n, D, CHUNK), bf16), V((n, CHUNK, D), bf16), V((R, D), bf16)
    return pl.pallas_call(
        functools.partial(cross_kernel, r),
        in_specs=[SM, VM] + [ANY] * 7 + [VM] * 7,
        out_specs=[ANY] + [VM] * (len(outs) - 1),
        out_shape=outs,
        scratch_shapes=[up, down, V(xqkv.shape, bf16), V(xo.shape, bf16), up, down] + [V((R, F), bf16)] * 6 + [row] * 3
        + [V((D // HD, R, R), bf16)] + [row] * 5 + [V((R, D), f32)] * 2 + [V((SMALL_ROWS, D), f32)] * 2
        + [V((segs, 16, D), bf16), pltpu.SemaphoreType.DMA((4 * n + 4,)), pltpu.SemaphoreType.DMA((segs,))],
        input_output_aliases={2: 0},
        compiler_params=PARAMS,
        name="cross_block", cost_estimate=cost(28),
    )(meta, rows_in, mixed, swu, swd, xqkv, xo, xu, xd, sbias, sgains, sshifts, xbias, xgains, xshifts, pos)


def finish_kernel(r, F, routed, meta, *rest):
    ins, (w_o, o_o, bias_o, gains_o, shifts_o) = rest[:-5], rest[-5:]
    if routed:
        lower = meta[1] == 0
        totals = []
        for x, other in (ins[0:2], ins[2:4]):
            a, b = x[...].astype(f32), other[...].astype(f32)
            totals.append(jnp.concatenate([jnp.where(lower, a, b), jnp.where(lower, b, a)], axis=0))
    else:
        totals = [ins[0][...], ins[1][...]]
    a, b = totals
    H = a.shape[1] // 2
    for m in range(2):
        w_o[m] = jnp.concatenate([a[:r, m * H:(m + 1) * H], b[:r, m * H:(m + 1) * H]], axis=1)
    w_o[2] = b[r:2 * r]
    o_o[...] = a[r:2 * r]
    bias, gains, shifts = own_vectors(b[2 * r:] + ins[-1][...], meta[0], r, F)
    bias_o[...] = bias
    gains_o[...] = gains
    shifts_o[...] = shifts


def finish(meta, parts, vec_c, r, F, routed):
    D = vec_c.shape[1]
    outs = [S((3, r, D), f32), S((r, D), f32), S((1, r * (F // D)), f32), S((2, r), f32), S((6, r), f32)]
    return pl.pallas_call(
        functools.partial(finish_kernel, r, F, routed), in_specs=[SM] + [VM] * (len(parts) + 1), out_specs=[VM] * len(outs), out_shape=outs,
        compiler_params=PARAMS, name="finish", cost_estimate=cost(2),
    )(meta, *parts, vec_c)


def add_up(a, b):
    return (a.astype(f32) + b.astype(f32)).astype(bf16)


def at(x, i, axis):
    return lax.dynamic_index_in_dim(x, i, axis, keepdims=False)


def fold(pieces, members, member):
    bits = members.bit_length() - 1
    x = pieces.reshape((2,) * bits + pieces.shape[1:])
    for bit in range(bits):
        axis = bits - 1 - bit
        mine = (member >> bit) & 1
        got = lax.ppermute(at(x, 1 - mine, axis), "seg", [(m, m ^ (1 << bit)) for m in range(members)])
        x = add_up(at(x, mine, axis), got)
    return x


def over_docs(x):
    docs = lax.axis_size("doc")
    total, part = x.astype(f32), x
    for _ in range(docs - 1):
        part = lax.ppermute(part, "doc", [(d, (d + 1) % docs) for d in range(docs)])
        total = total + part.astype(f32)
    return total


class Routed:
    def __init__(self, send, keep):
        self.members, member = lax.axis_size("seg"), lax.axis_index("seg")
        self.core, self.number = member & 1, lax.axis_index("doc") * self.members + member
        self.x, self.rows, self.steps = keep, send.shape[1], 0
        self.send = send

    def exchange(self, x, by_core):
        return lax.ppermute(x, ("doc", "seg"), [(m, m ^ by_core[m & 1]) for m in range(2 * self.members)])

    def bit_of(self, mask):
        return ((self.number & mask) != 0).astype(jnp.int32)

    def halve(self, axis, by_core):
        bit = jnp.where(self.core == 0, self.bit_of(by_core[0]), self.bit_of(by_core[1]))
        got = self.exchange(at(self.x, 1 - bit, axis), by_core)
        self.x = add_up(at(self.x, bit, axis), got)

    def step(self, count=1):
        X, Z0, Z1, Y = 2, 4, 8, self.members
        for _ in range(count):
            if self.steps == 0:
                x = add_up(self.x, self.exchange(self.send, (1, 1)))
                self.x = x.reshape(2, 2, 2, 2, self.rows // 2, -1)
            elif self.steps == 1:
                self.halve(2, (X, Z0))
            elif self.steps == 2:
                b = jnp.where(self.core == 0, self.bit_of(Z0), self.bit_of(X))
                y = self.bit_of(Y)
                part = lambda i, h: at(at(self.x, i, 1), h, 1)
                got = [self.exchange(part(1 - b, y), (Z0, X)), self.exchange(part(b, 1 - y), (Y, Y)),
                       self.exchange(part(1 - b, 1 - y), (Z0 + Y, X + Y))]
                total = part(b, y).astype(f32)
                for g in got:
                    total = total + g.astype(f32)
                self.x = total.astype(bf16)
            elif self.steps == 3:
                self.halve(0, (Z1, Z1))
            else:
                self.x = (self.x, self.exchange(self.x, (Y, Y)))
            self.steps += 1
        return self.x


def before(x, *others):
    vals = [f.x if isinstance(f, Routed) else f for f in others]
    res = lax.optimization_barrier((x, *vals))
    for f, v in zip(others, res[1:]):
        if isinstance(f, Routed):
            f.x = v
    return res[0]


def meet(*folds):
    for f, v in zip(folds, lax.optimization_barrier(tuple(f.x for f in folds))):
        f.x = v


def join(x, other):
    a, b = x.astype(f32), other.astype(f32)
    lower = lax.axis_index("doc") == 0
    return jnp.concatenate([jnp.where(lower, a, b), jnp.where(lower, b, a)], axis=0)


def trade(x, mask):
    members = lax.axis_size("seg")
    return lax.ppermute(x, ("doc", "seg"), [(m, m ^ mask) for m in range(2 * members)])


def gather_start(x):
    Z1, Y = 8, lax.axis_size("seg")
    near, far, both = trade(x, Z1), trade(x, Y), trade(x, Y + Z1)
    mine, theirs = jnp.stack([x, near]), jnp.stack([far, both])
    lower = lax.axis_index("doc") == 0
    return jnp.stack([jnp.where(lower, mine, theirs), jnp.where(lower, theirs, mine)])


def gather_middle(x):
    X, Z0 = 2, 4
    return jnp.concatenate([x, trade(x, X), trade(x, Z0), trade(x, X + Z0)], axis=1)


def gather_end(x):
    return jnp.concatenate([x, trade(x, 1)], axis=1)


def shards(tokens, token_mask, doc_lengths, seg_qkv, seg_proj, seg_up, seg_down, seg_bias, seg_gains, seg_shifts,
           cross_qkv, cross_proj, cross_up, cross_down, cross_bias, cross_gains, cross_shifts, positions, cotangent):
    segs, L, D = tokens.shape
    F = seg_up.shape[1]
    members, member = lax.axis_size("seg"), lax.axis_index("seg")
    docs, doc = lax.axis_size("doc"), lax.axis_index("doc")
    r, wide, T = D // members, F // D, segs * L
    all_groups = docs * members * segs <= 256
    few = members == 16 and docs == 2
    place = (doc * members if few else doc * members + member if all_groups else member) * segs
    meta = jnp.stack([member, doc, jnp.int32(members), member & 1, place]).astype(jnp.int32)
    tok, cot = tokens.reshape(T, D), cotangent.reshape(T, D)
    bias, xbias = seg_bias[None], cross_bias[None]

    q, k, v, p, ob, n1, inv1, y1b, dg, gm, gr2, mixed, pack, small_f, *gw_d = forward(
        meta, doc_lengths, tok, cot, token_mask, seg_qkv, seg_proj, seg_up, seg_down, bias, seg_gains, seg_shifts, members)
    routed = few and len(gw_d) == 2
    pack = pack.reshape(segs, -1)
    if few:
        pack = gather_start(pack)
    if routed:
        gm = before(gm, pack)
    gr1, gbias, small_b, *gw_u = ffn_back(meta, n1, inv1, y1b, dg, gm, gr2, seg_up, seg_down, seg_gains, members)
    if few:
        rows = gather_middle(pack)
    if routed:
        fold_d = Routed(*gw_d)
        fold_d.step()
        gw_u[0], rows = before(gw_u[0], fold_d, rows), rows
        fold_u = Routed(*gw_u)
    if few:
        rows = gather_end(rows).reshape(docs * members * segs, -1)
    else:
        rows = lax.all_gather(pack, ("doc", "seg") if all_groups else ("seg",), axis=0, tiled=True)
    if routed:
        rows = before(rows, fold_d)
    mixed, gr1c, svec, *sums = cross(
        meta, rows, mixed, (seg_up, seg_down, bias, seg_gains, seg_shifts),
        (cross_qkv, cross_proj, cross_up, cross_down, xbias, cross_gains, cross_shifts), positions, segs, r)
    if routed:
        fold_d.step()
        fold_u.step()
        gr1c = before(gr1c, fold_d, fold_u)
    gh, ga, first_v, sums_a, *gw_a = attn_back(meta, (gr1, gr1c, ob), p, q, k, v, tok, seg_qkv, seg_proj, members, False)
    if routed:
        fold_d.step()
        fold_u.step()
        gw_a[0] = before(gw_a[0], fold_d, fold_u)
        fold_a = Routed(*gw_a)
        ga = before(ga, fold_d, fold_u)
    gh, vec, *gw_b = attn_back(meta, (gh, first_v, small_f, small_b, sums_a, gbias, ga), p, q, k, v, tok, seg_qkv, seg_proj, members, True)
    if routed:
        fold_a.step()
        fold_d.step()
        fold_u.step()
        gw_b[0] = before(gw_b[0], fold_a, fold_d, fold_u)
        fold_b = Routed(*gw_b)

    if not all_groups:
        sums, svec = [over_docs(s.astype(bf16)) for s in sums], over_docs(svec.astype(bf16))
    gxqkv, gxo, gxu, gxd, gxbias, gxgains, gxshifts, gpos, gsu, gsd = sums

    if routed:
        fold_b.step()
        fold_a.step()
        meet(fold_a, fold_b)
        fold_b.step()
        fold_a.step()
        fold_u.step()
        fold_d.step()
        meet(fold_a, fold_b, fold_u)
        fold_b.step()
        fold_a.step()
        meet(fold_a, fold_b)
        fold_b.step()
        fold_a.step()
        fold_u.step()
        meet(fold_a, fold_b)
        fold_b.step()
        sum_d, sum_u = join(*fold_d.x), join(*fold_u.x)
        parts = fold_a.x + fold_b.x
    else:
        def whole_pieces(g, tall=False):
            if len(g) == 1:
                return g[0].reshape(members, -1, D) if tall else g[0].reshape(-1, members, r, D).swapaxes(0, 1).reshape(members, -1, D)
            send, keep = g
            c = member & 1
            first, second = jnp.where(c == 0, keep, send), jnp.where(c == 0, send, keep)
            if members > 4:
                second = second.reshape((-1, 2, 2) + second.shape[1:]).swapaxes(1, 2).reshape(second.shape)
            both = jnp.stack([first, second], axis=1)
            return both.reshape(members, -1, D)

        pieces = [whole_pieces(gw_d, True)] + [whole_pieces(g) for g in (gw_u, gw_a, gw_b)]
        if len(gw_b) == 1:
            tail = jnp.broadcast_to(vec.astype(bf16)[None], (members, SMALL_ROWS, D))
            pieces[3] = jnp.concatenate([pieces[3], tail], axis=1)
        sum_d, sum_u, *parts = [over_docs(fold(x, members, member)) for x in pieces]
    gqkv, go, gb, gg, gs = finish(meta, parts, svec, r, F, routed)
    up = sum_u.reshape(wide, r, D).swapaxes(0, 1).reshape(r, F) + gsu
    return (
        mixed.reshape(segs, L, D), gh.reshape(segs, L, D),
        gqkv, go, up, sum_d + gsd, gb.reshape(-1), gg, gs,
        gxqkv, gxo, gxu, gxd, gxbias.reshape(-1), gxgains, gxshifts, gpos,
    )


def solution(mesh):
    rows, seg, copied = P("doc", "seg", None), P("seg", None), P()
    grads = (P(None, "seg", None), seg, seg, seg, P("seg"), P(None, "seg"), P(None, "seg"))
    return jax.shard_map(
        shards,
        mesh=mesh,
        in_specs=(rows, P("doc", "seg"), P("doc", None)) + (copied,) * 15 + (rows,),
        out_specs=(rows, rows) + grads + grads + (P(None, "seg"),),
        check_vma=False,
    )
```

profile of v0, /device:TPU:0, one launch (start us, length us, event | category | flops | bytes accessed | tf_op | source)
XLA Modules:
  0.0 230.8 jit_solution(2926826484338467336)
XLA Ops:
  0.7 1.3 broadcast_in_dim.6.bias.sbias
  2.6 32.2 %seg_forward.1 = (bf16[768,768]{1,0:T(8,128)(2,1)}, bf16[768,768]{1,0:T(8,128)(2,1)}, bf16[768,768]{1,0:T(8,128)(2,1)}, bf16[6,6,128,256]{3,2,1,0:T(8,128)(2,1)}...) custom-call(s32[5]{0:T(128)} %stack.41.meta, ...), custom_call_target="tpu_custom_call" | custom-call | flops 30000001024 | bytes 90000000 | tf_op jit(solution)/shard_map/seg_forward/pallas_call | solution.py:250
  35.6 5.0 %collective-permute-start.2 = (bf16[6,1664]{1,0:T(8,128)(2,1)S(1)}, bf16[6,1664]{1,0:T(8,128)(2,1)S(1)}, u32[]{:S(2)}, u32[]{:S(2)}) collective-permute-start(bf16[6,1664]{1,0:T(8,128)(2,1)S(1)} %bitcast.113), channel_id=1, source_target_pairs={{0,24},{1,25},{2,26},{3,27},{4,28},{5,29},{6,30},{7,31},{8,16},{9,... | collective-permute-start | bytes 59912 | tf_op jit(solution)/shard_map/ppermute | solution.py:809
  42.7 1.7 collective-permute-done.1
  44.5 1.4 collective-permute-done
  45.9 1.5 collective-permute-start.3
  47.5 1.6 collective-permute-start.4
  49.5 32.9 %seg_ffn_back.1 = (f32[768,768]{1,0:T(8,128)}, f32[8,768]{1,0:T(8,128)}, f32[8,768]{1,0:T(8,128)}, bf16[8,192,768]{2,1,0:T(8,128)(2,1)}, bf16[8,192,768]{2,1,0:T(8,128)(2,1)}) custom-call(s32[5]{0:T(128)} %stack.41.meta, f32[768,768]{1,0:T(8,128)} %get-tuple-element.94.n1, f32[768,1]{1,0:T(8,128)} %get-tuple-element.95.inv1, ...), custom_call_target="tpu_custom_call" | custom-call | flops 20000000000 | bytes 60000000 | tf_op jit(solution)/shard_map/seg_ffn_back/pallas_call | solution.py:314
  82.7 1.7 collective-permute-done.6
  84.4 1.0 reshape.253.rows_in
  85.5 1.4 copy-done
  86.9 2.9 %add_convert_fusion.1 = bf16[8,192,768]{2,1,0:T(8,128)(2,1)S(1)} fusion(bf16[8,192,768]{2,1,0:T(8,128)(2,1)} %copy-done, bf16[8,192,768]{2,1,0:T(8,128)(2,1)} %get-tuple-element.102), kind=kLoop, calls=%fused_computation.1 | loop fusion | flops 4718592 | bytes 7077888 | tf_op jit(solution)/shard_map/convert_element_type | solution.py:716
  89.9 1.4 collective-permute-start.8
  91.3 30.7 %cross_block.1 = (bf16[768,768]{1,0:T(8,128)(2,1)}, f32[6,1,768]{2,1,0:T(1,128)}, f32[16,768]{1,0:T(8,128)}, f32[3,48,768]{2,1,0:T(8,128)}, f32[48,768]{1,0:T(8,...) custom-call(s32[5]{0:T(128)} %stack.41.meta, ...), custom_call_target="tpu_custom_call", output_to_operand_aliasing={{0}: (2, {})} | custom-call | flops 28000000000 | bytes 84000000 | tf_op jit(solution)/shard_map/cross_block/pallas_call | solution.py:670
  122.0 1.7 fusion.1
  124.0 2.2 add_convert_fusion
  127.1 2.5 %collective-permute-start.12 = (bf16[2,96,768]{2,1,0:T(8,128)(2,1)}, bf16[2,96,768]{2,1,0:T(8,128)(2,1)S(1)}, u32[]{:S(2)}, u32[]{:S(2)}) collective-permute-start(bf16[2,96,768]{2,1,0:T(8,128)(2,1)} %get-tuple-element.207), channel_id=1, source_target_pairs={{0,20},{1,19},{2,22},{3,17},{4,16},{5,23},{6,18},{7,21},{8,28},{9,... | collective-permute-start | bytes 884744 | tf_op jit(solution)/shard_map/ppermute | solution.py:751
  130.6 1.1 copy_bitcast_fusion
  131.7 1.5 collective-permute-start.13
  133.2 13.7 %seg_attention_back.2 = (f32[768,768]{1,0:T(8,128)}, bf16[768,768]{1,0:T(8,128)(2,1)}, bf16[768,384]{1,0:T(8,128)(2,1)}, f32[8,768]{1,0:T(8,128)}, bf16[8,96,768...) custom-call(s32[5]{0:T(128)} %stack.41.meta, f32[768,768]{1,0:T(8,128)} %get-tuple-element.108.rest_0_, ...), custom_call_target="tpu_custom_call" | custom-call | flops 12000000000 | bytes 36000000 | tf_op jit(solution)/shard_map/seg_attention_back/pallas_call | solution.py:442
  147.0 1.2 fusion.9
  148.2 3.8 %collective-permute-done.13 = bf16[2,2,2,96,768]{4,3,0,2,1:T(8,128)(2,1)} collective-permute-done((bf16[2,2,2,96,768]{4,3,0,2,1:T(8,128)(2,1)}, bf16[2,2,2,96,768]{4,3,0,2,1:T(8,128)(2,1)}, u32[]{:S(2)}, u32[]{:S(2)}) %collective-permute-start.13) | collective-permute-done | bytes 1179680 | tf_op jit(solution)/shard_map/ppermute | solution.py:751
  151.9 1.5 fusion
  154.7 2.1 collective-permute-start.18
  156.8 1.2 collective-permute-start.17
  158.2 13.5 %seg_attention_back.3 = (bf16[768,768]{1,0:T(8,128)(2,1)}, f32[16,768]{1,0:T(8,128)}, bf16[8,112,768]{2,1,0:T(8,128)(2,1)}, bf16[8,112,768]{2,1,0:T(8,128)(2,1)}) custom-call(s32[5]{0:T(128)} %stack.41.meta, f32[768,768]{1,0:T(8,128)} %get-tuple-element.119.rest_0_, bf16[768,384]{1,0:T(8,128)(2,1)} %get-tuple-element.120.rest_1_, ...), custom_call_target="tpu_custom_call" | custom-call | flops 12000000000 | bytes 36000000 | tf_op jit(solution)/shard_map/seg_attention_back/pallas_call | solution.py:442
  171.7 1.7 fusion.17
  173.5 1.1 fusion.6
  175.1 1.2 collective-permute-start.19
  177.8 2.5 %collective-permute-start.25 = (bf16[96,768]{1,0:T(8,128)(2,1)S(1)}, bf16[96,768]{1,0:T(8,128)(2,1)S(1)}, u32[]{:S(2)}, u32[]{:S(2)}) collective-permute-start(bf16[96,768]{1,0:T(8,128)(2,1)S(1)} %dynamic-slice_bitcast_fusion.9), channel_id=1, source_target_pairs={{0,8},{1,9},{2,10},{3,11},{4,12},{5,13},{6,14},{7,15},{8,0},{9,1},... | collective-permute-start | bytes 442376 | tf_op jit(solution)/shard_map/ppermute | solution.py:751
  180.3 2.9 %collective-permute-done.34 = bf16[96,768]{1,0:T(8,128)(2,1)} collective-permute-done((bf16[96,768]{1,0:T(8,128)(2,1)}, bf16[96,768]{1,0:T(8,128)(2,1)}, u32[]{:S(2)}, u32[]{:S(2)}) %collective-permute-start.34) | collective-permute-done | bytes 147488 | tf_op jit(solution)/shard_map/ppermute | solution.py:751
  183.2 1.0 convert_select_fusion.1
  185.1 1.2 fusion.3
  186.7 1.2 collective-permute-start.24
  188.8 2.0 collective-permute-start.23
  190.8 1.2 collective-permute-start.22
  192.4 4.2 %collective-permute-done.23 = bf16[2,48,768]{2,1,0:T(8,128)(2,1)S(1)} collective-permute-done((bf16[2,48,768]{2,1,0:T(8,128)(2,1)S(1)}, bf16[2,48,768]{2,1,0:T(8,128)(2,1)S(1)}, u32[]{:S(2)}, u32[]{:S(2)}) %collective-permute-start.23) | collective-permute-done | bytes 147488 | tf_op jit(solution)/shard_map/ppermute | solution.py:751
  196.6 3.2 %collective-permute-done.22 = bf16[2,48,768]{2,1,0:T(8,128)(2,1)S(1)} collective-permute-done((bf16[2,48,768]{2,1,0:T(8,128)(2,1)S(1)}, bf16[2,48,768]{2,1,0:T(8,128)(2,1)S(1)}, u32[]{:S(2)}, u32[]{:S(2)}) %collective-permute-start.22) | collective-permute-done | bytes 147488 | tf_op jit(solution)/shard_map/ppermute | solution.py:751
  201.1 2.7 %collective-permute-start.26 = (bf16[48,768]{1,0:T(8,128)(2,1)S(1)}, bf16[48,768]{1,0:T(8,128)(2,1)S(1)}, u32[]{:S(2)}, u32[]{:S(2)}) collective-permute-start(bf16[48,768]{1,0:T(8,128)(2,1)S(1)} %dynamic-slice_bitcast_fusion.15), channel_id=1, source_target_pairs={{0,8},{1,9},{2,10},{3,11},{4,12},{5,13},{6,14},{7,15},{8,0},{9,1},... | collective-permute-start | bytes 221192 | tf_op jit(solution)/shard_map/ppermute | solution.py:751
  203.8 1.9 collective-permute-start.29
  205.8 1.2 collective-permute-start.28
  208.0 4.1 %collective-permute-done.29 = bf16[2,56,768]{2,1,0:T(8,128)(2,1)S(1)} collective-permute-done((bf16[2,56,768]{2,1,0:T(8,128)(2,1)S(1)}, bf16[2,56,768]{2,1,0:T(8,128)(2,1)S(1)}, u32[]{:S(2)}, u32[]{:S(2)}) %collective-permute-start.29) | collective-permute-done | bytes 172064 | tf_op jit(solution)/shard_map/ppermute | solution.py:751
  212.1 3.7 %collective-permute-done.28 = bf16[2,56,768]{2,1,0:T(8,128)(2,1)S(1)} collective-permute-done((bf16[2,56,768]{2,1,0:T(8,128)(2,1)S(1)}, bf16[2,56,768]{2,1,0:T(8,128)(2,1)S(1)}, u32[]{:S(2)}, u32[]{:S(2)}) %collective-permute-start.28) | collective-permute-done | bytes 172064 | tf_op jit(solution)/shard_map/ppermute | solution.py:751
  216.5 2.1 collective-permute-done.33
  218.6 1.0 collective-permute-start.30
  219.6 3.5 %collective-permute-done.31 = bf16[56,768]{1,0:T(8,128)(2,1)S(1)} collective-permute-done((bf16[56,768]{1,0:T(8,128)(2,1)S(1)}, bf16[56,768]{1,0:T(8,128)(2,1)S(1)}, u32[]{:S(2)}, u32[]{:S(2)}) %collective-permute-start.31) | collective-permute-done | bytes 86048 | tf_op jit(solution)/shard_map/ppermute | solution.py:751
  225.0 2.8 %collective-permute-done.32.rest_3_ = bf16[56,768]{1,0:T(8,128)(2,1)S(1)} collective-permute-done((bf16[56,768]{1,0:T(8,128)(2,1)S(1)}, bf16[56,768]{1,0:T(8,128)(2,1)S(1)}, u32[]{:S(2)}, u32[]{:S(2)}) %collective-permute-start.32) | collective-permute-done | bytes 86048 | tf_op jit(solution)/shard_map/ppermute | solution.py:751
  228.4 2.2 finish.1
  (99 shorter events, 18.1 us)
Async XLA Ops:
  2.6 38.6 %copy-start.9 = (bf16[3072]{0:T(1024)(128)(2,1)S(1)}, bf16[3072]{0:T(1024)(128)(2,1)}, u32[]{:S(2)}) copy-start(bf16[3072]{0:T(1024)(128)(2,1)} %param.33) | copy-start | bytes 18436
  35.6 7.1 %collective-permute-start.2 = (bf16[6,1664]{1,0:T(8,128)(2,1)S(1)}, bf16[6,1664]{1,0:T(8,128)(2,1)S(1)}, u32[]{:S(2)}, u32[]{:S(2)}) collective-permute-start(bf16[6,1664]{1,0:T(8,128)(2,1)S(1)} %bitcast.113), channel_id=1, source_target_pairs={{0,24},{1,25},{2,26},{3,27},{4,28},{5,29},{6,30},{7,31},{8,16},{9,... | collective-permute-start | bytes 59912 | tf_op jit(solution)/shard_map/ppermute | solution.py:809
  40.6 3.8 %collective-permute-start.1 = (bf16[6,1664]{1,0:T(8,128)(2,1)S(1)}, bf16[6,1664]{1,0:T(8,128)(2,1)S(1)}, u32[]{:S(2)}, u32[]{:S(2)}) collective-permute-start(bf16[6,1664]{1,0:T(8,128)(2,1)S(1)} %bitcast.114), channel_id=1, source_target_pairs={{0,16},{1,17},{2,18},{3,19},{4,20},{5,21},{6,22},{7,23},{8,24},{9,... | collective-permute-start | bytes 59912 | tf_op jit(solution)/shard_map/ppermute | solution.py:809
  41.1 4.7 %collective-permute-start = (bf16[6,1664]{1,0:T(8,128)(2,1)S(1)}, bf16[6,1664]{1,0:T(8,128)(2,1)S(1)}, u32[]{:S(2)}, u32[]{:S(2)}) collective-permute-start(bf16[6,1664]{1,0:T(8,128)(2,1)S(1)} %bitcast.115), channel_id=1, source_target_pairs={{0,8},{1,9},{2,10},{3,11},{4,12},{5,13},{6,14},{7,15},{8,0},{9,1},... | collective-permute-start | bytes 59912 | tf_op jit(solution)/shard_map/ppermute | solution.py:809
  41.2 44.3 %collective-permute-start.7 = (bf16[8,192,768]{2,1,0:T(8,128)(2,1)}, bf16[8,192,768]{2,1,0:T(8,128)(2,1)S(1)}, u32[]{:S(2)}, u32[]{:S(2)}) collective-permute-start(bf16[8,192,768]{2,1,0:T(8,128)(2,1)} %get-tuple-element.103), channel_id=1, source_target_pairs={{0,1},{1,0},{2,3},{3,2},{4,5},{5,4},{6,7},{7,6},{8,9},{9,8},{10,11... | collective-permute-start | bytes 7077896 | tf_op jit(solution)/shard_map/ppermute | solution.py:751
  45.9 36.5 %collective-permute-start.3 = (bf16[2,2,6,1664]{3,2,1,0:T(8,128)(2,1)S(1)}, bf16[2,2,6,1664]{3,2,1,0:T(8,128)(2,1)S(1)}, u32[]{:S(2)}, u32[]{:S(2)}) collective-permute-start(bf16[2,2,6,1664]{3,2,1,0:T(8,128)(2,1)S(1)} %get-tuple-element.219), channel_id=1, source_target_pairs={{0,2},{1,3},{2,0},{3,1},{4,6},{5,7},{6,4},{7,5},{8,10},{9,11},{10,... | collective-permute-start | bytes 239624 | tf_op jit(solution)/shard_map/ppermute | solution.py:809
  47.5 35.0 %collective-permute-start.4 = (bf16[2,2,6,1664]{3,2,1,0:T(8,128)(2,1)S(1)}, bf16[2,2,6,1664]{3,2,1,0:T(8,128)(2,1)S(1)}, u32[]{:S(2)}, u32[]{:S(2)}) collective-permute-start(bf16[2,2,6,1664]{3,2,1,0:T(8,128)(2,1)S(1)} %get-tuple-element.219), channel_id=1, source_target_pairs={{0,4},{1,5},{2,6},{3,7},{4,0},{5,1},{6,2},{7,3},{8,12},{9,13},{10,... | collective-permute-start | bytes 239624 | tf_op jit(solution)/shard_map/ppermute | solution.py:809
  49.1 33.4 %collective-permute-start.5 = (bf16[2,2,6,1664]{3,2,1,0:T(8,128)(2,1)S(1)}, bf16[2,2,6,1664]{3,2,1,0:T(8,128)(2,1)S(1)}, u32[]{:S(2)}, u32[]{:S(2)}) collective-permute-start(bf16[2,2,6,1664]{3,2,1,0:T(8,128)(2,1)S(1)} %get-tuple-element.219), channel_id=1, source_target_pairs={{0,6},{1,7},{2,4},{3,5},{4,2},{5,3},{6,0},{7,1},{8,14},{9,15},{10,... | collective-permute-start | bytes 239624 | tf_op jit(solution)/shard_map/ppermute | solution.py:809
  82.6 1.8 collective-permute-start.6
  85.5 1.4 copy-start
  89.9 32.1 %collective-permute-start.8 = (bf16[2,2,2,96,768]{4,3,0,2,1:T(8,128)(2,1)S(1)}, bf16[2,2,2,96,768]{4,3,0,2,1:T(8,128)(2,1)}, u32[]{:S(2)}, u32[]{:S(2)}) collective-permute-start(bf16[2,2,2,96,768]{4,3,0,2,1:T(8,128)(2,1)S(1)} %copy_bitcast_fusion.1), channel_id=1, source_target_pairs={{0,2},{1,5},{2,0},{3,7},{4,6},{5,1},{6,4},{7,3},{8,10},{9,13},{10,... | collective-permute-start | bytes 3538952 | tf_op jit(solution)/shard_map/ppermute | solution.py:751
  91.3 32.4 %collective-permute-start.9 = (bf16[8,192,768]{2,1,0:T(8,128)(2,1)}, bf16[8,192,768]{2,1,0:T(8,128)(2,1)}, u32[]{:S(2)}, u32[]{:S(2)}) collective-permute-start(bf16[8,192,768]{2,1,0:T(8,128)(2,1)} %get-tuple-element.112), channel_id=1, source_target_pairs={{0,1},{1,0},{2,3},{3,2},{4,5},{5,4},{6,7},{7,6},{8,9},{9,8},{10,11... | collective-permute-start | bytes 7077896 | tf_op jit(solution)/shard_map/ppermute | solution.py:751
  122.0 2.0 copy-start.1
  127.1 19.8 %collective-permute-start.12 = (bf16[2,96,768]{2,1,0:T(8,128)(2,1)}, bf16[2,96,768]{2,1,0:T(8,128)(2,1)S(1)}, u32[]{:S(2)}, u32[]{:S(2)}) collective-permute-start(bf16[2,96,768]{2,1,0:T(8,128)(2,1)} %get-tuple-element.207), channel_id=1, source_target_pairs={{0,20},{1,19},{2,22},{3,17},{4,16},{5,23},{6,18},{7,21},{8,28},{9,... | collective-permute-start | bytes 884744 | tf_op jit(solution)/shard_map/ppermute | solution.py:751
  129.7 17.3 %collective-permute-start.11 = (bf16[2,96,768]{2,1,0:T(8,128)(2,1)}, bf16[2,96,768]{2,1,0:T(8,128)(2,1)}, u32[]{:S(2)}, u32[]{:S(2)}) collective-permute-start(bf16[2,96,768]{2,1,0:T(8,128)(2,1)} %get-tuple-element.208), channel_id=1, source_target_pairs={{0,16},{1,17},{2,18},{3,19},{4,20},{5,21},{6,22},{7,23},{8,24},{9,... | collective-permute-start | bytes 884744 | tf_op jit(solution)/shard_map/ppermute | solution.py:751
  130.2 16.8 %collective-permute-start.10 = (bf16[2,96,768]{2,1,0:T(8,128)(2,1)S(1)}, bf16[2,96,768]{2,1,0:T(8,128)(2,1)}, u32[]{:S(2)}, u32[]{:S(2)}) collective-permute-start(bf16[2,96,768]{2,1,0:T(8,128)(2,1)S(1)} %get-tuple-element.206), channel_id=1, source_target_pairs={{0,4},{1,3},{2,6},{3,1},{4,0},{5,7},{6,2},{7,5},{8,12},{9,11},{10,... | collective-permute-start | bytes 884744 | tf_op jit(solution)/shard_map/ppermute | solution.py:751
  131.7 20.2 %collective-permute-start.13 = (bf16[2,2,2,96,768]{4,3,0,2,1:T(8,128)(2,1)}, bf16[2,2,2,96,768]{4,3,0,2,1:T(8,128)(2,1)}, u32[]{:S(2)}, u32[]{:S(2)}) collective-permute-start(bf16[2,2,2,96,768]{4,3,0,2,1:T(8,128)(2,1)} %copy_bitcast_fusion), channel_id=1, source_target_pairs={{0,2},{1,5},{2,0},{3,7},{4,6},{5,1},{6,4},{7,3},{8,10},{9,13},{10,... | collective-permute-start | bytes 3538952 | tf_op jit(solution)/shard_map/ppermute | solution.py:751
  153.5 21.1 %collective-permute-start.14 = (bf16[8,96,768]{2,1,0:T(8,128)(2,1)}, bf16[8,96,768]{2,1,0:T(8,128)(2,1)S(1)}, u32[]{:S(2)}, u32[]{:S(2)}) collective-permute-start(bf16[8,96,768]{2,1,0:T(8,128)(2,1)} %get-tuple-element.135), channel_id=1, source_target_pairs={{0,1},{1,0},{2,3},{3,2},{4,5},{5,4},{6,7},{7,6},{8,9},{9,8},{10,11... | collective-permute-start | bytes 3538952 | tf_op jit(solution)/shard_map/ppermute | solution.py:751
  153.6 18.1 %collective-permute-start.15 = (bf16[96,768]{1,0:T(8,128)(2,1)S(1)}, bf16[96,768]{1,0:T(8,128)(2,1)}, u32[]{:S(2)}, u32[]{:S(2)}) collective-permute-start(bf16[96,768]{1,0:T(8,128)(2,1)S(1)} %dynamic-slice_bitcast_fusion.13), channel_id=1, source_target_pairs={{0,8},{1,9},{2,10},{3,11},{4,12},{5,13},{6,14},{7,15},{8,0},{9,1},... | collective-permute-start | bytes 442376 | tf_op jit(solution)/shard_map/ppermute | solution.py:751
  154.7 18.7 %collective-permute-start.18 = (bf16[2,96,768]{2,1,0:T(8,128)(2,1)}, bf16[2,96,768]{2,1,0:T(8,128)(2,1)S(1)}, u32[]{:S(2)}, u32[]{:S(2)}) collective-permute-start(bf16[2,96,768]{2,1,0:T(8,128)(2,1)} %get-tuple-element.204), channel_id=1, source_target_pairs={{0,20},{1,19},{2,22},{3,17},{4,16},{5,23},{6,18},{7,21},{8,28},{9,... | collective-permute-start | bytes 884744 | tf_op jit(solution)/shard_map/ppermute | solution.py:751
  156.8 16.6 %collective-permute-start.17 = (bf16[2,96,768]{2,1,0:T(8,128)(2,1)S(1)}, bf16[2,96,768]{2,1,0:T(8,128)(2,1)S(1)}, u32[]{:S(2)}, u32[]{:S(2)}) collective-permute-start(bf16[2,96,768]{2,1,0:T(8,128)(2,1)S(1)} %get-tuple-element.205), channel_id=1, source_target_pairs={{0,16},{1,17},{2,18},{3,19},{4,20},{5,21},{6,22},{7,23},{8,24},{9,... | collective-permute-start | bytes 884744 | tf_op jit(solution)/shard_map/ppermute | solution.py:751
  158.0 15.5 %collective-permute-start.16 = (bf16[2,96,768]{2,1,0:T(8,128)(2,1)S(1)}, bf16[2,96,768]{2,1,0:T(8,128)(2,1)}, u32[]{:S(2)}, u32[]{:S(2)}) collective-permute-start(bf16[2,96,768]{2,1,0:T(8,128)(2,1)S(1)} %get-tuple-element.203), channel_id=1, source_target_pairs={{0,4},{1,3},{2,6},{3,1},{4,0},{5,7},{6,2},{7,5},{8,12},{9,11},{10,... | collective-permute-start | bytes 884744 | tf_op jit(solution)/shard_map/ppermute | solution.py:751
  171.7 2.9 %copy-start.3 = (bf16[8,96,768]{2,1,0:T(8,128)(2,1)S(1)}, bf16[8,96,768]{2,1,0:T(8,128)(2,1)}, u32[]{:S(2)}) copy-start(bf16[8,96,768]{2,1,0:T(8,128)(2,1)} %get-tuple-element.134) | copy-start | bytes 3538948
  174.6 2.5 %copy-start.8 = (f32[64,48]{1,0:T(8,128)S(1)}, f32[64,48]{1,0:T(8,128)}, u32[]{:S(2)}) copy-start(f32[64,48]{1,0:T(8,128)} %get-tuple-element.202) | copy-start | bytes 36868
  174.9 11.4 %collective-permute-start.20 = (bf16[8,112,768]{2,1,0:T(8,128)(2,1)}, bf16[8,112,768]{2,1,0:T(8,128)(2,1)S(1)}, u32[]{:S(2)}, u32[]{:S(2)}) collective-permute-start(bf16[8,112,768]{2,1,0:T(8,128)(2,1)} %get-tuple-element.140), channel_id=1, source_target_pairs={{0,1},{1,0},{2,3},{3,2},{4,5},{5,4},{6,7},{7,6},{8,9},{9,8},{10,11... | collective-permute-start | bytes 4128776 | tf_op jit(solution)/shard_map/ppermute | solution.py:751
  175.1 10.1 %collective-permute-start.19 = (bf16[2,2,2,48,768]{4,3,0,2,1:T(8,128)(2,1)S(1)}, bf16[2,2,2,48,768]{4,3,0,2,1:T(8,128)(2,1)}, u32[]{:S(2)}, u32[]{:S(2)}) collective-permute-start(bf16[2,2,2,48,768]{4,3,0,2,1:T(8,128)(2,1)S(1)} %copy_bitcast_fusion.3), channel_id=1, source_target_pairs={{0,2},{1,5},{2,0},{3,7},{4,6},{5,1},{6,4},{7,3},{8,10},{9,13},{10,... | collective-permute-start | bytes 1769480 | tf_op jit(solution)/shard_map/ppermute | solution.py:751
  176.2 7.0 %collective-permute-start.34 = (bf16[96,768]{1,0:T(8,128)(2,1)}, bf16[96,768]{1,0:T(8,128)(2,1)}, u32[]{:S(2)}, u32[]{:S(2)}) collective-permute-start(bf16[96,768]{1,0:T(8,128)(2,1)} %fusion.17), channel_id=1, source_target_pairs={{0,16},{1,17},{2,18},{3,19},{4,20},{5,21},{6,22},{7,23},{8,24},{9,... | collective-permute-start | bytes 442376 | tf_op jit(solution)/shard_map/ppermute | solution.py:751
  177.8 8.6 %copy-start.2 = (bf16[8,112,768]{2,1,0:T(8,128)(2,1)S(1)}, bf16[8,112,768]{2,1,0:T(8,128)(2,1)}, u32[]{:S(2)}) copy-start(bf16[8,112,768]{2,1,0:T(8,128)(2,1)} %get-tuple-element.139) | copy-start | bytes 4128772
  177.8 14.6 %collective-permute-start.25 = (bf16[96,768]{1,0:T(8,128)(2,1)S(1)}, bf16[96,768]{1,0:T(8,128)(2,1)S(1)}, u32[]{:S(2)}, u32[]{:S(2)}) collective-permute-start(bf16[96,768]{1,0:T(8,128)(2,1)S(1)} %dynamic-slice_bitcast_fusion.9), channel_id=1, source_target_pairs={{0,8},{1,9},{2,10},{3,11},{4,12},{5,13},{6,14},{7,15},{8,0},{9,1},... | collective-permute-start | bytes 442376 | tf_op jit(solution)/shard_map/ppermute | solution.py:751
  186.7 1.2 copy-start.5
  186.7 14.2 %collective-permute-start.24 = (bf16[2,2,2,56,768]{4,3,0,2,1:T(8,128)(2,1)S(1)}, bf16[2,2,2,56,768]{4,3,0,2,1:T(8,128)(2,1)S(1)}, u32[]{:S(2)}, u32[]{:S(2)}) collective-permute-start(bf16[2,2,2,56,768]{4,3,0,2,1:T(8,128)(2,1)S(1)} %copy_bitcast_fusion.2), channel_id=1, source_target_pairs={{0,2},{1,5},{2,0},{3,7},{4,6},{5,1},{6,4},{7,3},{8,10},{9,13},{10,... | collective-permute-start | bytes 2064392 | tf_op jit(solution)/shard_map/ppermute | solution.py:751
  188.8 7.8 %collective-permute-start.23 = (bf16[2,48,768]{2,1,0:T(8,128)(2,1)S(1)}, bf16[2,48,768]{2,1,0:T(8,128)(2,1)S(1)}, u32[]{:S(2)}, u32[]{:S(2)}) collective-permute-start(bf16[2,48,768]{2,1,0:T(8,128)(2,1)S(1)} %get-tuple-element.213), channel_id=1, source_target_pairs={{0,20},{1,19},{2,22},{3,17},{4,16},{5,23},{6,18},{7,21},{8,28},{9,... | collective-permute-start | bytes 442376 | tf_op jit(solution)/shard_map/ppermute | solution.py:751
  190.8 9.1 %collective-permute-start.22 = (bf16[2,48,768]{2,1,0:T(8,128)(2,1)S(1)}, bf16[2,48,768]{2,1,0:T(8,128)(2,1)S(1)}, u32[]{:S(2)}, u32[]{:S(2)}) collective-permute-start(bf16[2,48,768]{2,1,0:T(8,128)(2,1)S(1)} %get-tuple-element.214), channel_id=1, source_target_pairs={{0,16},{1,17},{2,18},{3,19},{4,20},{5,21},{6,22},{7,23},{8,24},{9,... | collective-permute-start | bytes 442376 | tf_op jit(solution)/shard_map/ppermute | solution.py:751
  192.0 7.9 %collective-permute-start.21 = (bf16[2,48,768]{2,1,0:T(8,128)(2,1)S(1)}, bf16[2,48,768]{2,1,0:T(8,128)(2,1)S(1)}, u32[]{:S(2)}, u32[]{:S(2)}) collective-permute-start(bf16[2,48,768]{2,1,0:T(8,128)(2,1)S(1)} %get-tuple-element.212), channel_id=1, source_target_pairs={{0,4},{1,3},{2,6},{3,1},{4,0},{5,7},{6,2},{7,5},{8,12},{9,11},{10,... | collective-permute-start | bytes 442376 | tf_op jit(solution)/shard_map/ppermute | solution.py:751
  201.1 6.9 %collective-permute-start.26 = (bf16[48,768]{1,0:T(8,128)(2,1)S(1)}, bf16[48,768]{1,0:T(8,128)(2,1)S(1)}, u32[]{:S(2)}, u32[]{:S(2)}) collective-permute-start(bf16[48,768]{1,0:T(8,128)(2,1)S(1)} %dynamic-slice_bitcast_fusion.15), channel_id=1, source_target_pairs={{0,8},{1,9},{2,10},{3,11},{4,12},{5,13},{6,14},{7,15},{8,0},{9,1},... | collective-permute-start | bytes 221192 | tf_op jit(solution)/shard_map/ppermute | solution.py:751
  203.8 8.3 %collective-permute-start.29 = (bf16[2,56,768]{2,1,0:T(8,128)(2,1)S(1)}, bf16[2,56,768]{2,1,0:T(8,128)(2,1)S(1)}, u32[]{:S(2)}, u32[]{:S(2)}) collective-permute-start(bf16[2,56,768]{2,1,0:T(8,128)(2,1)S(1)} %get-tuple-element.210), channel_id=1, source_target_pairs={{0,20},{1,19},{2,22},{3,17},{4,16},{5,23},{6,18},{7,21},{8,28},{9,... | collective-permute-start | bytes 516104 | tf_op jit(solution)/shard_map/ppermute | solution.py:751
  205.8 10.0 %collective-permute-start.28 = (bf16[2,56,768]{2,1,0:T(8,128)(2,1)S(1)}, bf16[2,56,768]{2,1,0:T(8,128)(2,1)S(1)}, u32[]{:S(2)}, u32[]{:S(2)}) collective-permute-start(bf16[2,56,768]{2,1,0:T(8,128)(2,1)S(1)} %get-tuple-element.211), channel_id=1, source_target_pairs={{0,16},{1,17},{2,18},{3,19},{4,20},{5,21},{6,22},{7,23},{8,24},{9,... | collective-permute-start | bytes 516104 | tf_op jit(solution)/shard_map/ppermute | solution.py:751
  206.9 8.9 %collective-permute-start.27 = (bf16[2,56,768]{2,1,0:T(8,128)(2,1)S(1)}, bf16[2,56,768]{2,1,0:T(8,128)(2,1)S(1)}, u32[]{:S(2)}, u32[]{:S(2)}) collective-permute-start(bf16[2,56,768]{2,1,0:T(8,128)(2,1)S(1)} %get-tuple-element.209), channel_id=1, source_target_pairs={{0,4},{1,3},{2,6},{3,1},{4,0},{5,7},{6,2},{7,5},{8,12},{9,11},{10,... | collective-permute-start | bytes 516104 | tf_op jit(solution)/shard_map/ppermute | solution.py:751
  207.4 11.2 %collective-permute-start.33 = (bf16[96,768]{1,0:T(8,128)(2,1)S(1)}, bf16[96,768]{1,0:T(8,128)(2,1)S(1)}, u32[]{:S(2)}, u32[]{:S(2)}) collective-permute-start(bf16[96,768]{1,0:T(8,128)(2,1)S(1)} %fusion.13), channel_id=1, source_target_pairs={{0,16},{1,17},{2,18},{3,19},{4,20},{5,21},{6,22},{7,23},{8,24},{9,... | collective-permute-start | bytes 442376 | tf_op jit(solution)/shard_map/ppermute | solution.py:751
  208.0 16.0 %copy-start.7 = (bf16[48,768]{1,0:T(8,128)(2,1)}, bf16[48,768]{1,0:T(8,128)(2,1)S(1)}, u32[]{:S(2)}) copy-start(bf16[48,768]{1,0:T(8,128)(2,1)S(1)} %fusion.19.rest_0_) | copy-start | bytes 221188
  215.9 7.2 %collective-permute-start.31 = (bf16[56,768]{1,0:T(8,128)(2,1)S(1)}, bf16[56,768]{1,0:T(8,128)(2,1)S(1)}, u32[]{:S(2)}, u32[]{:S(2)}) collective-permute-start(bf16[56,768]{1,0:T(8,128)(2,1)S(1)} %dynamic-slice_bitcast_fusion.14), channel_id=1, source_target_pairs={{0,8},{1,9},{2,10},{3,11},{4,12},{5,13},{6,14},{7,15},{8,0},{9,1},... | collective-permute-start | bytes 258056 | tf_op jit(solution)/shard_map/ppermute | solution.py:751
  218.6 5.5 %copy-start.4 = (f32[48,3072]{1,0:T(8,128)S(1)}, f32[48,3072]{1,0:T(8,128)}, u32[]{:S(2)}) copy-start(f32[48,3072]{1,0:T(8,128)} %get-tuple-element.155) | copy-start | bytes 1769476
  218.6 4.6 %collective-permute-start.30 = (bf16[48,768]{1,0:T(8,128)(2,1)S(1)}, bf16[48,768]{1,0:T(8,128)(2,1)S(1)}, u32[]{:S(2)}, u32[]{:S(2)}) collective-permute-start(bf16[48,768]{1,0:T(8,128)(2,1)S(1)} %fusion.19.rest_0_), channel_id=1, source_target_pairs={{0,16},{1,17},{2,18},{3,19},{4,20},{5,21},{6,22},{7,23},{8,24},{9,... | collective-permute-start | bytes 221192 | tf_op jit(solution)/shard_map/ppermute | solution.py:751
  223.2 1.8 copy-start.6
  223.2 1.8 copy-start.11
  223.2 4.6 %collective-permute-start.32 = (bf16[56,768]{1,0:T(8,128)(2,1)S(1)}, bf16[56,768]{1,0:T(8,128)(2,1)S(1)}, u32[]{:S(2)}, u32[]{:S(2)}) collective-permute-start(bf16[56,768]{1,0:T(8,128)(2,1)S(1)} %fusion.18.rest_2_), channel_id=1, source_target_pairs={{0,16},{1,17},{2,18},{3,19},{4,20},{5,21},{6,22},{7,23},{8,24},{9,... | collective-permute-start | bytes 258056 | tf_op jit(solution)/shard_map/ppermute | solution.py:751
  227.8 0.6 copy-start.10
where the time goes:
time: 232 us; the launch traced here: 231 us
  Pallas kernels  125 us (54%)
  starting transfers between devices  37.9 us (16%)
  waiting for transfers between devices  37.9 us (16%)
  other arithmetic  17.8 us (8%)
  local copies, waits for them, and re-layouts  10.7 us (5%)
    pallas_call x1, Pallas kernels, ffn_back(): pl.pallas_call(functools.partial(ffn_back_kernel, split_of(members, n, Fa...  32.9 us
    ppermute x28, waiting for transfers between devices, exchange(): lax.ppermute(x, ('doc', 'seg'), [(m, m ^ by_core[m & 1]) for m in range(2...  32.2 us
    pallas_call x1, Pallas kernels, forward(): pl.pallas_call(functools.partial(forward_kernel, lengths.shape[1], split_...  32.2 us
    pallas_call x1, Pallas kernels, cross(): pl.pallas_call(functools.partial(cross_kernel, r), in_specs=[SM, VM] + [A...  30.7 us
    ppermute x28, starting transfers between devices, exchange(): lax.ppermute(x, ('doc', 'seg'), [(m, m ^ by_core[m & 1]) for m in range(2...  28.7 us
    pallas_call x2, Pallas kernels, attn_back(): pl.pallas_call(functools.partial(attn_back_kernel, split, len(grads), is_...  27.2 us
    convert_element_type x12, other arithmetic, add_up(): return (a.astype(f32) + b.astype(f32)).astype(bf16)  12.2 us
    ppermute x7, starting transfers between devices, trade(): lax.ppermute(x, ('doc', 'seg'), [(m, m ^ mask) for m in range(2 * members)])  9.26 us
  transfers between devices with their start and end apart: 35, of which 15 were waited for; matrix products, arithmetic and copies ran while one was open for 7% of the time, Pallas kernels for 39%

commit v1 on v0

--- a/solution.py
+++ b/solution.py
@@ -83,6 +83,12 @@
     return copies
 
 
+def bias_row(bias, j):
+    k = CHUNK // 128
+    rows = bias[...].astype(f32)
+    return jnp.concatenate([rows[j * k + m:j * k + m + 1] for m in range(k)], axis=1)
+
+
 def whole(a):
     return pl.BlockSpec(a.shape, lambda i, n=len(a.shape): (0,) * n)
 
@@ -101,8 +107,13 @@
     return [S((members // 2, rows + extra, D), bf16)] * 2, [V((n, D // (2 * per), 2, per, D), bf16), pltpu.SemaphoreType.DMA((n, 2))]
 
 
-def turned(m, bits):
-    return m if bits < 2 else (m & ~3) | ((m & 1) << 1) | ((m >> 1) & 1)
+def placed_at(m, bits, core):
+    if bits < 2:
+        return m
+    low, next_, high = m & 1, (m >> 1) & 1, m >> 2
+    first = (low << (bits - 1)) | (high << 1) | next_
+    second = (next_ << (bits - 1)) | (high << 1) | low
+    return jnp.where(core == 0, first, second)
 
 
 def emit_grads(split, core, left, right, outs, stage, sems):
@@ -116,7 +127,7 @@
         res = []
         for k in range(stage.shape[1]):
             m = j * step + k if step else k
-            theirs, ours = jnp.where(core == 1, m, turned(m, bits)), jnp.where(core == 0, m, turned(m, bits))
+            theirs, ours = placed_at(m, bits, 1 - core), placed_at(m, bits, core)
             rows = pl.ds(0, per) if step else pl.ds(j * per, per)
             res += [pltpu.make_async_copy(stage.at[j, k, 1 - core], outs[0].at[theirs, rows], sems.at[j, 0]),
                     pltpu.make_async_copy(stage.at[j, k, core], outs[1].at[ours, rows], sems.at[j, 1])]
@@ -142,8 +153,8 @@
 
 
 def forward_kernel(n_docs, split, n_grads, meta, lengths, tok, cot, mask, wqkv_h, wo_h, wu_h, wd_h, bias, gains, shifts, *rest):
-    (q_o, k_o, v_o, p_o, ob_o, n_o, inv_o, y1b_o, dg_o, gm_o, gr2_o, mixed_o, pack_o, small_o), rest = rest[:14], rest[14:]
-    grads, (wqkv, wo, wu, wd, gb_s, gm_s, sems, stage, gsems) = rest[:n_grads], rest[n_grads:]
+    (q_o, k_o, v_o, p_o, ob_o, n_o, inv_o, dg_o, gr2_o, mixed_o, pack_o, small_o), rest = rest[:12], rest[12:]
+    grads, (wqkv, wo, wu, wd, y1b, gb_s, gm_s, sems, stage, gsems) = rest[:n_grads], rest[n_grads:]
     i = pl.program_id(0)
     segs, pairs = p_o.shape[0], p_o.shape[1]
     B, D = tok.shape
@@ -186,8 +197,8 @@
     n_o[...] = n1
     inv_o[...] = inv1
     y1 = n1 * ga[0:1] + sh[3:4]
-    y1b_o[...] = y1.astype(bf16)
-    up = lambda j: nn(y1b_o[...], wu[j]) + bias[:, cs[j]].astype(f32)
+    y1b[...] = y1.astype(bf16)
+    up = lambda j: nn(y1b[...], wu[j]) + bias_row(bias, j)
     here = pl.ds(pl.multiple_of(i * B, B), B)
     u, acc = up(0), y1 + sh[4:5]
     for j in range(n):
@@ -207,7 +218,6 @@
     gr2 = norm_back(gz, n2, inv2, ga[1:2])
     gr2_o[...] = gr2
     gm = gr2.astype(bf16)
-    gm_o[...] = gm
     gm_s[here, :] = gm
     small_o[2:3, :] += row_sum(gm.astype(f32))
 
@@ -242,8 +252,8 @@
     row = lambda dt: (S((T, D), dt), rowblk)
     outs = [row(bf16), row(bf16), row(bf16),
             (S((segs_dev, pairs, L, 2 * L), bf16), pl.BlockSpec((step, pairs, L, 2 * L), lambda i: (i, 0, 0, 0))),
-            row(bf16), row(f32), (S((T, 1), f32), pl.BlockSpec((B, 1), lambda i: (i, 0))), row(bf16), (S((n, T, CHUNK), bf16), wide),
-            row(bf16), row(f32), row(bf16),
+            row(bf16), row(f32), (S((T, 1), f32), pl.BlockSpec((B, 1), lambda i: (i, 0))), (S((n, T, CHUNK), bf16), wide),
+            row(f32), row(bf16),
             (S((segs_dev, 1, 2 * D + 128), bf16), pl.BlockSpec((step, 1, 2 * D + 128), lambda i: (i, 0, 0))),
             (S((8, D), f32), whole(S((8, D), f32)))]
     grads, scratch = grad_outs(members, n, True, D)
@@ -253,59 +263,63 @@
         in_specs=[SM, SM, rowblk, rowblk, whole(mask), ANY, ANY, ANY, ANY, whole(bias), whole(gains), whole(shifts)],
         out_specs=[o[1] for o in outs] + [ANY] * len(grads),
         out_shape=[o[0] for o in outs] + grads,
-        scratch_shapes=[V(wqkv.shape, bf16), V(wo.shape, bf16), V((n, D, CHUNK), bf16), V((n, CHUNK, D), bf16), V((n, T, CHUNK), bf16),
+        scratch_shapes=[V(wqkv.shape, bf16), V(wo.shape, bf16), V((n, D, CHUNK), bf16), V((n, CHUNK, D), bf16), V((B, D), bf16), V((n, T, CHUNK), bf16),
                         V((T, D), bf16), pltpu.SemaphoreType.DMA((2 + 2 * n,))] + scratch,
         compiler_params=PARAMS,
         name="seg_forward", cost_estimate=cost(30),
     )(meta, lengths, tok, cot, mask, wqkv, wo, wu, wd, bias, gains, shifts)
 
 
-def ffn_back_kernel(split, n_grads, meta, n1, inv1, y1b, dg, gm, gr2, wu_h, wd_h, gains, gr1_o, gbias_o, small_o, *rest):
-    grads, (wu, wd, y1b_s, gu_s, sems, stage, gsems) = rest[:n_grads], rest[n_grads:]
+def ffn_back_kernel(split, n_grads, meta, n1, inv1, dg, gr2, wu_h, wd_h, gains, shifts, gr1_o, gbias_o, small_o, *rest):
+    grads, (wu, wd, gm, y1b_s, gu_s, sems, stage, gsems) = rest[:n_grads], rest[n_grads:]
     i = pl.program_id(0)
     n = wu.shape[0]
     B = n1.shape[0]
     cs = [slice(c * CHUNK, (c + 1) * CHUNK) for c in range(n)]
     ups = [pltpu.make_async_copy(wu_h.at[:, c], wu.at[j], sems.at[0, j]) for j, c in enumerate(cs)]
     downs = [pltpu.make_async_copy(wd_h.at[c, :], wd.at[j], sems.at[1, j]) for j, c in enumerate(cs)]
+    order = [c for pair in zip(downs, ups) for c in pair]
 
     @pl.when(i == 0)
     def _():
-        for j in range(n):
-            downs[j].start()
-            ups[j].start()
+        for c in order[:3]:
+            c.start()
         small_o[...] = jnp.zeros_like(small_o)
         gbias_o[...] = jnp.zeros_like(gbias_o)
 
-    def await_first(*copies):
+    def await_first(m, count):
         @pl.when(i == 0)
         def _():
-            for c in copies:
-                c.wait()
+            for k in range(m, min(m + count, 2 * n)):
+                order[k].wait()
+                if k + 3 < 2 * n:
+                    order[k + 3].start()
 
     here = pl.ds(pl.multiple_of(i * B, B), B)
-    y1b_s[here, :] = y1b[...]
-    await_first(downs[0])
-    t, acc = nt(gm[...], wd[0]), gr2[...]
+    n1v, gfirst = n1[...], gains[...].astype(f32)[0:1]
+    y1b_s[here, :] = (n1v * gfirst + shifts[...].astype(f32)[3:4]).astype(bf16)
+    acc = gr2[...]
+    gm[...] = acc.astype(bf16)
+    await_first(0, 1)
+    t = nt(gm[...], wd[0])
     for j in range(n):
-        await_first(ups[j], *downs[j + 1:j + 2])
+        await_first(2 * j + 1, 2)
         after = nt(gm[...], wd[j + 1]) if j + 1 < n else None
         gu = (t * dg[j].astype(f32)).astype(bf16)
         gu_s[j, here, :] = gu
         gbias_o[j:j + 1, :] += row_sum(gu.astype(f32))
         acc = acc + nt(gu, wu[j])
         t = after
-    n1v = n1[...]
     small_o[0:1, :] += row_sum(acc * n1v)
     small_o[1:2, :] += row_sum(acc)
-    gr1_o[...] = norm_back(acc, n1v, inv1[...], gains[...].astype(f32)[0:1])
+    gr1_o[...] = norm_back(acc, n1v, inv1[...], gfirst)
 
     @pl.when(i == pl.num_programs(0) - 1)
     def _():
         emit_grads(split, meta[3], lambda j, c: y1b_s[:, c], lambda j: gu_s[j], grads, stage, gsems)()
 
 
-def ffn_back(meta, n1, inv1, y1b, dg, gm, gr2, wu, wd, gains, members, B=256):
+def ffn_back(meta, n1, inv1, dg, gr2, wu, wd, gains, shifts, members, B=256):
     T, D = n1.shape
     n = wu.shape[1] // CHUNK
     rowblk = pl.BlockSpec((B, D), lambda i: (i, 0))
@@ -314,27 +328,55 @@
     return pl.pallas_call(
         functools.partial(ffn_back_kernel, split_of(members, n, False, D), len(grads)),
         grid=(T // B,),
-        in_specs=[SM, rowblk, pl.BlockSpec((B, 1), lambda i: (i, 0)), rowblk, pl.BlockSpec((n, B, CHUNK), lambda i: (0, i, 0)), rowblk, rowblk,
-                  ANY, ANY, whole(gains)],
+        in_specs=[SM, rowblk, pl.BlockSpec((B, 1), lambda i: (i, 0)), pl.BlockSpec((n, B, CHUNK), lambda i: (0, i, 0)), rowblk,
+                  ANY, ANY, whole(gains), whole(shifts)],
         out_specs=[rowblk, whole(shapes[1]), whole(shapes[2])] + [ANY] * len(grads),
         out_shape=shapes + grads,
-        scratch_shapes=[V((n, D, CHUNK), bf16), V((n, CHUNK, D), bf16), V((T, D), bf16), V((n, T, CHUNK), bf16),
+        scratch_shapes=[V((n, D, CHUNK), bf16), V((n, CHUNK, D), bf16), V((B, D), bf16), V((T, D), bf16), V((n, T, CHUNK), bf16),
                         pltpu.SemaphoreType.DMA((2, n))] + scratch,
         compiler_params=PARAMS,
         name="seg_ffn_back", cost_estimate=cost(20),
-    )(meta, n1, inv1, y1b, dg, gm, gr2, wu, wd, gains)
+    )(meta, n1, inv1, dg, gr2, wu, wd, gains, shifts)
+
+
+def with_cls(rows, cls):
+    row = lax.broadcasted_iota(jnp.int32, (rows.shape[0], 1), 0)
+    for s in range(cls.shape[0]):
+        rows = jnp.where(row == s * (rows.shape[0] // cls.shape[0]), cls[s], rows)
+    return rows
+
+
+def input_grad_kernel(gr1, gr1c, qk0, qk1, vv, wqkv, o):
+    H = qk0.shape[1] // 2
+    part = lambda a: jnp.concatenate([qk0[:, a:a + H], qk1[:, a:a + H]], axis=1)
+    o[...] = (with_cls(gr1[...], gr1c) + nt(part(0), wqkv[0]) + nt(part(H), wqkv[1]) + nt(vv[...], wqkv[2])).astype(bf16)
+
+
+def input_grad(gr1, gr1c, qk0, qk1, vv, wqkv, step=2):
+    T, D = gr1.shape
+    segs = gr1c.shape[0]
+    rowblk = pl.BlockSpec((T // segs * step, D), lambda i: (i, 0))
+    return pl.pallas_call(
+        input_grad_kernel,
+        grid=(segs // step,),
+        in_specs=[rowblk, pl.BlockSpec((step, 1, D), lambda i: (i, 0, 0)), rowblk, rowblk, rowblk, whole(wqkv)],
+        out_specs=rowblk,
+        out_shape=S((T, D), bf16),
+        compiler_params=PARAMS,
+        name="input_grad", cost_estimate=cost(6),
+    )(gr1, gr1c, qk0, qk1, vv, wqkv)
 
 
 def attn_back_kernel(split, n_grads, is_last, meta, *rest):
     if is_last:
-        (base_gh, first_v, small_f, small_b, sums_a, gbias, ga_in), rest = rest[:7], rest[7:]
+        (first_v, small_f, small_b, sums_a, gbias, ga_in), rest = rest[:6], rest[6:]
     else:
         (gr1, gr1c, ob), rest = rest[:3], rest[3:]
-    (p, q, k, v, tok, wqkv, wo), rest = rest[:7], rest[7:]
+    (p, q, k, v, tok, wo), rest = rest[:6], rest[6:]
     if is_last:
-        (gh_o, vec_o), rest = rest[:2], rest[2:]
+        (qk_o, vv_o, vec_o), rest = rest[:3], rest[3:]
     else:
-        (gh_o, ga_o, first_v_o, sums_o), rest = rest[:4], rest[4:]
+        (qk_o, ga_o, first_v_o, sums_o), rest = rest[:4], rest[4:]
     grads, rest = rest[:n_grads], rest[n_grads:]
     go_s, g_s, left_s, sums, rest = *rest[:4], rest[4:]
     if is_last:
@@ -352,13 +394,9 @@
 
     left_s[0, here, :] = tok[...]
     if is_last:
-        acc, ga = base_gh[...], ga_in[...]
+        ga = ga_in[...]
     else:
-        row = lax.broadcasted_iota(jnp.int32, (B, 1), 0)
-        acc = gr1[...]
-        for s in range(segs):
-            acc = jnp.where(row == s * L, gr1c[s], acc)
-        ga = acc.astype(bf16)
+        ga = with_cls(gr1[...], gr1c).astype(bf16)
         ga_o[...] = ga
         g_s[1, here, :] = ga
         left_s[1, here, :] = ob[...]
@@ -390,11 +428,8 @@
             g_s[0, out, beside(c)] = tn(jnp.concatenate(gs, axis=0), two(q[rows, c])).astype(bf16)
     if is_last:
         g_s[1, here, :H] = first_v[...]
-        gv = g_s[1, here, H:]
-    else:
-        gv = first_v_o[...]
-    gq, gk = g_s[0, here, :H], g_s[0, here, H:]
-    gh_o[...] = (acc + nt(gq, wqkv[0]) + nt(gk, wqkv[1]) + nt(gv, wqkv[2])).astype(gh_o.dtype)
+        vv_o[...] = g_s[1, here, :]
+    qk_o[...] = g_s[0, here, :]
     for m in range(2):
         sums[m:m + 1, :] += row_sum(g_s[m, here, :].astype(f32))
 
@@ -419,7 +454,7 @@
             x.wait()
 
 
-def attn_back(meta, before_it, p, q, k, v, tok, wqkv, wo, members, is_last, step=2):
+def attn_back(meta, before_it, p, q, k, v, tok, wo, members, is_last, step=2):
     T, D = tok.shape
     segs_dev, all_pairs, L = p.shape[:3]
     pairs, H, half = all_pairs // 2, D // 2, int(is_last)
@@ -432,24 +467,24 @@
     small = S((8, D), f32)
     if is_last:
         vec = S((SMALL_ROWS, D), f32)
-        specs = [rowblk, firstblk] + [whole(x) for x in before_it[2:6]] + [rowblk]
-        outs = [(S((T, D), bf16), rowblk), (vec, whole(vec))]
+        specs = [firstblk] + [whole(x) for x in before_it[1:5]] + [rowblk]
+        outs = [(S((T, D), bf16), rowblk), (S((T, D), bf16), rowblk), (vec, whole(vec))]
         more = [V((members // 2, SMALL_ROWS, D), bf16), pltpu.SemaphoreType.DMA((2,))]
     else:
         specs = [rowblk, pl.BlockSpec((step, 1, D), lambda i: (i, 0, 0)), rowblk]
-        outs = [(S((T, D), f32), rowblk), (S((T, D), bf16), rowblk), (S((T, H), bf16), firstblk), (small, whole(small))]
+        outs = [(S((T, D), bf16), rowblk), (S((T, D), bf16), rowblk), (S((T, H), bf16), firstblk), (small, whole(small))]
         more = []
     return pl.pallas_call(
         functools.partial(attn_back_kernel, split, len(grads), is_last),
         grid=(segs_dev // step,),
         in_specs=[SM] + specs + [pl.BlockSpec((step, pairs, L, 2 * L), lambda i: (i, half, 0, 0)), halfblk, halfblk, halfblk, rowblk,
-                                 pl.BlockSpec((3, D, H), lambda i: (0, 0, half)), pl.BlockSpec((H, D), lambda i: (half, 0))],
+                                 pl.BlockSpec((H, D), lambda i: (half, 0))],
         out_specs=[o[1] for o in outs] + [ANY] * len(grads),
         out_shape=[o[0] for o in outs] + grads,
         scratch_shapes=[V((B, H), bf16), V((2, T, D), bf16), V((2, T, D), bf16), V((8, D), f32)] + more + scratch,
         compiler_params=PARAMS,
         name="seg_attention_back", cost_estimate=cost(12),
-    )(meta, *before_it, p, q, k, v, tok, wqkv, wo)
+    )(meta, *before_it, p, q, k, v, tok, wo)
 
 
 def onehot(rows, width, start):
@@ -490,7 +525,7 @@
             queue += [(wu_h.at[:, c], wu.at[j]), (wd_h.at[c, :], wd.at[j])]
     queue[2 * n:2 * n] = [(xqkv_h.at[m], xqkv.at[m]) for m in range(3)] + [(xo_h, xo)]
     copies = [pltpu.make_async_copy(a, b, sems.at[m]) for m, (a, b) in enumerate(queue)]
-    ahead, waited = 6, [0]
+    ahead, waited = 4, [0]
     for x in copies[:ahead]:
         x.start()
 
@@ -513,7 +548,7 @@
     def ffn_f(acc, yb, wu, wd, bias, gb_s, dg_s):
         def up(j):
             need(1)
-            return nn(yb, wu[j]) + bias[:, cs[j]].astype(f32)
+            return nn(yb, wu[j]) + bias_row(bias, j)
 
         for j in range(n):
             g, d = gelu_both(up(j))
@@ -744,58 +779,73 @@
     def __init__(self, send, keep):
         self.members, member = lax.axis_size("seg"), lax.axis_index("seg")
         self.core, self.number = member & 1, lax.axis_index("doc") * self.members + member
-        self.x, self.rows, self.steps = keep, send.shape[1], 0
-        self.send = send
-
-    def exchange(self, x, by_core):
-        return lax.ppermute(x, ("doc", "seg"), [(m, m ^ by_core[m & 1]) for m in range(2 * self.members)])
-
-    def bit_of(self, mask):
-        return ((self.number & mask) != 0).astype(jnp.int32)
-
-    def halve(self, axis, by_core):
-        bit = jnp.where(self.core == 0, self.bit_of(by_core[0]), self.bit_of(by_core[1]))
-        got = self.exchange(at(self.x, 1 - bit, axis), by_core)
-        self.x = add_up(at(self.x, bit, axis), got)
-
-    def step(self, count=1):
+        self.step, self.out = 0, [send]
+        self.shape = (2, 2, 2, 2, send.shape[1] // 2, send.shape[2])
+        self.terms, self.fresh = [(keep, ())], 0
+
+    def bit(self, first, second):
+        return jnp.where(self.core == 0, (self.number & first) != 0, (self.number & second) != 0).astype(jnp.int32)
+
+    def sum(self, *choices):
+        total = 0.0
+        for x, path in self.terms:
+            for axis, i in path + choices:
+                x = at(x, i, axis)
+            total = total + x.astype(f32)
+        return total.astype(bf16)
+
+    def ready(self):
         X, Z0, Z1, Y = 2, 4, 8, self.members
-        for _ in range(count):
-            if self.steps == 0:
-                x = add_up(self.x, self.exchange(self.send, (1, 1)))
-                self.x = x.reshape(2, 2, 2, 2, self.rows // 2, -1)
-            elif self.steps == 1:
-                self.halve(2, (X, Z0))
-            elif self.steps == 2:
-                b = jnp.where(self.core == 0, self.bit_of(Z0), self.bit_of(X))
-                y = self.bit_of(Y)
-                part = lambda i, h: at(at(self.x, i, 1), h, 1)
-                got = [self.exchange(part(1 - b, y), (Z0, X)), self.exchange(part(b, 1 - y), (Y, Y)),
-                       self.exchange(part(1 - b, 1 - y), (Z0 + Y, X + Y))]
-                total = part(b, y).astype(f32)
-                for g in got:
-                    total = total + g.astype(f32)
-                self.x = total.astype(bf16)
-            elif self.steps == 3:
-                self.halve(0, (Z1, Z1))
-            else:
-                self.x = (self.x, self.exchange(self.x, (Y, Y)))
-            self.steps += 1
-        return self.x
+        if self.step == 1:
+            self.terms = [(x.reshape(self.shape), path) for x, path in self.terms]
+            b = self.bit(X, Z0)
+            self.masks, self.out, self.choice = [(X, Z0)], [self.sum((0, 1 - b))], ((0, b),)
+        elif self.step == 2:
+            b, y = self.bit(Z0, X), self.bit(Y, Y)
+            self.masks = [(Z0, X), (Y, Y), (Z0 + Y, X + Y)]
+            self.out = [self.sum((1, i), (1, h)) for i, h in ((1 - b, y), (b, 1 - y), (1 - b, 1 - y))]
+            self.choice = ((1, b), (1, y))
+        elif self.step == 3:
+            b = self.bit(Z1, Z1)
+            self.terms, self.fresh = [(lax.optimization_barrier(self.sum()), ())], 0
+            self.masks, self.out, self.choice = [(Z1, Z1)], [self.sum((0, 1 - b))], ((0, b),)
+        else:
+            self.masks, self.out = [(Y, Y)], [self.sum()]
+        return self
+
+    def go(self):
+        masks = self.masks if self.step else [(1, 1)]
+        got = [lax.ppermute(x, ("doc", "seg"), [(m, m ^ by[m & 1]) for m in range(2 * self.members)]) for x, by in zip(self.out, masks)]
+        if self.step == 4:
+            self.x = (self.out[0], got[0])
+        elif self.step:
+            self.terms = [(x, path + self.choice) for x, path in self.terms] + [(x, ()) for x in got]
+        else:
+            self.terms.append((got[0], ()))
+        self.fresh = len(got)
+        self.step += 1
+        return self
+
+    def hold(self, *arrays):
+        old = self.terms[:len(self.terms) - self.fresh]
+        vals = lax.optimization_barrier(tuple(x for x, _ in old) + arrays)
+        self.terms = [(v, path) for v, (_, path) in zip(vals, old)] + self.terms[len(old):]
+        return self
+
+    def after(self, *others):
+        return self.hold(*(x for f in others for x in f.out))
 
 
 def before(x, *others):
-    vals = [f.x if isinstance(f, Routed) else f for f in others]
+    vals = [v for f in others for v in (f.out if isinstance(f, Routed) else [f])]
     res = lax.optimization_barrier((x, *vals))
-    for f, v in zip(others, res[1:]):
+    rest = list(res[1:])
+    for f in others:
         if isinstance(f, Routed):
-            f.x = v
+            f.out = [rest.pop(0) for _ in f.out]
+        else:
+            rest.pop(0)
     return res[0]
-
-
-def meet(*folds):
-    for f, v in zip(folds, lax.optimization_barrier(tuple(f.x for f in folds))):
-        f.x = v
 
 
 def join(x, other):
@@ -838,73 +888,67 @@
     place = (doc * members if few else doc * members + member if all_groups else member) * segs
     meta = jnp.stack([member, doc, jnp.int32(members), member & 1, place]).astype(jnp.int32)
     tok, cot = tokens.reshape(T, D), cotangent.reshape(T, D)
-    bias, xbias = seg_bias[None], cross_bias[None]
-
-    q, k, v, p, ob, n1, inv1, y1b, dg, gm, gr2, mixed, pack, small_f, *gw_d = forward(
+    bias, xbias = seg_bias.reshape(-1, 128), cross_bias.reshape(-1, 128)
+
+    q, k, v, p, ob, n1, inv1, dg, gr2, mixed, pack, small_f, *gw_d = forward(
         meta, doc_lengths, tok, cot, token_mask, seg_qkv, seg_proj, seg_up, seg_down, bias, seg_gains, seg_shifts, members)
     routed = few and len(gw_d) == 2
     pack = pack.reshape(segs, -1)
     if few:
         pack = gather_start(pack)
     if routed:
-        gm = before(gm, pack)
-    gr1, gbias, small_b, *gw_u = ffn_back(meta, n1, inv1, y1b, dg, gm, gr2, seg_up, seg_down, seg_gains, members)
+        fold_d = Routed(*gw_d).go()
+        inv1 = before(inv1, pack)
+    gr1, gbias, small_b, *gw_u = ffn_back(meta, n1, inv1, dg, gr2, seg_up, seg_down, seg_gains, seg_shifts, members)
     if few:
         rows = gather_middle(pack)
     if routed:
-        fold_d = Routed(*gw_d)
-        fold_d.step()
-        gw_u[0], rows = before(gw_u[0], fold_d, rows), rows
-        fold_u = Routed(*gw_u)
+        gw_u[0] = before(gw_u[0], fold_d.ready(), rows)
+        fold_u = Routed(*gw_u).go()
     if few:
         rows = gather_end(rows).reshape(docs * members * segs, -1)
     else:
         rows = lax.all_gather(pack, ("doc", "seg") if all_groups else ("seg",), axis=0, tiled=True)
     if routed:
         rows = before(rows, fold_d)
+        fold_d.go()
     mixed, gr1c, svec, *sums = cross(
         meta, rows, mixed, (seg_up, seg_down, bias, seg_gains, seg_shifts),
         (cross_qkv, cross_proj, cross_up, cross_down, xbias, cross_gains, cross_shifts), positions, segs, r)
     if routed:
-        fold_d.step()
-        fold_u.step()
-        gr1c = before(gr1c, fold_d, fold_u)
-    gh, ga, first_v, sums_a, *gw_a = attn_back(meta, (gr1, gr1c, ob), p, q, k, v, tok, seg_qkv, seg_proj, members, False)
+        gr1c = before(gr1c, fold_d.ready(), fold_u.ready())
+        fold_d.go()
+        fold_u.go()
+    qk0, ga, first_v, sums_a, *gw_a = attn_back(meta, (gr1, gr1c, ob), p, q, k, v, tok, seg_proj, members, False)
     if routed:
-        fold_d.step()
-        fold_u.step()
-        gw_a[0] = before(gw_a[0], fold_d, fold_u)
-        fold_a = Routed(*gw_a)
+        gw_a[0] = before(gw_a[0], fold_d.ready(), fold_u.ready())
         ga = before(ga, fold_d, fold_u)
-    gh, vec, *gw_b = attn_back(meta, (gh, first_v, small_f, small_b, sums_a, gbias, ga), p, q, k, v, tok, seg_qkv, seg_proj, members, True)
+        fold_a = Routed(*gw_a).go()
+        fold_d.go()
+        fold_u.go()
+    qk1, vv, vec, *gw_b = attn_back(meta, (first_v, small_f, small_b, sums_a, gbias, ga), p, q, k, v, tok, seg_proj, members, True)
     if routed:
-        fold_a.step()
-        fold_d.step()
-        fold_u.step()
-        gw_b[0] = before(gw_b[0], fold_a, fold_d, fold_u)
-        fold_b = Routed(*gw_b)
+        gw_b[0] = before(gw_b[0], fold_a.ready(), fold_d.ready(), fold_u.ready())
+        fold_b = Routed(*gw_b).go()
+        for f in (fold_a, fold_d, fold_u):
+            f.go()
 
     if not all_groups:
         sums, svec = [over_docs(s.astype(bf16)) for s in sums], over_docs(svec.astype(bf16))
     gxqkv, gxo, gxu, gxd, gxbias, gxgains, gxshifts, gpos, gsu, gsd = sums
 
     if routed:
-        fold_b.step()
-        fold_a.step()
-        meet(fold_a, fold_b)
-        fold_b.step()
-        fold_a.step()
-        fold_u.step()
-        fold_d.step()
-        meet(fold_a, fold_b, fold_u)
-        fold_b.step()
-        fold_a.step()
-        meet(fold_a, fold_b)
-        fold_b.step()
-        fold_a.step()
-        fold_u.step()
-        meet(fold_a, fold_b)
-        fold_b.step()
+        gh = input_grad(gr1, gr1c, qk0, qk1, vv, seg_qkv)
+        fold_b.hold(gh)
+        for m in range(3):
+            fold_b.ready()
+            fold_a.after(fold_b)
+            fold_b.go()
+            fold_a.ready()
+            fold_b.after(fold_a)
+            fold_a.go()
+        fold_b.ready().go()
+        fold_u.ready().go()
         sum_d, sum_u = join(*fold_d.x), join(*fold_u.x)
         parts = fold_a.x + fold_b.x
     else:
@@ -915,7 +959,9 @@
             c = member & 1
             first, second = jnp.where(c == 0, keep, send), jnp.where(c == 0, send, keep)
             if members > 4:
-                second = second.reshape((-1, 2, 2) + second.shape[1:]).swapaxes(1, 2).reshape(second.shape)
+                apart = lambda x: x.reshape((2, -1, 2) + x.shape[1:])
+                first = jnp.moveaxis(apart(first), 0, 2).reshape(first.shape)
+                second = apart(second).swapaxes(0, 1).reshape(second.shape)
             both = jnp.stack([first, second], axis=1)
             return both.reshape(members, -1, D)
 
@@ -924,6 +970,8 @@
             tail = jnp.broadcast_to(vec.astype(bf16)[None], (members, SMALL_ROWS, D))
             pieces[3] = jnp.concatenate([pieces[3], tail], axis=1)
         sum_d, sum_u, *parts = [over_docs(fold(x, members, member)) for x in pieces]
+    if not routed:
+        gh = input_grad(gr1, gr1c, qk0, qk1, vv, seg_qkv)
     gqkv, go, gb, gg, gs = finish(meta, parts, svec, r, F, routed)
     up = sum_u.reshape(wide, r, D).swapaxes(0, 1).reshape(r, F) + gsu
     return (

time: 232 us -> 227 us (0.978)
  local copies, waits for them, and re-layouts: 10.7 us -> 6.26 us
    pallas_call x0 -> x1, Pallas kernels: none -> 7.47 us  [input_grad(): pl.pallas_call(input_grad_kernel, grid=(segs // step,), in_specs=[rowblk,...]
    pallas_call x2, Pallas kernels: 27.2 us -> 21.8 us  [attn_back(): pl.pallas_call(functools.partial(attn_back_kernel, split, len(grads), is_...]
    ppermute x28, waiting for transfers between devices: 32.2 us -> 28.6 us  [go(): lax.ppermute(x, ('doc', 'seg'), [(m, m ^ by[m & 1]) for m in range(2 * se...]
    convert_element_type x16, other arithmetic: 14.7 us -> 17.2 us  [sum(): return total.astype(bf16)]
  transfers between devices with their start and end apart: 35 -> 35, of which waited for: 15 -> 17; matrix products, arithmetic and copies ran while one was open for 7% -> 6% of each run, Pallas kernels for 39% -> 41%
where the time goes in v1:
time: 227 us; the launch traced here: 226 us
  Pallas kernels  127 us (56%)
  waiting for transfers between devices  35.9 us (16%)
  starting transfers between devices  35.8 us (16%)
  other arithmetic  19.3 us (9%)
  local copies, waits for them, and re-layouts  6.26 us (3%)
    pallas_call x1, Pallas kernels, ffn_back(): pl.pallas_call(functools.partial(ffn_back_kernel, split_of(members, n, Fa...  33.3 us
    pallas_call x1, Pallas kernels, forward(): pl.pallas_call(functools.partial(forward_kernel, lengths.shape[1], split_...  31.8 us
    pallas_call x1, Pallas kernels, cross(): pl.pallas_call(functools.partial(cross_kernel, r), in_specs=[SM, VM] + [A...  30.7 us
    ppermute x28, waiting for transfers between devices, go(): lax.ppermute(x, ('doc', 'seg'), [(m, m ^ by[m & 1]) for m in range(2 * se...  28.6 us
    ppermute x28, starting transfers between devices, go(): lax.ppermute(x, ('doc', 'seg'), [(m, m ^ by[m & 1]) for m in range(2 * se...  26.6 us
    pallas_call x2, Pallas kernels, attn_back(): pl.pallas_call(functools.partial(attn_back_kernel, split, len(grads), is_...  21.8 us
    convert_element_type x16, other arithmetic, sum(): return total.astype(bf16)  17.2 us
    ppermute x7, starting transfers between devices, trade(): lax.ppermute(x, ('doc', 'seg'), [(m, m ^ mask) for m in range(2 * members)])  9.19 us
  transfers between devices with their start and end apart: 35, of which 17 were waited for; matrix products, arithmetic and copies ran while one was open for 6% of the time, Pallas kernels for 41%

profile of v1, /device:TPU:0, one launch (start us, length us, event | category | flops | bytes accessed | tf_op | source)
XLA Modules:
  0.0 225.7 jit_solution(966881334608644797)
XLA Ops:
  1.3 31.8 %seg_forward.1 = (bf16[768,768]{1,0:T(8,128)(2,1)}, bf16[768,768]{1,0:T(8,128)(2,1)}, bf16[768,768]{1,0:T(8,128)(2,1)}, bf16[6,6,128,256]{3,2,1,0:T(8,128)(2,1)}...) custom-call(s32[5]{0:T(128)} %stack.41.meta, ...), custom_call_target="tpu_custom_call" | custom-call | flops 30000001024 | bytes 90000000 | tf_op jit(solution)/shard_map/seg_forward/pallas_call | solution.py:260
  33.9 4.0 %collective-permute-start = (bf16[6,1664]{1,0:T(8,128)(2,1)S(1)}, bf16[6,1664]{1,0:T(8,128)(2,1)S(1)}, u32[]{:S(2)}, u32[]{:S(2)}) collective-permute-start(bf16[6,1664]{1,0:T(8,128)(2,1)S(1)} %bitcast.193), channel_id=1, source_target_pairs={{0,8},{1,9},{2,10},{3,11},{4,12},{5,13},{6,14},{7,15},{8,0},{9,1},... | collective-permute-start | bytes 59912 | tf_op jit(solution)/shard_map/ppermute | solution.py:859
  38.0 1.5 collective-permute-start.1
  39.8 2.0 collective-permute-done.1
  41.8 3.3 %collective-permute-done.2 = bf16[6,1664]{1,0:T(8,128)(2,1)S(1)} collective-permute-done((bf16[6,1664]{1,0:T(8,128)(2,1)S(1)}, bf16[6,1664]{1,0:T(8,128)(2,1)S(1)}, u32[]{:S(2)}, u32[]{:S(2)}) %collective-permute-start.2) | collective-permute-done | bytes 20000 | tf_op jit(solution)/shard_map/ppermute | solution.py:859
  45.2 1.6 collective-permute-start.3
  46.8 1.6 collective-permute-start.4
  48.8 33.3 %seg_ffn_back.1 = (f32[768,768]{1,0:T(8,128)}, f32[8,768]{1,0:T(8,128)}, f32[8,768]{1,0:T(8,128)}, bf16[8,192,768]{2,1,0:T(8,128)(2,1)}, bf16[8,192,768]{2,1,0:T(8,128)(2,1)}) custom-call(s32[5]{0:T(128)} %stack.41.meta, f32[768,768]{1,0:T(8,128)} %get-tuple-element.102.n1, f32[768,1]{1,0:T(8,128)} %get-tuple-element.104.inv1, ...), custom_call_target="tpu_custom_call" | custom-call | flops 20000000000 | bytes 60000000 | tf_op jit(solution)/shard_map/seg_ffn_back/pallas_call | solution.py:328
  82.4 1.7 collective-permute-done.6
  84.1 1.1 reshape.456.rows_in
  85.2 2.6 %fusion = bf16[2,2,2,96,768]{4,3,0,2,1:T(8,128)(2,1)} fusion(bf16[2,2,2,2,96,768]{5,4,3,2,1,0:T(8,128)(2,1)S(1)} %bitcast.175, s32[]{:T(128)S(6)} %select_n.253, bf16[2,2,2,2,96,768]{5,4,3,2,1,0:T(8,128)(2,1)} %bitcast.11), kind=kLoop, calls=%fused_computation.3 | loop fusion | flops 2359296 | bytes 3539968 | tf_op jit(solution)/shard_map/convert_element_type | solution.py:795
  87.9 1.4 collective-permute-start.8
  89.3 30.7 %cross_block.1 = (bf16[768,768]{1,0:T(8,128)(2,1)}, f32[6,1,768]{2,1,0:T(1,128)}, f32[16,768]{1,0:T(8,128)}, f32[3,48,768]{2,1,0:T(8,128)}, f32[48,768]{1,0:T(8,...) custom-call(s32[5]{0:T(128)} %stack.41.meta, ...), custom_call_target="tpu_custom_call", output_to_operand_aliasing={{0}: (2, {})} | custom-call | flops 28000000000 | bytes 84000000 | tf_op jit(solution)/shard_map/cross_block/pallas_call | solution.py:705
  120.1 2.8 %fusion.15 = (bf16[2,96,768]{2,1,0:T(8,128)(2,1)S(1)}, bf16[2,96,768]{2,1,0:T(8,128)(2,1)}, bf16[2,96,768]{2,1,0:T(8,128)(2,1)}) fusion(bf16[2,2,2,96,768]{4,3,0,2,1:T(8,128)(2,1)S(1)} %collective-permute-done.8, s32[]{:T(128)S(6)} %select_n.258, s32[]{:T(128)S(6)} %select_n.264, bf16[2,2,2,2,96,768]{5,4,3,2,1,0:T(8,128)(2,1)} %bitcast.11, ...), kind=kLoop, calls=%fused_computation.27 | loop fusion | flops 2654208 | bytes 3538964 | tf_op jit(solution)/shard_map/convert_element_type | solution.py:795
  122.8 2.6 %fusion.1 = bf16[2,2,2,96,768]{4,3,0,2,1:T(8,128)(2,1)} fusion(bf16[2,2,2,2,96,768]{5,4,3,2,1,0:T(8,128)(2,1)S(1)} %bitcast.180, s32[]{:T(128)S(6)} %select_n.253, bf16[2,2,2,2,96,768]{5,4,3,2,1,0:T(8,128)(2,1)} %bitcast.22), kind=kLoop, calls=%fused_computation.4 | loop fusion | flops 2359296 | bytes 3539968 | tf_op jit(solution)/shard_map/convert_element_type | solution.py:795
  126.0 1.5 collective-permute-start.10
  128.1 1.5 collective-permute-start.12
  129.5 11.2 %seg_attention_back.2 = (bf16[768,768]{1,0:T(8,128)(2,1)}, bf16[768,768]{1,0:T(8,128)(2,1)}, bf16[768,384]{1,0:T(8,128)(2,1)}, f32[8,768]{1,0:T(8,128)}, bf16[8,...) custom-call(s32[5]{0:T(128)} %stack.41.meta, f32[768,768]{1,0:T(8,128)} %get-tuple-element.114.rest_0_.gr1, ...), custom_call_target="tpu_custom_call" | custom-call | flops 12000000000 | bytes 36000000 | tf_op jit(solution)/shard_map/seg_attention_back/pallas_call | solution.py:477
  140.7 1.8 collective-permute-done.11
  142.6 1.5 fusion.14
  145.5 2.1 collective-permute-done.13
  147.6 2.2 fusion.8
  149.8 1.6 collective-permute-start.16
  151.9 1.5 collective-permute-start.18
  153.8 10.6 %seg_attention_back.3 = (bf16[768,768]{1,0:T(8,128)(2,1)}, bf16[768,768]{1,0:T(8,128)(2,1)}, f32[16,768]{1,0:T(8,128)}, bf16[8,112,768]{2,1,0:T(8,128)(2,1)}, bf16[8,112,768]{2,1,0:T(8,128)(2,1)}) custom-call(s32[5]{0:T(128)} %stack.41.meta, bf16[768,384]{1,0:T(8,128)(2,1)} %get-tuple-element.126.rest_0_, f32[8,768]{1,0:T(8,128)} %get-tuple-element.127.rest_1_, ...), custom_call_target="tpu_custom_call" | custom-call | flops 12000000000 | bytes 36000000 | tf_op jit(solution)/shard_map/seg_attention_back/pallas_call | solution.py:477
  164.4 1.0 fusion.33
  166.2 1.5 fusion.7
  168.4 1.1 fusion.3
  170.4 2.4 %collective-permute-start.32 = (bf16[96,768]{1,0:T(8,128)(2,1)}, bf16[96,768]{1,0:T(8,128)(2,1)}, u32[]{:S(2)}, u32[]{:S(2)}) collective-permute-start(bf16[96,768]{1,0:T(8,128)(2,1)} %dynamic-slice_bitcast_fusion), channel_id=1, source_target_pairs={{0,8},{1,9},{2,10},{3,11},{4,12},{5,13},{6,14},{7,15},{8,0},{9,1},... | collective-permute-start | bytes 442376 | tf_op jit(solution)/shard_map/ppermute | solution.py:818
  172.7 7.5 %input_grad.1 = bf16[768,768]{1,0:T(8,128)(2,1)} custom-call(f32[768,768]{1,0:T(8,128)} %get-tuple-element.114.rest_0_.gr1, f32[6,1,768]{2,1,0:T(1,128)} %get-tuple-element.119.rest_1_.gr1c, bf16[768,768]{1,0:T(8,128)(2,1)} %get-tuple-element.125.qk0, bf16[768,768]{1,0:T(8,128)(2,1)} %get-tuple-element.142.qk1, bf16[768,768]{1,0:T(8,128)(2,1)} %get-tuple-element.143.vv, ...), custom_call_target="tpu_custom_call" | custom-call | flops 6000000000 | bytes 18000000 | tf_op jit(solution)/shard_map/input_grad/pallas_call | solution.py:359
  180.7 1.1 collective-permute-start.20
  181.8 1.0 fusion.25
  182.9 1.6 collective-permute-start.33
  184.5 1.8 collective-permute-done.34
  186.5 1.2 collective-permute-start.21
  188.9 1.9 collective-permute-done.20
  191.0 1.6 collective-permute-start.22
  192.5 1.5 collective-permute-start.23
  194.5 6.8 %collective-permute-done.21 = bf16[2,2,2,56,768]{4,3,0,2,1:T(8,128)(2,1)S(1)} collective-permute-done((bf16[2,2,2,56,768]{4,3,0,2,1:T(8,128)(2,1)S(1)}, bf16[2,2,2,56,768]{4,3,0,2,1:T(8,128)(2,1)S(1)}, u32[]{:S(2)}, u32[]{:S(2)}) %collective-permute-start.21) | collective-permute-done | bytes 688160 | tf_op jit(solution)/shard_map/ppermute | solution.py:818
  201.5 1.6 collective-permute-start.25
  203.1 1.5 collective-permute-start.26
  205.9 1.9 collective-permute-done.25
  207.8 1.5 collective-permute-done.26
  209.3 2.6 %collective-permute-done.27 = bf16[2,56,768]{2,1,0:T(8,128)(2,1)S(1)} collective-permute-done((bf16[2,56,768]{2,1,0:T(8,128)(2,1)S(1)}, bf16[2,56,768]{2,1,0:T(8,128)(2,1)S(1)}, u32[]{:S(2)}, u32[]{:S(2)}) %collective-permute-start.27) | collective-permute-done | bytes 172064 | tf_op jit(solution)/shard_map/ppermute | solution.py:818
  212.9 1.6 collective-permute-start.29
  214.5 3.7 %collective-permute-done.30 = bf16[56,768]{1,0:T(8,128)(2,1)S(1)} collective-permute-done((bf16[56,768]{1,0:T(8,128)(2,1)S(1)}, bf16[56,768]{1,0:T(8,128)(2,1)S(1)}, u32[]{:S(2)}, u32[]{:S(2)}) %collective-permute-start.30) | collective-permute-done | bytes 86048 | tf_op jit(solution)/shard_map/ppermute | solution.py:818
  220.0 2.7 %collective-permute-done.31.rest_3_ = bf16[56,768]{1,0:T(8,128)(2,1)S(1)} collective-permute-done((bf16[56,768]{1,0:T(8,128)(2,1)S(1)}, bf16[56,768]{1,0:T(8,128)(2,1)S(1)}, u32[]{:S(2)}, u32[]{:S(2)}) %collective-permute-start.31) | collective-permute-done | bytes 86048 | tf_op jit(solution)/shard_map/ppermute | solution.py:818
  223.4 2.2 finish.1
  (102 shorter events, 15.8 us)
Async XLA Ops:
  33.9 5.9 %collective-permute-start = (bf16[6,1664]{1,0:T(8,128)(2,1)S(1)}, bf16[6,1664]{1,0:T(8,128)(2,1)S(1)}, u32[]{:S(2)}, u32[]{:S(2)}) collective-permute-start(bf16[6,1664]{1,0:T(8,128)(2,1)S(1)} %bitcast.193), channel_id=1, source_target_pairs={{0,8},{1,9},{2,10},{3,11},{4,12},{5,13},{6,14},{7,15},{8,0},{9,1},... | collective-permute-start | bytes 59912 | tf_op jit(solution)/shard_map/ppermute | solution.py:859
  38.0 3.8 %collective-permute-start.1 = (bf16[6,1664]{1,0:T(8,128)(2,1)S(1)}, bf16[6,1664]{1,0:T(8,128)(2,1)S(1)}, u32[]{:S(2)}, u32[]{:S(2)}) collective-permute-start(bf16[6,1664]{1,0:T(8,128)(2,1)S(1)} %bitcast.194), channel_id=1, source_target_pairs={{0,16},{1,17},{2,18},{3,19},{4,20},{5,21},{6,22},{7,23},{8,24},{9,... | collective-permute-start | bytes 59912 | tf_op jit(solution)/shard_map/ppermute | solution.py:859
  39.5 5.6 %collective-permute-start.2 = (bf16[6,1664]{1,0:T(8,128)(2,1)S(1)}, bf16[6,1664]{1,0:T(8,128)(2,1)S(1)}, u32[]{:S(2)}, u32[]{:S(2)}) collective-permute-start(bf16[6,1664]{1,0:T(8,128)(2,1)S(1)} %bitcast.195), channel_id=1, source_target_pairs={{0,24},{1,25},{2,26},{3,27},{4,28},{5,29},{6,30},{7,31},{8,16},{9,... | collective-permute-start | bytes 59912 | tf_op jit(solution)/shard_map/ppermute | solution.py:859
  39.5 45.7 %collective-permute-start.7 = (bf16[8,192,768]{2,1,0:T(8,128)(2,1)}, bf16[8,192,768]{2,1,0:T(8,128)(2,1)}, u32[]{:S(2)}, u32[]{:S(2)}) collective-permute-start(bf16[8,192,768]{2,1,0:T(8,128)(2,1)} %get-tuple-element.109), channel_id=1, source_target_pairs={{0,1},{1,0},{2,3},{3,2},{4,5},{5,4},{6,7},{7,6},{8,9},{9,8},{10,11... | collective-permute-start | bytes 7077896 | tf_op jit(solution)/shard_map/ppermute | solution.py:818
  45.2 36.9 %collective-permute-start.3 = (bf16[2,2,6,1664]{3,2,1,0:T(8,128)(2,1)S(1)}, bf16[2,2,6,1664]{3,2,1,0:T(8,128)(2,1)S(1)}, u32[]{:S(2)}, u32[]{:S(2)}) collective-permute-start(bf16[2,2,6,1664]{3,2,1,0:T(8,128)(2,1)S(1)} %get-tuple-element.235), channel_id=1, source_target_pairs={{0,2},{1,3},{2,0},{3,1},{4,6},{5,7},{6,4},{7,5},{8,10},{9,11},{10,... | collective-permute-start | bytes 239624 | tf_op jit(solution)/shard_map/ppermute | solution.py:859
  46.8 35.3 %collective-permute-start.4 = (bf16[2,2,6,1664]{3,2,1,0:T(8,128)(2,1)S(1)}, bf16[2,2,6,1664]{3,2,1,0:T(8,128)(2,1)S(1)}, u32[]{:S(2)}, u32[]{:S(2)}) collective-permute-start(bf16[2,2,6,1664]{3,2,1,0:T(8,128)(2,1)S(1)} %get-tuple-element.235), channel_id=1, source_target_pairs={{0,4},{1,5},{2,6},{3,7},{4,0},{5,1},{6,2},{7,3},{8,12},{9,13},{10,... | collective-permute-start | bytes 239624 | tf_op jit(solution)/shard_map/ppermute | solution.py:859
  48.3 33.8 %collective-permute-start.5 = (bf16[2,2,6,1664]{3,2,1,0:T(8,128)(2,1)S(1)}, bf16[2,2,6,1664]{3,2,1,0:T(8,128)(2,1)S(1)}, u32[]{:S(2)}, u32[]{:S(2)}) collective-permute-start(bf16[2,2,6,1664]{3,2,1,0:T(8,128)(2,1)S(1)} %get-tuple-element.235), channel_id=1, source_target_pairs={{0,6},{1,7},{2,4},{3,5},{4,2},{5,3},{6,0},{7,1},{8,14},{9,15},{10,... | collective-permute-start | bytes 239624 | tf_op jit(solution)/shard_map/ppermute | solution.py:859
  82.2 1.8 collective-permute-start.6
  82.3 2.8 %copy-start = (bf16[8,192,768]{2,1,0:T(8,128)(2,1)S(1)}, bf16[8,192,768]{2,1,0:T(8,128)(2,1)}, u32[]{:S(2)}) copy-start(bf16[8,192,768]{2,1,0:T(8,128)(2,1)} %get-tuple-element.108) | copy-start | bytes 7077892
  87.8 35.1 %collective-permute-start.9 = (bf16[8,192,768]{2,1,0:T(8,128)(2,1)}, bf16[8,192,768]{2,1,0:T(8,128)(2,1)}, u32[]{:S(2)}, u32[]{:S(2)}) collective-permute-start(bf16[8,192,768]{2,1,0:T(8,128)(2,1)} %get-tuple-element.118), channel_id=1, source_target_pairs={{0,1},{1,0},{2,3},{3,2},{4,5},{5,4},{6,7},{7,6},{8,9},{9,8},{10,11... | collective-permute-start | bytes 7077896 | tf_op jit(solution)/shard_map/ppermute | solution.py:818
  87.9 32.2 %collective-permute-start.8 = (bf16[2,2,2,96,768]{4,3,0,2,1:T(8,128)(2,1)}, bf16[2,2,2,96,768]{4,3,0,2,1:T(8,128)(2,1)S(1)}, u32[]{:S(2)}, u32[]{:S(2)}) collective-permute-start(bf16[2,2,2,96,768]{4,3,0,2,1:T(8,128)(2,1)} %fusion), channel_id=1, source_target_pairs={{0,2},{1,5},{2,0},{3,7},{4,6},{5,1},{6,4},{7,3},{8,10},{9,13},{10,... | collective-permute-start | bytes 3538952 | tf_op jit(solution)/shard_map/ppermute | solution.py:818
  120.0 2.8 %copy-start.1 = (bf16[8,192,768]{2,1,0:T(8,128)(2,1)S(1)}, bf16[8,192,768]{2,1,0:T(8,128)(2,1)}, u32[]{:S(2)}) copy-start(bf16[8,192,768]{2,1,0:T(8,128)(2,1)} %get-tuple-element.117) | copy-start | bytes 7077892
  120.1 5.4 %copy-start.7 = (bf16[2,2,2,96,768]{4,3,0,2,1:T(8,128)(2,1)}, bf16[2,2,2,96,768]{4,3,0,2,1:T(8,128)(2,1)S(1)}, u32[]{:S(2)}) copy-start(bf16[2,2,2,96,768]{4,3,0,2,1:T(8,128)(2,1)S(1)} %collective-permute-done.8) | copy-start | bytes 3538948
  125.4 22.2 %collective-permute-start.13 = (bf16[2,2,2,96,768]{4,3,0,2,1:T(8,128)(2,1)}, bf16[2,2,2,96,768]{4,3,0,2,1:T(8,128)(2,1)S(1)}, u32[]{:S(2)}, u32[]{:S(2)}) collective-permute-start(bf16[2,2,2,96,768]{4,3,0,2,1:T(8,128)(2,1)} %fusion.1), channel_id=1, source_target_pairs={{0,2},{1,5},{2,0},{3,7},{4,6},{5,1},{6,4},{7,3},{8,10},{9,13},{10,... | collective-permute-start | bytes 3538952 | tf_op jit(solution)/shard_map/ppermute | solution.py:818
  126.0 14.7 %collective-permute-start.10 = (bf16[2,96,768]{2,1,0:T(8,128)(2,1)}, bf16[2,96,768]{2,1,0:T(8,128)(2,1)}, u32[]{:S(2)}, u32[]{:S(2)}) collective-permute-start(bf16[2,96,768]{2,1,0:T(8,128)(2,1)} %get-tuple-element.133), channel_id=1, source_target_pairs={{0,4},{1,3},{2,6},{3,1},{4,0},{5,7},{6,2},{7,5},{8,12},{9,11},{10,... | collective-permute-start | bytes 884744 | tf_op jit(solution)/shard_map/ppermute | solution.py:818
  127.5 15.0 %collective-permute-start.11 = (bf16[2,96,768]{2,1,0:T(8,128)(2,1)}, bf16[2,96,768]{2,1,0:T(8,128)(2,1)}, u32[]{:S(2)}, u32[]{:S(2)}) collective-permute-start(bf16[2,96,768]{2,1,0:T(8,128)(2,1)} %get-tuple-element.134), channel_id=1, source_target_pairs={{0,16},{1,17},{2,18},{3,19},{4,20},{5,21},{6,22},{7,23},{8,24},{9,... | collective-permute-start | bytes 884744 | tf_op jit(solution)/shard_map/ppermute | solution.py:818
  128.1 14.5 %collective-permute-start.12 = (bf16[2,96,768]{2,1,0:T(8,128)(2,1)S(1)}, bf16[2,96,768]{2,1,0:T(8,128)(2,1)}, u32[]{:S(2)}, u32[]{:S(2)}) collective-permute-start(bf16[2,96,768]{2,1,0:T(8,128)(2,1)S(1)} %get-tuple-element.135), channel_id=1, source_target_pairs={{0,20},{1,19},{2,22},{3,17},{4,16},{5,23},{6,18},{7,21},{8,28},{9,... | collective-permute-start | bytes 884744 | tf_op jit(solution)/shard_map/ppermute | solution.py:818
  147.6 2.2 copy-start.6
  149.8 15.7 %collective-permute-start.16 = (bf16[2,96,768]{2,1,0:T(8,128)(2,1)S(1)}, bf16[2,96,768]{2,1,0:T(8,128)(2,1)S(1)}, u32[]{:S(2)}, u32[]{:S(2)}) collective-permute-start(bf16[2,96,768]{2,1,0:T(8,128)(2,1)S(1)} %get-tuple-element.150), channel_id=1, source_target_pairs={{0,4},{1,3},{2,6},{3,1},{4,0},{5,7},{6,2},{7,5},{8,12},{9,11},{10,... | collective-permute-start | bytes 884744 | tf_op jit(solution)/shard_map/ppermute | solution.py:818
  151.4 14.8 %collective-permute-start.17 = (bf16[2,96,768]{2,1,0:T(8,128)(2,1)S(1)}, bf16[2,96,768]{2,1,0:T(8,128)(2,1)}, u32[]{:S(2)}, u32[]{:S(2)}) collective-permute-start(bf16[2,96,768]{2,1,0:T(8,128)(2,1)S(1)} %get-tuple-element.151), channel_id=1, source_target_pairs={{0,16},{1,17},{2,18},{3,19},{4,20},{5,21},{6,22},{7,23},{8,24},{9,... | collective-permute-start | bytes 884744 | tf_op jit(solution)/shard_map/ppermute | solution.py:818
  151.9 14.3 %collective-permute-start.18 = (bf16[2,96,768]{2,1,0:T(8,128)(2,1)S(1)}, bf16[2,96,768]{2,1,0:T(8,128)(2,1)}, u32[]{:S(2)}, u32[]{:S(2)}) collective-permute-start(bf16[2,96,768]{2,1,0:T(8,128)(2,1)S(1)} %get-tuple-element.152), channel_id=1, source_target_pairs={{0,20},{1,19},{2,22},{3,17},{4,16},{5,23},{6,18},{7,21},{8,28},{9,... | collective-permute-start | bytes 884744 | tf_op jit(solution)/shard_map/ppermute | solution.py:818
  153.4 11.1 %collective-permute-start.15 = (bf16[96,768]{1,0:T(8,128)(2,1)}, bf16[96,768]{1,0:T(8,128)(2,1)}, u32[]{:S(2)}, u32[]{:S(2)}) collective-permute-start(bf16[96,768]{1,0:T(8,128)(2,1)} %dynamic-slice_bitcast_fusion.1), channel_id=1, source_target_pairs={{0,8},{1,9},{2,10},{3,11},{4,12},{5,13},{6,14},{7,15},{8,0},{9,1},... | collective-permute-start | bytes 442376 | tf_op jit(solution)/shard_map/ppermute | solution.py:818
  153.8 14.7 %collective-permute-start.14 = (bf16[8,96,768]{2,1,0:T(8,128)(2,1)}, bf16[8,96,768]{2,1,0:T(8,128)(2,1)S(1)}, u32[]{:S(2)}, u32[]{:S(2)}) collective-permute-start(bf16[8,96,768]{2,1,0:T(8,128)(2,1)} %get-tuple-element.145), channel_id=1, source_target_pairs={{0,1},{1,0},{2,3},{3,2},{4,5},{5,4},{6,7},{7,6},{8,9},{9,8},{10,11... | collective-permute-start | bytes 3538952 | tf_op jit(solution)/shard_map/ppermute | solution.py:818
  153.8 10.6 %copy-start.9 = (bf16[2,96,768]{2,1,0:T(8,128)(2,1)S(1)}, bf16[2,96,768]{2,1,0:T(8,128)(2,1)}, u32[]{:S(2)}) copy-start(bf16[2,96,768]{2,1,0:T(8,128)(2,1)} %copy-done.8) | copy-start | bytes 884740
  164.4 4.0 %copy-start.3 = (bf16[8,96,768]{2,1,0:T(8,128)(2,1)S(1)}, bf16[8,96,768]{2,1,0:T(8,128)(2,1)}, u32[]{:S(2)}) copy-start(bf16[8,96,768]{2,1,0:T(8,128)(2,1)} %get-tuple-element.144) | copy-start | bytes 3538948
  167.7 1.9 copy-start.15
  169.7 16.6 %collective-permute-start.19 = (bf16[8,112,768]{2,1,0:T(8,128)(2,1)}, bf16[8,112,768]{2,1,0:T(8,128)(2,1)S(1)}, u32[]{:S(2)}, u32[]{:S(2)}) collective-permute-start(bf16[8,112,768]{2,1,0:T(8,128)(2,1)} %get-tuple-element.153), channel_id=1, source_target_pairs={{0,1},{1,0},{2,3},{3,2},{4,5},{5,4},{6,7},{7,6},{8,9},{9,8},{10,11... | collective-permute-start | bytes 4128776 | tf_op jit(solution)/shard_map/ppermute | solution.py:818
  170.4 11.5 %collective-permute-start.32 = (bf16[96,768]{1,0:T(8,128)(2,1)}, bf16[96,768]{1,0:T(8,128)(2,1)}, u32[]{:S(2)}, u32[]{:S(2)}) collective-permute-start(bf16[96,768]{1,0:T(8,128)(2,1)} %dynamic-slice_bitcast_fusion), channel_id=1, source_target_pairs={{0,8},{1,9},{2,10},{3,11},{4,12},{5,13},{6,14},{7,15},{8,0},{9,1},... | collective-permute-start | bytes 442376 | tf_op jit(solution)/shard_map/ppermute | solution.py:818
  172.7 13.6 %copy-start.2 = (bf16[8,112,768]{2,1,0:T(8,128)(2,1)S(1)}, bf16[8,112,768]{2,1,0:T(8,128)(2,1)}, u32[]{:S(2)}) copy-start(bf16[8,112,768]{2,1,0:T(8,128)(2,1)} %get-tuple-element.147) | copy-start | bytes 4128772
  180.2 6.0 %collective-permute-start.34 = (bf16[96,768]{1,0:T(8,128)(2,1)S(1)}, bf16[96,768]{1,0:T(8,128)(2,1)S(1)}, u32[]{:S(2)}, u32[]{:S(2)}) collective-permute-start(bf16[96,768]{1,0:T(8,128)(2,1)S(1)} %fusion.33), channel_id=1, source_target_pairs={{0,16},{1,17},{2,18},{3,19},{4,20},{5,21},{6,22},{7,23},{8,24},{9,... | collective-permute-start | bytes 442376 | tf_op jit(solution)/shard_map/ppermute | solution.py:818
  180.7 10.1 %collective-permute-start.20 = (bf16[2,2,2,48,768]{4,3,0,2,1:T(8,128)(2,1)}, bf16[2,2,2,48,768]{4,3,0,2,1:T(8,128)(2,1)S(1)}, u32[]{:S(2)}, u32[]{:S(2)}) collective-permute-start(bf16[2,2,2,48,768]{4,3,0,2,1:T(8,128)(2,1)} %fusion.3), channel_id=1, source_target_pairs={{0,2},{1,5},{2,0},{3,7},{4,6},{5,1},{6,4},{7,3},{8,10},{9,13},{10,... | collective-permute-start | bytes 1769480 | tf_op jit(solution)/shard_map/ppermute | solution.py:818
  182.9 4.8 %copy-start.12 = (f32[192,768]{1,0:T(8,128)S(1)}, f32[192,768]{1,0:T(8,128)}, u32[]{:S(2)}) copy-start(f32[192,768]{1,0:T(8,128)} %get-tuple-element.173) | copy-start | bytes 1769476
  182.9 6.0 %collective-permute-start.33 = (bf16[96,768]{1,0:T(8,128)(2,1)S(1)}, bf16[96,768]{1,0:T(8,128)(2,1)S(1)}, u32[]{:S(2)}, u32[]{:S(2)}) collective-permute-start(bf16[96,768]{1,0:T(8,128)(2,1)S(1)} %fusion.25), channel_id=1, source_target_pairs={{0,16},{1,17},{2,18},{3,19},{4,20},{5,21},{6,22},{7,23},{8,24},{9,... | collective-permute-start | bytes 442376 | tf_op jit(solution)/shard_map/ppermute | solution.py:818
  186.5 4.3 %copy-start.5 = (bf16[8,96,768]{2,1,0:T(8,128)(2,1)S(1)}, bf16[8,96,768]{2,1,0:T(8,128)(2,1)}, u32[]{:S(2)}) copy-start(bf16[8,96,768]{2,1,0:T(8,128)(2,1)} %copy-done.4) | copy-start | bytes 3538948
  186.5 14.9 %collective-permute-start.21 = (bf16[2,2,2,56,768]{4,3,0,2,1:T(8,128)(2,1)S(1)}, bf16[2,2,2,56,768]{4,3,0,2,1:T(8,128)(2,1)S(1)}, u32[]{:S(2)}, u32[]{:S(2)}) collective-permute-start(bf16[2,2,2,56,768]{4,3,0,2,1:T(8,128)(2,1)S(1)} %fusion.2), channel_id=1, source_target_pairs={{0,2},{1,5},{2,0},{3,7},{4,6},{5,1},{6,4},{7,3},{8,10},{9,13},{10,... | collective-permute-start | bytes 2064392 | tf_op jit(solution)/shard_map/ppermute | solution.py:818
  191.0 13.6 %collective-permute-start.22 = (bf16[2,48,768]{2,1,0:T(8,128)(2,1)S(1)}, bf16[2,48,768]{2,1,0:T(8,128)(2,1)S(1)}, u32[]{:S(2)}, u32[]{:S(2)}) collective-permute-start(bf16[2,48,768]{2,1,0:T(8,128)(2,1)S(1)} %get-tuple-element.228), channel_id=1, source_target_pairs={{0,4},{1,3},{2,6},{3,1},{4,0},{5,7},{6,2},{7,5},{8,12},{9,11},{10,... | collective-permute-start | bytes 442376 | tf_op jit(solution)/shard_map/ppermute | solution.py:818
  192.5 12.6 %collective-permute-start.23 = (bf16[2,48,768]{2,1,0:T(8,128)(2,1)S(1)}, bf16[2,48,768]{2,1,0:T(8,128)(2,1)S(1)}, u32[]{:S(2)}, u32[]{:S(2)}) collective-permute-start(bf16[2,48,768]{2,1,0:T(8,128)(2,1)S(1)} %get-tuple-element.230), channel_id=1, source_target_pairs={{0,16},{1,17},{2,18},{3,19},{4,20},{5,21},{6,22},{7,23},{8,24},{9,... | collective-permute-start | bytes 442376 | tf_op jit(solution)/shard_map/ppermute | solution.py:818
  194.0 11.1 %collective-permute-start.24 = (bf16[2,48,768]{2,1,0:T(8,128)(2,1)S(1)}, bf16[2,48,768]{2,1,0:T(8,128)(2,1)S(1)}, u32[]{:S(2)}, u32[]{:S(2)}) collective-permute-start(bf16[2,48,768]{2,1,0:T(8,128)(2,1)S(1)} %get-tuple-element.229), channel_id=1, source_target_pairs={{0,20},{1,19},{2,22},{3,17},{4,16},{5,23},{6,18},{7,21},{8,28},{9,... | collective-permute-start | bytes 442376 | tf_op jit(solution)/shard_map/ppermute | solution.py:818
  201.5 6.3 %collective-permute-start.25 = (bf16[2,56,768]{2,1,0:T(8,128)(2,1)S(1)}, bf16[2,56,768]{2,1,0:T(8,128)(2,1)S(1)}, u32[]{:S(2)}, u32[]{:S(2)}) collective-permute-start(bf16[2,56,768]{2,1,0:T(8,128)(2,1)S(1)} %get-tuple-element.227), channel_id=1, source_target_pairs={{0,4},{1,3},{2,6},{3,1},{4,0},{5,7},{6,2},{7,5},{8,12},{9,11},{10,... | collective-permute-start | bytes 516104 | tf_op jit(solution)/shard_map/ppermute | solution.py:818
  203.1 6.2 %collective-permute-start.26 = (bf16[2,56,768]{2,1,0:T(8,128)(2,1)S(1)}, bf16[2,56,768]{2,1,0:T(8,128)(2,1)S(1)}, u32[]{:S(2)}, u32[]{:S(2)}) collective-permute-start(bf16[2,56,768]{2,1,0:T(8,128)(2,1)S(1)} %get-tuple-element.226), channel_id=1, source_target_pairs={{0,16},{1,17},{2,18},{3,19},{4,20},{5,21},{6,22},{7,23},{8,24},{9,... | collective-permute-start | bytes 516104 | tf_op jit(solution)/shard_map/ppermute | solution.py:818
  204.6 7.3 %collective-permute-start.27 = (bf16[2,56,768]{2,1,0:T(8,128)(2,1)S(1)}, bf16[2,56,768]{2,1,0:T(8,128)(2,1)S(1)}, u32[]{:S(2)}, u32[]{:S(2)}) collective-permute-start(bf16[2,56,768]{2,1,0:T(8,128)(2,1)S(1)} %get-tuple-element.225), channel_id=1, source_target_pairs={{0,20},{1,19},{2,22},{3,17},{4,16},{5,23},{6,18},{7,21},{8,28},{9,... | collective-permute-start | bytes 516104 | tf_op jit(solution)/shard_map/ppermute | solution.py:818
  205.3 7.6 %collective-permute-start.28 = (bf16[48,768]{1,0:T(8,128)(2,1)S(1)}, bf16[48,768]{1,0:T(8,128)(2,1)S(1)}, u32[]{:S(2)}, u32[]{:S(2)}) collective-permute-start(bf16[48,768]{1,0:T(8,128)(2,1)S(1)} %dynamic-slice_bitcast_fusion.3), channel_id=1, source_target_pairs={{0,8},{1,9},{2,10},{3,11},{4,12},{5,13},{6,14},{7,15},{8,0},{9,1},... | collective-permute-start | bytes 221192 | tf_op jit(solution)/shard_map/ppermute | solution.py:818
  212.1 7.0 %copy-start.11 = (f32[48,3072]{1,0:T(8,128)S(1)}, f32[48,3072]{1,0:T(8,128)}, u32[]{:S(2)}) copy-start(f32[48,3072]{1,0:T(8,128)} %get-tuple-element.171) | copy-start | bytes 1769476
  212.1 6.0 %collective-permute-start.30 = (bf16[56,768]{1,0:T(8,128)(2,1)S(1)}, bf16[56,768]{1,0:T(8,128)(2,1)S(1)}, u32[]{:S(2)}, u32[]{:S(2)}) collective-permute-start(bf16[56,768]{1,0:T(8,128)(2,1)S(1)} %dynamic-slice_bitcast_fusion.2), channel_id=1, source_target_pairs={{0,8},{1,9},{2,10},{3,11},{4,12},{5,13},{6,14},{7,15},{8,0},{9,1},... | collective-permute-start | bytes 258056 | tf_op jit(solution)/shard_map/ppermute | solution.py:818
  212.9 7.1 %copy-start.14 = (bf16[48,768]{1,0:T(8,128)(2,1)}, bf16[48,768]{1,0:T(8,128)(2,1)S(1)}, u32[]{:S(2)}) copy-start(bf16[48,768]{1,0:T(8,128)(2,1)S(1)} %fusion.35.rest_0_) | copy-start | bytes 221188
  212.9 7.1 %collective-permute-start.29 = (bf16[48,768]{1,0:T(8,128)(2,1)S(1)}, bf16[48,768]{1,0:T(8,128)(2,1)S(1)}, u32[]{:S(2)}, u32[]{:S(2)}) collective-permute-start(bf16[48,768]{1,0:T(8,128)(2,1)S(1)} %fusion.35.rest_0_), channel_id=1, source_target_pairs={{0,16},{1,17},{2,18},{3,19},{4,20},{5,21},{6,22},{7,23},{8,24},{9,... | collective-permute-start | bytes 221192 | tf_op jit(solution)/shard_map/ppermute | solution.py:818
  218.2 4.6 %collective-permute-start.31 = (bf16[56,768]{1,0:T(8,128)(2,1)S(1)}, bf16[56,768]{1,0:T(8,128)(2,1)S(1)}, u32[]{:S(2)}, u32[]{:S(2)}) collective-permute-start(bf16[56,768]{1,0:T(8,128)(2,1)S(1)} %fusion.34.rest_2_), channel_id=1, source_target_pairs={{0,16},{1,17},{2,18},{3,19},{4,20},{5,21},{6,22},{7,23},{8,24},{9,... | collective-permute-start | bytes 258056 | tf_op jit(solution)/shard_map/ppermute | solution.py:818
  220.0 2.8 %copy-start.17 = (bf16[48,768]{1,0:T(8,128)(2,1)}, bf16[48,768]{1,0:T(8,128)(2,1)S(1)}, u32[]{:S(2)}) copy-start(bf16[48,768]{1,0:T(8,128)(2,1)S(1)} %collective-permute-done.29.rest_1_) | copy-start | bytes 221188
  (5 other events, 6.2 us)

commit v2 on v1

--- a/solution.py
+++ b/solution.py
@@ -513,7 +513,7 @@
 
 def cross_kernel(r, meta, rows_in, mixed_h, swu_h, swd_h, xqkv_h, xo_h, xu_h, xd_h, sbias, sgains, sshifts, xbias, xgains, xshifts, pos,
                  mixed_o, gr1_o, svec_o, gqkv_o, go_o, gu_o, gd_o, gbias_o, ggains_o, gshifts_o, gpos_o, sgu_o, sgd_o,
-                 swu, swd, xqkv, xo, xu, xd, sgb, sdg, xgb, xdg, sgu, xgu, q_s, k_s, v_s, p_s, o_s, go_s, gq_s, gk_s, gv_s,
+                 swu, swd, xqkv, xo, xu, xd, sgb, sdg, xgb, xdg, sgu, xgu, q_s, k_s, v_s, p_s, o_s, go_s, gq_s, gk_s, gv_s, hb_s, z1_s, y1_s,
                  cls_s, gr1_s, vec_s, svec_s, patch, sems, psems):
     n, D = swu.shape[0], swu.shape[1]
     R = rows_in.shape[0]
@@ -669,16 +669,24 @@
 
     member = meta[0]
     pick = onehot(r, D, member * r)
-    own = lambda x: nt(pick, x).astype(bf16)
-    pick_wide = onehot(r * n, n * D, member * r * n)
-    own_wide = lambda x: nt(pick_wide, x).astype(bf16)
-    hbt = own(hb)
+    window = 256
+
+    def own(x, count):
+        width = x.shape[1]
+        at_col = jnp.minimum(lax.div(member * count, 128) * 128, width - window)
+        near = x[:, pl.ds(pl.multiple_of(at_col, 128), window)]
+        return nt(onehot(count, window, member * count - at_col), near).astype(bf16)
+
+    hb_s[...] = hb
+    z1_s[...] = z1b
+    y1_s[...] = y1b
+    hbt = own(hb_s, r)
     for m, g in enumerate((gq_s, gk_s, gv_s)):
         gqkv_o[m] = nn(hbt, g[...])
-    go_o[...] = nn(own(o_s[...]), xga)
-    gd_o[...] = nn(own_wide(xgb[...]), xgm)
-    sgd_o[...] = nn(own_wide(sgb[...]), sgm)
-    z1t, y1t = own(z1b), own(y1b)
+    go_o[...] = nn(own(o_s, r), xga)
+    gd_o[...] = nn(own(xgb, r * n), xgm)
+    sgd_o[...] = nn(own(sgb, r * n), sgm)
+    z1t, y1t = own(z1_s, r), own(y1_s, r)
     for c in cs:
         gu_o[:, c] = nn(z1t, xgu[:, c])
         sgu_o[:, c] = nn(y1t, sgu[:, c])
@@ -708,7 +716,7 @@
         out_specs=[ANY] + [VM] * (len(outs) - 1),
         out_shape=outs,
         scratch_shapes=[up, down, V(xqkv.shape, bf16), V(xo.shape, bf16), up, down] + [V((R, F), bf16)] * 6 + [row] * 3
-        + [V((D // HD, R, R), bf16)] + [row] * 5 + [V((R, D), f32)] * 2 + [V((SMALL_ROWS, D), f32)] * 2
+        + [V((D // HD, R, R), bf16)] + [row] * 8 + [V((R, D), f32)] * 2 + [V((SMALL_ROWS, D), f32)] * 2
         + [V((segs, 16, D), bf16), pltpu.SemaphoreType.DMA((4 * n + 4,)), pltpu.SemaphoreType.DMA((segs,))],
         input_output_aliases={2: 0},
         compiler_params=PARAMS,

time: 227 us -> 226 us (level)
  no operation moved by 1% of the time
where the time goes in v2:
time: 226 us; the launch traced here: 224 us
  Pallas kernels  126 us (56%)
  waiting for transfers between devices  36 us (16%)
  starting transfers between devices  35.7 us (16%)
  other arithmetic  19.3 us (9%)
  local copies, waits for them, and re-layouts  6.26 us (3%)
    pallas_call x1, Pallas kernels, ffn_back(): pl.pallas_call(functools.partial(ffn_back_kernel, split_of(members, n, Fa...  33.3 us
    pallas_call x1, Pallas kernels, forward(): pl.pallas_call(functools.partial(forward_kernel, lengths.shape[1], split_...  31.8 us
    pallas_call x1, Pallas kernels, cross(): pl.pallas_call(functools.partial(cross_kernel, r), in_specs=[SM, VM] + [A...  29.4 us
    ppermute x28, waiting for transfers between devices, go(): lax.ppermute(x, ('doc', 'seg'), [(m, m ^ by[m & 1]) for m in range(2 * se...  28.7 us
    ppermute x28, starting transfers between devices, go(): lax.ppermute(x, ('doc', 'seg'), [(m, m ^ by[m & 1]) for m in range(2 * se...  26.6 us
    pallas_call x2, Pallas kernels, attn_back(): pl.pallas_call(functools.partial(attn_back_kernel, split, len(grads), is_...  21.8 us
    convert_element_type x16, other arithmetic, sum(): return total.astype(bf16)  17.2 us
    ppermute x7, starting transfers between devices, trade(): lax.ppermute(x, ('doc', 'seg'), [(m, m ^ mask) for m in range(2 * members)])  9.19 us
  transfers between devices with their start and end apart: 35, of which 17 were waited for; matrix products, arithmetic and copies ran while one was open for 6% of the time, Pallas kernels for 41%

profile of v2, /device:TPU:0, one launch (start us, length us, event | category | flops | bytes accessed | tf_op | source)
XLA Modules:
  0.0 224.4 jit_solution(1385536120583488455)
XLA Ops:
  1.3 31.8 %seg_forward.1 = (bf16[768,768]{1,0:T(8,128)(2,1)}, bf16[768,768]{1,0:T(8,128)(2,1)}, bf16[768,768]{1,0:T(8,128)(2,1)}, bf16[6,6,128,256]{3,2,1,0:T(8,128)(2,1)}...) custom-call(s32[5]{0:T(128)} %stack.41.meta, ...), custom_call_target="tpu_custom_call" | custom-call | flops 30000001024 | bytes 90000000 | tf_op jit(solution)/shard_map/seg_forward/pallas_call | solution.py:260
  33.9 4.0 %collective-permute-start = (bf16[6,1664]{1,0:T(8,128)(2,1)S(1)}, bf16[6,1664]{1,0:T(8,128)(2,1)S(1)}, u32[]{:S(2)}, u32[]{:S(2)}) collective-permute-start(bf16[6,1664]{1,0:T(8,128)(2,1)S(1)} %bitcast.193), channel_id=1, source_target_pairs={{0,8},{1,9},{2,10},{3,11},{4,12},{5,13},{6,14},{7,15},{8,0},{9,1},... | collective-permute-start | bytes 59912 | tf_op jit(solution)/shard_map/ppermute | solution.py:867
  38.0 1.5 collective-permute-start.1
  39.8 2.0 collective-permute-done.1
  41.8 3.3 %collective-permute-done.2 = bf16[6,1664]{1,0:T(8,128)(2,1)S(1)} collective-permute-done((bf16[6,1664]{1,0:T(8,128)(2,1)S(1)}, bf16[6,1664]{1,0:T(8,128)(2,1)S(1)}, u32[]{:S(2)}, u32[]{:S(2)}) %collective-permute-start.2) | collective-permute-done | bytes 20000 | tf_op jit(solution)/shard_map/ppermute | solution.py:867
  45.2 1.6 collective-permute-start.3
  46.8 1.6 collective-permute-start.4
  48.8 33.3 %seg_ffn_back.1 = (f32[768,768]{1,0:T(8,128)}, f32[8,768]{1,0:T(8,128)}, f32[8,768]{1,0:T(8,128)}, bf16[8,192,768]{2,1,0:T(8,128)(2,1)}, bf16[8,192,768]{2,1,0:T(8,128)(2,1)}) custom-call(s32[5]{0:T(128)} %stack.41.meta, f32[768,768]{1,0:T(8,128)} %get-tuple-element.102.n1, f32[768,1]{1,0:T(8,128)} %get-tuple-element.104.inv1, ...), custom_call_target="tpu_custom_call" | custom-call | flops 20000000000 | bytes 60000000 | tf_op jit(solution)/shard_map/seg_ffn_back/pallas_call | solution.py:328
  82.4 1.7 collective-permute-done.6
  84.1 1.1 reshape.456.rows_in
  85.2 2.6 %fusion = bf16[2,2,2,96,768]{4,3,0,2,1:T(8,128)(2,1)} fusion(bf16[2,2,2,2,96,768]{5,4,3,2,1,0:T(8,128)(2,1)S(1)} %bitcast.175, s32[]{:T(128)S(6)} %select_n.253, bf16[2,2,2,2,96,768]{5,4,3,2,1,0:T(8,128)(2,1)} %bitcast.11), kind=kLoop, calls=%fused_computation.3 | loop fusion | flops 2359296 | bytes 3539968 | tf_op jit(solution)/shard_map/convert_element_type | solution.py:803
  87.9 1.4 collective-permute-start.8
  89.3 29.4 %cross_block.1 = (bf16[768,768]{1,0:T(8,128)(2,1)}, f32[6,1,768]{2,1,0:T(1,128)}, f32[16,768]{1,0:T(8,128)}, f32[3,48,768]{2,1,0:T(8,128)}, f32[48,768]{1,0:T(8,...) custom-call(s32[5]{0:T(128)} %stack.41.meta, ...), custom_call_target="tpu_custom_call", output_to_operand_aliasing={{0}: (2, {})} | custom-call | flops 28000000000 | bytes 84000000 | tf_op jit(solution)/shard_map/cross_block/pallas_call | solution.py:713
  118.7 2.8 %fusion.15 = (bf16[2,96,768]{2,1,0:T(8,128)(2,1)S(1)}, bf16[2,96,768]{2,1,0:T(8,128)(2,1)}, bf16[2,96,768]{2,1,0:T(8,128)(2,1)}) fusion(bf16[2,2,2,96,768]{4,3,0,2,1:T(8,128)(2,1)S(1)} %collective-permute-done.8, s32[]{:T(128)S(6)} %select_n.258, s32[]{:T(128)S(6)} %select_n.264, bf16[2,2,2,2,96,768]{5,4,3,2,1,0:T(8,128)(2,1)} %bitcast.11, ...), kind=kLoop, calls=%fused_computation.27 | loop fusion | flops 2654208 | bytes 3538964 | tf_op jit(solution)/shard_map/convert_element_type | solution.py:803
  121.5 2.6 %fusion.1 = bf16[2,2,2,96,768]{4,3,0,2,1:T(8,128)(2,1)} fusion(bf16[2,2,2,2,96,768]{5,4,3,2,1,0:T(8,128)(2,1)S(1)} %bitcast.180, s32[]{:T(128)S(6)} %select_n.253, bf16[2,2,2,2,96,768]{5,4,3,2,1,0:T(8,128)(2,1)} %bitcast.22), kind=kLoop, calls=%fused_computation.4 | loop fusion | flops 2359296 | bytes 3539968 | tf_op jit(solution)/shard_map/convert_element_type | solution.py:803
  124.7 1.5 collective-permute-start.10
  126.7 1.5 collective-permute-start.12
  128.2 11.2 %seg_attention_back.2 = (bf16[768,768]{1,0:T(8,128)(2,1)}, bf16[768,768]{1,0:T(8,128)(2,1)}, bf16[768,384]{1,0:T(8,128)(2,1)}, f32[8,768]{1,0:T(8,128)}, bf16[8,...) custom-call(s32[5]{0:T(128)} %stack.41.meta, f32[768,768]{1,0:T(8,128)} %get-tuple-element.114.rest_0_.gr1, ...), custom_call_target="tpu_custom_call" | custom-call | flops 12000000000 | bytes 36000000 | tf_op jit(solution)/shard_map/seg_attention_back/pallas_call | solution.py:477
  139.4 1.8 collective-permute-done.11
  141.2 1.5 fusion.14
  144.1 2.1 collective-permute-done.13
  146.3 2.2 fusion.8
  148.5 1.6 collective-permute-start.16
  150.5 1.5 collective-permute-start.18
  152.4 10.6 %seg_attention_back.3 = (bf16[768,768]{1,0:T(8,128)(2,1)}, bf16[768,768]{1,0:T(8,128)(2,1)}, f32[16,768]{1,0:T(8,128)}, bf16[8,112,768]{2,1,0:T(8,128)(2,1)}, bf16[8,112,768]{2,1,0:T(8,128)(2,1)}) custom-call(s32[5]{0:T(128)} %stack.41.meta, bf16[768,384]{1,0:T(8,128)(2,1)} %get-tuple-element.126.rest_0_, f32[8,768]{1,0:T(8,128)} %get-tuple-element.127.rest_1_, ...), custom_call_target="tpu_custom_call" | custom-call | flops 12000000000 | bytes 36000000 | tf_op jit(solution)/shard_map/seg_attention_back/pallas_call | solution.py:477
  163.1 1.0 fusion.33
  164.8 1.5 fusion.7
  167.1 1.1 fusion.3
  169.0 2.4 %collective-permute-start.32 = (bf16[96,768]{1,0:T(8,128)(2,1)}, bf16[96,768]{1,0:T(8,128)(2,1)}, u32[]{:S(2)}, u32[]{:S(2)}) collective-permute-start(bf16[96,768]{1,0:T(8,128)(2,1)} %dynamic-slice_bitcast_fusion), channel_id=1, source_target_pairs={{0,8},{1,9},{2,10},{3,11},{4,12},{5,13},{6,14},{7,15},{8,0},{9,1},... | collective-permute-start | bytes 442376 | tf_op jit(solution)/shard_map/ppermute | solution.py:826
  171.4 7.5 %input_grad.1 = bf16[768,768]{1,0:T(8,128)(2,1)} custom-call(f32[768,768]{1,0:T(8,128)} %get-tuple-element.114.rest_0_.gr1, f32[6,1,768]{2,1,0:T(1,128)} %get-tuple-element.119.rest_1_.gr1c, bf16[768,768]{1,0:T(8,128)(2,1)} %get-tuple-element.125.qk0, bf16[768,768]{1,0:T(8,128)(2,1)} %get-tuple-element.142.qk1, bf16[768,768]{1,0:T(8,128)(2,1)} %get-tuple-element.143.vv, ...), custom_call_target="tpu_custom_call" | custom-call | flops 6000000000 | bytes 18000000 | tf_op jit(solution)/shard_map/input_grad/pallas_call | solution.py:359
  179.4 1.1 collective-permute-start.20
  180.5 1.0 fusion.25
  181.5 1.6 collective-permute-start.33
  183.1 1.8 collective-permute-done.34
  185.2 1.2 collective-permute-start.21
  187.6 1.9 collective-permute-done.20
  189.6 1.6 collective-permute-start.22
  191.2 1.5 collective-permute-start.23
  193.2 6.8 %collective-permute-done.21 = bf16[2,2,2,56,768]{4,3,0,2,1:T(8,128)(2,1)S(1)} collective-permute-done((bf16[2,2,2,56,768]{4,3,0,2,1:T(8,128)(2,1)S(1)}, bf16[2,2,2,56,768]{4,3,0,2,1:T(8,128)(2,1)S(1)}, u32[]{:S(2)}, u32[]{:S(2)}) %collective-permute-start.21) | collective-permute-done | bytes 688160 | tf_op jit(solution)/shard_map/ppermute | solution.py:826
  200.2 1.6 collective-permute-start.25
  201.8 1.5 collective-permute-start.26
  204.6 1.9 collective-permute-done.25
  206.5 1.5 collective-permute-done.26
  208.0 2.6 %collective-permute-done.27 = bf16[2,56,768]{2,1,0:T(8,128)(2,1)S(1)} collective-permute-done((bf16[2,56,768]{2,1,0:T(8,128)(2,1)S(1)}, bf16[2,56,768]{2,1,0:T(8,128)(2,1)S(1)}, u32[]{:S(2)}, u32[]{:S(2)}) %collective-permute-start.27) | collective-permute-done | bytes 172064 | tf_op jit(solution)/shard_map/ppermute | solution.py:826
  211.5 1.6 collective-permute-start.29
  213.1 3.7 %collective-permute-done.30 = bf16[56,768]{1,0:T(8,128)(2,1)S(1)} collective-permute-done((bf16[56,768]{1,0:T(8,128)(2,1)S(1)}, bf16[56,768]{1,0:T(8,128)(2,1)S(1)}, u32[]{:S(2)}, u32[]{:S(2)}) %collective-permute-start.30) | collective-permute-done | bytes 86048 | tf_op jit(solution)/shard_map/ppermute | solution.py:826
  218.7 2.8 %collective-permute-done.31.rest_3_ = bf16[56,768]{1,0:T(8,128)(2,1)S(1)} collective-permute-done((bf16[56,768]{1,0:T(8,128)(2,1)S(1)}, bf16[56,768]{1,0:T(8,128)(2,1)S(1)}, u32[]{:S(2)}, u32[]{:S(2)}) %collective-permute-start.31) | collective-permute-done | bytes 86048 | tf_op jit(solution)/shard_map/ppermute | solution.py:826
  222.1 2.2 finish.1
  (102 shorter events, 15.7 us)
Async XLA Ops:
  33.9 5.9 %collective-permute-start = (bf16[6,1664]{1,0:T(8,128)(2,1)S(1)}, bf16[6,1664]{1,0:T(8,128)(2,1)S(1)}, u32[]{:S(2)}, u32[]{:S(2)}) collective-permute-start(bf16[6,1664]{1,0:T(8,128)(2,1)S(1)} %bitcast.193), channel_id=1, source_target_pairs={{0,8},{1,9},{2,10},{3,11},{4,12},{5,13},{6,14},{7,15},{8,0},{9,1},... | collective-permute-start | bytes 59912 | tf_op jit(solution)/shard_map/ppermute | solution.py:867
  38.0 3.8 %collective-permute-start.1 = (bf16[6,1664]{1,0:T(8,128)(2,1)S(1)}, bf16[6,1664]{1,0:T(8,128)(2,1)S(1)}, u32[]{:S(2)}, u32[]{:S(2)}) collective-permute-start(bf16[6,1664]{1,0:T(8,128)(2,1)S(1)} %bitcast.194), channel_id=1, source_target_pairs={{0,16},{1,17},{2,18},{3,19},{4,20},{5,21},{6,22},{7,23},{8,24},{9,... | collective-permute-start | bytes 59912 | tf_op jit(solution)/shard_map/ppermute | solution.py:867
  39.5 5.6 %collective-permute-start.2 = (bf16[6,1664]{1,0:T(8,128)(2,1)S(1)}, bf16[6,1664]{1,0:T(8,128)(2,1)S(1)}, u32[]{:S(2)}, u32[]{:S(2)}) collective-permute-start(bf16[6,1664]{1,0:T(8,128)(2,1)S(1)} %bitcast.195), channel_id=1, source_target_pairs={{0,24},{1,25},{2,26},{3,27},{4,28},{5,29},{6,30},{7,31},{8,16},{9,... | collective-permute-start | bytes 59912 | tf_op jit(solution)/shard_map/ppermute | solution.py:867
  39.5 45.7 %collective-permute-start.7 = (bf16[8,192,768]{2,1,0:T(8,128)(2,1)}, bf16[8,192,768]{2,1,0:T(8,128)(2,1)}, u32[]{:S(2)}, u32[]{:S(2)}) collective-permute-start(bf16[8,192,768]{2,1,0:T(8,128)(2,1)} %get-tuple-element.109), channel_id=1, source_target_pairs={{0,1},{1,0},{2,3},{3,2},{4,5},{5,4},{6,7},{7,6},{8,9},{9,8},{10,11... | collective-permute-start | bytes 7077896 | tf_op jit(solution)/shard_map/ppermute | solution.py:826
  45.2 36.9 %collective-permute-start.3 = (bf16[2,2,6,1664]{3,2,1,0:T(8,128)(2,1)S(1)}, bf16[2,2,6,1664]{3,2,1,0:T(8,128)(2,1)S(1)}, u32[]{:S(2)}, u32[]{:S(2)}) collective-permute-start(bf16[2,2,6,1664]{3,2,1,0:T(8,128)(2,1)S(1)} %get-tuple-element.235), channel_id=1, source_target_pairs={{0,2},{1,3},{2,0},{3,1},{4,6},{5,7},{6,4},{7,5},{8,10},{9,11},{10,... | collective-permute-start | bytes 239624 | tf_op jit(solution)/shard_map/ppermute | solution.py:867
  46.8 35.3 %collective-permute-start.4 = (bf16[2,2,6,1664]{3,2,1,0:T(8,128)(2,1)S(1)}, bf16[2,2,6,1664]{3,2,1,0:T(8,128)(2,1)S(1)}, u32[]{:S(2)}, u32[]{:S(2)}) collective-permute-start(bf16[2,2,6,1664]{3,2,1,0:T(8,128)(2,1)S(1)} %get-tuple-element.235), channel_id=1, source_target_pairs={{0,4},{1,5},{2,6},{3,7},{4,0},{5,1},{6,2},{7,3},{8,12},{9,13},{10,... | collective-permute-start | bytes 239624 | tf_op jit(solution)/shard_map/ppermute | solution.py:867
  48.3 33.8 %collective-permute-start.5 = (bf16[2,2,6,1664]{3,2,1,0:T(8,128)(2,1)S(1)}, bf16[2,2,6,1664]{3,2,1,0:T(8,128)(2,1)S(1)}, u32[]{:S(2)}, u32[]{:S(2)}) collective-permute-start(bf16[2,2,6,1664]{3,2,1,0:T(8,128)(2,1)S(1)} %get-tuple-element.235), channel_id=1, source_target_pairs={{0,6},{1,7},{2,4},{3,5},{4,2},{5,3},{6,0},{7,1},{8,14},{9,15},{10,... | collective-permute-start | bytes 239624 | tf_op jit(solution)/shard_map/ppermute | solution.py:867
  82.2 1.8 collective-permute-start.6
  82.3 2.8 %copy-start = (bf16[8,192,768]{2,1,0:T(8,128)(2,1)S(1)}, bf16[8,192,768]{2,1,0:T(8,128)(2,1)}, u32[]{:S(2)}) copy-start(bf16[8,192,768]{2,1,0:T(8,128)(2,1)} %get-tuple-element.108) | copy-start | bytes 7077892
  87.8 33.7 %collective-permute-start.9 = (bf16[8,192,768]{2,1,0:T(8,128)(2,1)}, bf16[8,192,768]{2,1,0:T(8,128)(2,1)}, u32[]{:S(2)}, u32[]{:S(2)}) collective-permute-start(bf16[8,192,768]{2,1,0:T(8,128)(2,1)} %get-tuple-element.118), channel_id=1, source_target_pairs={{0,1},{1,0},{2,3},{3,2},{4,5},{5,4},{6,7},{7,6},{8,9},{9,8},{10,11... | collective-permute-start | bytes 7077896 | tf_op jit(solution)/shard_map/ppermute | solution.py:826
  87.9 30.8 %collective-permute-start.8 = (bf16[2,2,2,96,768]{4,3,0,2,1:T(8,128)(2,1)}, bf16[2,2,2,96,768]{4,3,0,2,1:T(8,128)(2,1)S(1)}, u32[]{:S(2)}, u32[]{:S(2)}) collective-permute-start(bf16[2,2,2,96,768]{4,3,0,2,1:T(8,128)(2,1)} %fusion), channel_id=1, source_target_pairs={{0,2},{1,5},{2,0},{3,7},{4,6},{5,1},{6,4},{7,3},{8,10},{9,13},{10,... | collective-permute-start | bytes 3538952 | tf_op jit(solution)/shard_map/ppermute | solution.py:826
  118.7 2.8 %copy-start.1 = (bf16[8,192,768]{2,1,0:T(8,128)(2,1)S(1)}, bf16[8,192,768]{2,1,0:T(8,128)(2,1)}, u32[]{:S(2)}) copy-start(bf16[8,192,768]{2,1,0:T(8,128)(2,1)} %get-tuple-element.117) | copy-start | bytes 7077892
  118.7 5.4 %copy-start.7 = (bf16[2,2,2,96,768]{4,3,0,2,1:T(8,128)(2,1)}, bf16[2,2,2,96,768]{4,3,0,2,1:T(8,128)(2,1)S(1)}, u32[]{:S(2)}) copy-start(bf16[2,2,2,96,768]{4,3,0,2,1:T(8,128)(2,1)S(1)} %collective-permute-done.8) | copy-start | bytes 3538948
  124.1 22.2 %collective-permute-start.13 = (bf16[2,2,2,96,768]{4,3,0,2,1:T(8,128)(2,1)}, bf16[2,2,2,96,768]{4,3,0,2,1:T(8,128)(2,1)S(1)}, u32[]{:S(2)}, u32[]{:S(2)}) collective-permute-start(bf16[2,2,2,96,768]{4,3,0,2,1:T(8,128)(2,1)} %fusion.1), channel_id=1, source_target_pairs={{0,2},{1,5},{2,0},{3,7},{4,6},{5,1},{6,4},{7,3},{8,10},{9,13},{10,... | collective-permute-start | bytes 3538952 | tf_op jit(solution)/shard_map/ppermute | solution.py:826
  124.7 14.7 %collective-permute-start.10 = (bf16[2,96,768]{2,1,0:T(8,128)(2,1)}, bf16[2,96,768]{2,1,0:T(8,128)(2,1)}, u32[]{:S(2)}, u32[]{:S(2)}) collective-permute-start(bf16[2,96,768]{2,1,0:T(8,128)(2,1)} %get-tuple-element.133), channel_id=1, source_target_pairs={{0,4},{1,3},{2,6},{3,1},{4,0},{5,7},{6,2},{7,5},{8,12},{9,11},{10,... | collective-permute-start | bytes 884744 | tf_op jit(solution)/shard_map/ppermute | solution.py:826
  126.2 15.0 %collective-permute-start.11 = (bf16[2,96,768]{2,1,0:T(8,128)(2,1)}, bf16[2,96,768]{2,1,0:T(8,128)(2,1)}, u32[]{:S(2)}, u32[]{:S(2)}) collective-permute-start(bf16[2,96,768]{2,1,0:T(8,128)(2,1)} %get-tuple-element.134), channel_id=1, source_target_pairs={{0,16},{1,17},{2,18},{3,19},{4,20},{5,21},{6,22},{7,23},{8,24},{9,... | collective-permute-start | bytes 884744 | tf_op jit(solution)/shard_map/ppermute | solution.py:826
  126.7 14.5 %collective-permute-start.12 = (bf16[2,96,768]{2,1,0:T(8,128)(2,1)S(1)}, bf16[2,96,768]{2,1,0:T(8,128)(2,1)}, u32[]{:S(2)}, u32[]{:S(2)}) collective-permute-start(bf16[2,96,768]{2,1,0:T(8,128)(2,1)S(1)} %get-tuple-element.135), channel_id=1, source_target_pairs={{0,20},{1,19},{2,22},{3,17},{4,16},{5,23},{6,18},{7,21},{8,28},{9,... | collective-permute-start | bytes 884744 | tf_op jit(solution)/shard_map/ppermute | solution.py:826
  146.3 2.2 copy-start.6
  148.5 15.7 %collective-permute-start.16 = (bf16[2,96,768]{2,1,0:T(8,128)(2,1)S(1)}, bf16[2,96,768]{2,1,0:T(8,128)(2,1)S(1)}, u32[]{:S(2)}, u32[]{:S(2)}) collective-permute-start(bf16[2,96,768]{2,1,0:T(8,128)(2,1)S(1)} %get-tuple-element.150), channel_id=1, source_target_pairs={{0,4},{1,3},{2,6},{3,1},{4,0},{5,7},{6,2},{7,5},{8,12},{9,11},{10,... | collective-permute-start | bytes 884744 | tf_op jit(solution)/shard_map/ppermute | solution.py:826
  150.0 14.8 %collective-permute-start.17 = (bf16[2,96,768]{2,1,0:T(8,128)(2,1)S(1)}, bf16[2,96,768]{2,1,0:T(8,128)(2,1)}, u32[]{:S(2)}, u32[]{:S(2)}) collective-permute-start(bf16[2,96,768]{2,1,0:T(8,128)(2,1)S(1)} %get-tuple-element.151), channel_id=1, source_target_pairs={{0,16},{1,17},{2,18},{3,19},{4,20},{5,21},{6,22},{7,23},{8,24},{9,... | collective-permute-start | bytes 884744 | tf_op jit(solution)/shard_map/ppermute | solution.py:826
  150.5 14.3 %collective-permute-start.18 = (bf16[2,96,768]{2,1,0:T(8,128)(2,1)S(1)}, bf16[2,96,768]{2,1,0:T(8,128)(2,1)}, u32[]{:S(2)}, u32[]{:S(2)}) collective-permute-start(bf16[2,96,768]{2,1,0:T(8,128)(2,1)S(1)} %get-tuple-element.152), channel_id=1, source_target_pairs={{0,20},{1,19},{2,22},{3,17},{4,16},{5,23},{6,18},{7,21},{8,28},{9,... | collective-permute-start | bytes 884744 | tf_op jit(solution)/shard_map/ppermute | solution.py:826
  152.0 11.0 %collective-permute-start.15 = (bf16[96,768]{1,0:T(8,128)(2,1)}, bf16[96,768]{1,0:T(8,128)(2,1)}, u32[]{:S(2)}, u32[]{:S(2)}) collective-permute-start(bf16[96,768]{1,0:T(8,128)(2,1)} %dynamic-slice_bitcast_fusion.1), channel_id=1, source_target_pairs={{0,8},{1,9},{2,10},{3,11},{4,12},{5,13},{6,14},{7,15},{8,0},{9,1},... | collective-permute-start | bytes 442376 | tf_op jit(solution)/shard_map/ppermute | solution.py:826
  152.4 14.7 %collective-permute-start.14 = (bf16[8,96,768]{2,1,0:T(8,128)(2,1)}, bf16[8,96,768]{2,1,0:T(8,128)(2,1)S(1)}, u32[]{:S(2)}, u32[]{:S(2)}) collective-permute-start(bf16[8,96,768]{2,1,0:T(8,128)(2,1)} %get-tuple-element.145), channel_id=1, source_target_pairs={{0,1},{1,0},{2,3},{3,2},{4,5},{5,4},{6,7},{7,6},{8,9},{9,8},{10,11... | collective-permute-start | bytes 3538952 | tf_op jit(solution)/shard_map/ppermute | solution.py:826
  152.4 10.6 %copy-start.9 = (bf16[2,96,768]{2,1,0:T(8,128)(2,1)S(1)}, bf16[2,96,768]{2,1,0:T(8,128)(2,1)}, u32[]{:S(2)}) copy-start(bf16[2,96,768]{2,1,0:T(8,128)(2,1)} %copy-done.8) | copy-start | bytes 884740
  163.1 4.0 %copy-start.3 = (bf16[8,96,768]{2,1,0:T(8,128)(2,1)S(1)}, bf16[8,96,768]{2,1,0:T(8,128)(2,1)}, u32[]{:S(2)}) copy-start(bf16[8,96,768]{2,1,0:T(8,128)(2,1)} %get-tuple-element.144) | copy-start | bytes 3538948
  166.4 1.9 copy-start.15
  168.3 16.6 %collective-permute-start.19 = (bf16[8,112,768]{2,1,0:T(8,128)(2,1)}, bf16[8,112,768]{2,1,0:T(8,128)(2,1)S(1)}, u32[]{:S(2)}, u32[]{:S(2)}) collective-permute-start(bf16[8,112,768]{2,1,0:T(8,128)(2,1)} %get-tuple-element.153), channel_id=1, source_target_pairs={{0,1},{1,0},{2,3},{3,2},{4,5},{5,4},{6,7},{7,6},{8,9},{9,8},{10,11... | collective-permute-start | bytes 4128776 | tf_op jit(solution)/shard_map/ppermute | solution.py:826
  169.0 11.5 %collective-permute-start.32 = (bf16[96,768]{1,0:T(8,128)(2,1)}, bf16[96,768]{1,0:T(8,128)(2,1)}, u32[]{:S(2)}, u32[]{:S(2)}) collective-permute-start(bf16[96,768]{1,0:T(8,128)(2,1)} %dynamic-slice_bitcast_fusion), channel_id=1, source_target_pairs={{0,8},{1,9},{2,10},{3,11},{4,12},{5,13},{6,14},{7,15},{8,0},{9,1},... | collective-permute-start | bytes 442376 | tf_op jit(solution)/shard_map/ppermute | solution.py:826
  171.4 13.6 %copy-start.2 = (bf16[8,112,768]{2,1,0:T(8,128)(2,1)S(1)}, bf16[8,112,768]{2,1,0:T(8,128)(2,1)}, u32[]{:S(2)}) copy-start(bf16[8,112,768]{2,1,0:T(8,128)(2,1)} %get-tuple-element.147) | copy-start | bytes 4128772
  178.9 6.0 %collective-permute-start.34 = (bf16[96,768]{1,0:T(8,128)(2,1)S(1)}, bf16[96,768]{1,0:T(8,128)(2,1)S(1)}, u32[]{:S(2)}, u32[]{:S(2)}) collective-permute-start(bf16[96,768]{1,0:T(8,128)(2,1)S(1)} %fusion.33), channel_id=1, source_target_pairs={{0,16},{1,17},{2,18},{3,19},{4,20},{5,21},{6,22},{7,23},{8,24},{9,... | collective-permute-start | bytes 442376 | tf_op jit(solution)/shard_map/ppermute | solution.py:826
  179.4 10.1 %collective-permute-start.20 = (bf16[2,2,2,48,768]{4,3,0,2,1:T(8,128)(2,1)}, bf16[2,2,2,48,768]{4,3,0,2,1:T(8,128)(2,1)S(1)}, u32[]{:S(2)}, u32[]{:S(2)}) collective-permute-start(bf16[2,2,2,48,768]{4,3,0,2,1:T(8,128)(2,1)} %fusion.3), channel_id=1, source_target_pairs={{0,2},{1,5},{2,0},{3,7},{4,6},{5,1},{6,4},{7,3},{8,10},{9,13},{10,... | collective-permute-start | bytes 1769480 | tf_op jit(solution)/shard_map/ppermute | solution.py:826
  181.5 4.8 %copy-start.12 = (f32[192,768]{1,0:T(8,128)S(1)}, f32[192,768]{1,0:T(8,128)}, u32[]{:S(2)}) copy-start(f32[192,768]{1,0:T(8,128)} %get-tuple-element.173) | copy-start | bytes 1769476
  181.5 6.0 %collective-permute-start.33 = (bf16[96,768]{1,0:T(8,128)(2,1)S(1)}, bf16[96,768]{1,0:T(8,128)(2,1)S(1)}, u32[]{:S(2)}, u32[]{:S(2)}) collective-permute-start(bf16[96,768]{1,0:T(8,128)(2,1)S(1)} %fusion.25), channel_id=1, source_target_pairs={{0,16},{1,17},{2,18},{3,19},{4,20},{5,21},{6,22},{7,23},{8,24},{9,... | collective-permute-start | bytes 442376 | tf_op jit(solution)/shard_map/ppermute | solution.py:826
  185.2 4.3 %copy-start.5 = (bf16[8,96,768]{2,1,0:T(8,128)(2,1)S(1)}, bf16[8,96,768]{2,1,0:T(8,128)(2,1)}, u32[]{:S(2)}) copy-start(bf16[8,96,768]{2,1,0:T(8,128)(2,1)} %copy-done.4) | copy-start | bytes 3538948
  185.2 14.8 %collective-permute-start.21 = (bf16[2,2,2,56,768]{4,3,0,2,1:T(8,128)(2,1)S(1)}, bf16[2,2,2,56,768]{4,3,0,2,1:T(8,128)(2,1)S(1)}, u32[]{:S(2)}, u32[]{:S(2)}) collective-permute-start(bf16[2,2,2,56,768]{4,3,0,2,1:T(8,128)(2,1)S(1)} %fusion.2), channel_id=1, source_target_pairs={{0,2},{1,5},{2,0},{3,7},{4,6},{5,1},{6,4},{7,3},{8,10},{9,13},{10,... | collective-permute-start | bytes 2064392 | tf_op jit(solution)/shard_map/ppermute | solution.py:826
  189.6 13.6 %collective-permute-start.22 = (bf16[2,48,768]{2,1,0:T(8,128)(2,1)S(1)}, bf16[2,48,768]{2,1,0:T(8,128)(2,1)S(1)}, u32[]{:S(2)}, u32[]{:S(2)}) collective-permute-start(bf16[2,48,768]{2,1,0:T(8,128)(2,1)S(1)} %get-tuple-element.228), channel_id=1, source_target_pairs={{0,4},{1,3},{2,6},{3,1},{4,0},{5,7},{6,2},{7,5},{8,12},{9,11},{10,... | collective-permute-start | bytes 442376 | tf_op jit(solution)/shard_map/ppermute | solution.py:826
  191.2 12.6 %collective-permute-start.23 = (bf16[2,48,768]{2,1,0:T(8,128)(2,1)S(1)}, bf16[2,48,768]{2,1,0:T(8,128)(2,1)S(1)}, u32[]{:S(2)}, u32[]{:S(2)}) collective-permute-start(bf16[2,48,768]{2,1,0:T(8,128)(2,1)S(1)} %get-tuple-element.230), channel_id=1, source_target_pairs={{0,16},{1,17},{2,18},{3,19},{4,20},{5,21},{6,22},{7,23},{8,24},{9,... | collective-permute-start | bytes 442376 | tf_op jit(solution)/shard_map/ppermute | solution.py:826
  192.7 11.1 %collective-permute-start.24 = (bf16[2,48,768]{2,1,0:T(8,128)(2,1)S(1)}, bf16[2,48,768]{2,1,0:T(8,128)(2,1)S(1)}, u32[]{:S(2)}, u32[]{:S(2)}) collective-permute-start(bf16[2,48,768]{2,1,0:T(8,128)(2,1)S(1)} %get-tuple-element.229), channel_id=1, source_target_pairs={{0,20},{1,19},{2,22},{3,17},{4,16},{5,23},{6,18},{7,21},{8,28},{9,... | collective-permute-start | bytes 442376 | tf_op jit(solution)/shard_map/ppermute | solution.py:826
  200.2 6.3 %collective-permute-start.25 = (bf16[2,56,768]{2,1,0:T(8,128)(2,1)S(1)}, bf16[2,56,768]{2,1,0:T(8,128)(2,1)S(1)}, u32[]{:S(2)}, u32[]{:S(2)}) collective-permute-start(bf16[2,56,768]{2,1,0:T(8,128)(2,1)S(1)} %get-tuple-element.227), channel_id=1, source_target_pairs={{0,4},{1,3},{2,6},{3,1},{4,0},{5,7},{6,2},{7,5},{8,12},{9,11},{10,... | collective-permute-start | bytes 516104 | tf_op jit(solution)/shard_map/ppermute | solution.py:826
  201.8 6.2 %collective-permute-start.26 = (bf16[2,56,768]{2,1,0:T(8,128)(2,1)S(1)}, bf16[2,56,768]{2,1,0:T(8,128)(2,1)S(1)}, u32[]{:S(2)}, u32[]{:S(2)}) collective-permute-start(bf16[2,56,768]{2,1,0:T(8,128)(2,1)S(1)} %get-tuple-element.226), channel_id=1, source_target_pairs={{0,16},{1,17},{2,18},{3,19},{4,20},{5,21},{6,22},{7,23},{8,24},{9,... | collective-permute-start | bytes 516104 | tf_op jit(solution)/shard_map/ppermute | solution.py:826
  203.3 7.3 %collective-permute-start.27 = (bf16[2,56,768]{2,1,0:T(8,128)(2,1)S(1)}, bf16[2,56,768]{2,1,0:T(8,128)(2,1)S(1)}, u32[]{:S(2)}, u32[]{:S(2)}) collective-permute-start(bf16[2,56,768]{2,1,0:T(8,128)(2,1)S(1)} %get-tuple-element.225), channel_id=1, source_target_pairs={{0,20},{1,19},{2,22},{3,17},{4,16},{5,23},{6,18},{7,21},{8,28},{9,... | collective-permute-start | bytes 516104 | tf_op jit(solution)/shard_map/ppermute | solution.py:826
  203.9 7.6 %collective-permute-start.28 = (bf16[48,768]{1,0:T(8,128)(2,1)S(1)}, bf16[48,768]{1,0:T(8,128)(2,1)S(1)}, u32[]{:S(2)}, u32[]{:S(2)}) collective-permute-start(bf16[48,768]{1,0:T(8,128)(2,1)S(1)} %dynamic-slice_bitcast_fusion.3), channel_id=1, source_target_pairs={{0,8},{1,9},{2,10},{3,11},{4,12},{5,13},{6,14},{7,15},{8,0},{9,1},... | collective-permute-start | bytes 221192 | tf_op jit(solution)/shard_map/ppermute | solution.py:826
  210.8 6.9 %copy-start.11 = (f32[48,3072]{1,0:T(8,128)S(1)}, f32[48,3072]{1,0:T(8,128)}, u32[]{:S(2)}) copy-start(f32[48,3072]{1,0:T(8,128)} %get-tuple-element.171) | copy-start | bytes 1769476
  210.8 6.0 %collective-permute-start.30 = (bf16[56,768]{1,0:T(8,128)(2,1)S(1)}, bf16[56,768]{1,0:T(8,128)(2,1)S(1)}, u32[]{:S(2)}, u32[]{:S(2)}) collective-permute-start(bf16[56,768]{1,0:T(8,128)(2,1)S(1)} %dynamic-slice_bitcast_fusion.2), channel_id=1, source_target_pairs={{0,8},{1,9},{2,10},{3,11},{4,12},{5,13},{6,14},{7,15},{8,0},{9,1},... | collective-permute-start | bytes 258056 | tf_op jit(solution)/shard_map/ppermute | solution.py:826
  211.5 7.1 %copy-start.14 = (bf16[48,768]{1,0:T(8,128)(2,1)}, bf16[48,768]{1,0:T(8,128)(2,1)S(1)}, u32[]{:S(2)}) copy-start(bf16[48,768]{1,0:T(8,128)(2,1)S(1)} %fusion.35.rest_0_) | copy-start | bytes 221188
  211.5 7.1 %collective-permute-start.29 = (bf16[48,768]{1,0:T(8,128)(2,1)S(1)}, bf16[48,768]{1,0:T(8,128)(2,1)S(1)}, u32[]{:S(2)}, u32[]{:S(2)}) collective-permute-start(bf16[48,768]{1,0:T(8,128)(2,1)S(1)} %fusion.35.rest_0_), channel_id=1, source_target_pairs={{0,16},{1,17},{2,18},{3,19},{4,20},{5,21},{6,22},{7,23},{8,24},{9,... | collective-permute-start | bytes 221192 | tf_op jit(solution)/shard_map/ppermute | solution.py:826
  216.9 4.6 %collective-permute-start.31 = (bf16[56,768]{1,0:T(8,128)(2,1)S(1)}, bf16[56,768]{1,0:T(8,128)(2,1)S(1)}, u32[]{:S(2)}, u32[]{:S(2)}) collective-permute-start(bf16[56,768]{1,0:T(8,128)(2,1)S(1)} %fusion.34.rest_2_), channel_id=1, source_target_pairs={{0,16},{1,17},{2,18},{3,19},{4,20},{5,21},{6,22},{7,23},{8,24},{9,... | collective-permute-start | bytes 258056 | tf_op jit(solution)/shard_map/ppermute | solution.py:826
  218.6 2.8 %copy-start.17 = (bf16[48,768]{1,0:T(8,128)(2,1)}, bf16[48,768]{1,0:T(8,128)(2,1)S(1)}, u32[]{:S(2)}) copy-start(bf16[48,768]{1,0:T(8,128)(2,1)S(1)} %collective-permute-done.29.rest_1_) | copy-start | bytes 221188
  (5 other events, 6.2 us)
